TPU v7x, 32 devices: a whole 2x2x4 slice. The times are simulated.
32 devices in a mesh: dp: 8 (over z, y), sp: 4 (over x, core).
Axes of the slice: x: 2, y: 2, z: 4, core: 2. Of those that a mesh axis runs over, the one named last changes fastest.
Arguments:
- queries: bfloat16 [4096, 3584], P(('dp', 'sp')), may hold values from -128 to 128
- keys: bfloat16 [4096, 512], P(('dp', 'sp')), may hold values from -6 to 6
- values: bfloat16 [4096, 512], P(('dp', 'sp')), may hold values from -6 to 6
- document_lengths: int32 [8, 8], P('dp'), may hold values from 1 to 256, 512 in all within a row
- pair_ids: int32 [64], P('dp'), may hold values from 0 to 63, as said below
Outputs:
- embeddings: bfloat16 [64, 3584], P('dp', 'sp')
- grads: float32 [64, 3584], P('dp', 'sp')
Inputs may be any that keep to these rules, and one draw needn't show every extreme that they name: `document_lengths`: each row's 8 lengths sum to 512; the longest is exactly 256. pair_ids pairs the 64 documents two by two: pair_ids[pair_ids[i]] = i and pair_ids[i] != i.
All inputs are finite; a program needn't handle non-finite values.
Results may differ from a plain program's by a relative error of at most 0.0055.
Values may be sent and summed in bfloat16 or wider, within the bound.
No kernel may reach another device: no remote copies, remote signals or barrier semaphores. Data moves between devices by JAX's collectives and lax.ppermute only.
A program may use at most 64 MiB of HBM per device.

v0:
```python
import math

import jax
import jax.numpy as jnp
from jax import lax
from jax.sharding import PartitionSpec as P

QUERY_HEADS = 28
KEY_VALUE_HEADS = 4
HEAD_SIZE = 128
DOCS = 8


SOFTMAX_TEMP = 0.02


def segment_of(lengths, count):
    ends = jnp.cumsum(lengths)
    places = jnp.arange(count, dtype=jnp.int32)
    return jnp.sum((places[:, None] >= ends[None, :]).astype(jnp.int32), axis=1)


def attend(query_flat, row_segment, key_head, value_head, segment):
    total = query_flat.shape[0]
    block_rows = math.gcd(total, 512)
    query_blocks = query_flat.reshape(total // block_rows, block_rows, query_flat.shape[1])
    segment_blocks = row_segment.reshape(total // block_rows, block_rows)

    def one_block(inputs):
        query_block, segment_block = inputs
        scores = lax.dot_general(
            query_block, key_head, (((1,), (1,)), ((), ())), preferred_element_type=jnp.float32
        ) * HEAD_SIZE ** (-0.5)
        scores = jnp.where(segment_block[:, None] == segment[None, :], scores, -jnp.inf)
        largest = jnp.max(scores, axis=1, keepdims=True)
        weights = jnp.exp(scores - largest)
        probs = (weights / jnp.sum(weights, axis=1, keepdims=True)).astype(jnp.bfloat16)
        return jnp.dot(probs, value_head, preferred_element_type=jnp.float32).astype(jnp.bfloat16)

    return lax.map(one_block, (query_blocks, segment_blocks)).reshape(total, value_head.shape[1])


def per_device(queries, keys, values, document_lengths, pair_ids):
    lengths = document_lengths[0]
    parts = lax.axis_size("sp")
    tokens_here = queries.shape[0]
    seq_len = tokens_here * parts
    segment = segment_of(lengths, seq_len)
    head_group = QUERY_HEADS // KEY_VALUE_HEADS
    doc_index = jnp.arange(DOCS, dtype=jnp.int32)
    stacked = jnp.stack([keys, values])
    query_rows, kv_rows = (
        lax.all_to_all(queries[None], "sp", split_axis=2, concat_axis=1, tiled=True),
        lax.all_to_all(stacked, "sp", split_axis=2, concat_axis=1, tiled=True),
    )
    flat = query_rows[0].reshape(seq_len * head_group, HEAD_SIZE)
    result = attend(flat, jnp.repeat(segment, head_group), kv_rows[0], kv_rows[1], segment)
    attended = result.reshape(seq_len, head_group * HEAD_SIZE)
    onehot = (segment[None, :] == doc_index[:, None]).astype(jnp.bfloat16)
    summed = jnp.dot(onehot, attended, preferred_element_type=jnp.float32)
    pooled = summed / lengths[:, None].astype(jnp.float32)
    squares = lax.psum(jnp.sum(pooled * pooled, axis=1), "sp")
    radius = jnp.sqrt(squares + 1e-06)[:, None]
    embeddings = (pooled / radius).astype(jnp.bfloat16)
    every = lax.all_gather(embeddings, "dp", axis=0, tiled=True)
    partial_scores = lax.dot_general(
        embeddings, every, (((1,), (1,)), ((), ())), preferred_element_type=jnp.float32
    )
    score_logits = lax.psum(partial_scores, "sp") / SOFTMAX_TEMP
    columns = jnp.arange(every.shape[0], dtype=jnp.int32)
    own_rows = lax.axis_index("dp") * DOCS + doc_index
    score_logits = jnp.where(own_rows[:, None] == columns[None, :], -jnp.inf, score_logits)
    largest = jnp.max(score_logits, axis=1, keepdims=True)
    weights = jnp.exp(score_logits - largest)
    probs = weights / jnp.sum(weights, axis=1, keepdims=True)
    loss_coefficient = probs - (columns[None, :] == pair_ids[:, None]).astype(jnp.float32)
    every_wide = every.astype(jnp.float32)
    own_wide = embeddings.astype(jnp.float32)
    row_piece = jnp.dot(loss_coefficient, every_wide, precision=lax.Precision.HIGHEST)
    column_piece = lax.psum_scatter(
        jnp.dot(loss_coefficient.T, own_wide, precision=lax.Precision.HIGHEST),
        "dp",
        scatter_dimension=0,
        tiled=True,
    )
    embedding_gradient = (row_piece + column_piece) / SOFTMAX_TEMP
    along = lax.psum(jnp.sum(own_wide * embedding_gradient, axis=1), "sp")
    grads = (embedding_gradient - own_wide * along[:, None]) / radius
    return (embeddings, grads)


def solution(mesh):
    return jax.shard_map(
        per_device,
        mesh=mesh,
        in_specs=(
            P(("dp", "sp"), None),
            P(("dp", "sp"), None),
            P(("dp", "sp"), None),
            P("dp", None),
            P("dp"),
        ),
        out_specs=(P("dp", "sp"), P("dp", "sp")),
        check_vma=False,
    )
```

profile of v0, /device:TPU:0, one launch (start us, length us, event | category | flops | bytes accessed | tf_op | source)
XLA Modules:
  0.0 195.3 jit_solution(5647473992604037813)
XLA Ops:
  7.2 1.1 pad_maximum_fusion
  8.3 0.9 copy.28
  9.1 4.2 %all-to-all-start.1 = ((bf16[2,128,512]{1,0,2:T(2,128)(2,1)}), bf16[2,128,512]{1,0,2:T(2,128)(2,1)S(1)}, u32[]{:S(2)}, u32[]{:S(2)}) async-start(bf16[2,128,512]{1,0,2:T(2,128)(2,1)} %copy.28), calls=%async_computation.1 | async-start | bytes 524288 | tf_op jit(solution)/shard_map/all_to_all | solution.py:54
  13.3 2.5 %copy.26 = bf16[1,128,3584]{1,0,2:T(2,128)(2,1)S(1)} copy(bf16[1,128,3584]{2,1,0:T(8,128)(2,1)S(1)} %bitcast.53) | data formatting | bytes 1835008 | tf_op jit(solution)/shard_map/broadcast_in_dim | solution.py:53
  15.8 0.5 broadcast.27
  16.3 19.7 %reduce = bf16[3584,128]{1,0:T(8,128)(2,1)S(1)} reduce(bf16[3584,1,128]{2,1,0:T(2,128)(2,1)S(1)} %bitcast.49, bf16[]{:T(256)} %broadcast.27), dimensions={1}, to_apply=%bitcast.28.reduce_sub_computation | reduce | bytes 1835010
  36.0 1.6 reshape.59
  37.8 3.5 %all-to-all-start = ((bf16[4,2,57344]{2,1,0:T(2,128)(2,1)}), bf16[4,2,57344]{2,1,0:T(2,128)(2,1)S(1)}, u32[]{:S(2)}, u32[]{:S(2)}) async-start(bf16[4,2,57344]{2,1,0:T(2,128)(2,1)} %reshape.59), calls=%async_computation | async-start | bytes 1835008 | tf_op jit(solution)/shard_map/all_to_all | solution.py:53
  41.9 0.4 fusion.20
  42.5 11.8 %all-to-all-done = bf16[4,2,57344]{2,1,0:T(2,128)(2,1)S(1)} async-done(((bf16[4,2,57344]{2,1,0:T(2,128)(2,1)}), bf16[4,2,57344]{2,1,0:T(2,128)(2,1)S(1)}, u32[]{:S(2)}, u32[]{:S(2)}) %all-to-all-start) | async-done | bytes 917536 | tf_op jit(solution)/shard_map/all_to_all | solution.py:53
  54.4 0.8 reshape.60
  55.4 0.6 copy.27
  56.0 0.9 reshape_reshape_squeeze.3
  56.9 6.9 %while.10 = (s32[]{:T(128)}, bf16[7,512,128]{2,1,0:T(8,128)(2,1)S(1)}, s32[7,512]{1,0:T(8,128)S(1)}, s32[512]{0:T(512)S(1)}, bf16[7,512,128]{2,1,0:T(8,128)(2,1)...) while((s32[]{:T(128)}, bf16[7,512,128]{2,1,0:T(8,128)(2,1)S(1)}, ...), condition=%wide.region_5.6_spmd, body=%wide.region_2.5_spmd.sunk | while | flops 136641536 | bytes 3688545 | solution.py:40
  57.4 0.4 fusion.38
  58.4 0.4 fusion.38
  59.4 0.4 fusion.38
  60.4 0.4 fusion.38
  61.4 0.4 fusion.38
  62.4 0.4 fusion.38
  63.4 0.4 fusion.38
  63.8 0.9 reshape_reshape.7
  64.7 0.4 multiply_reduce_fusion
  65.1 5.8 %psum.21 = f32[8]{0:T(128)S(1)} all-reduce(f32[8]{0:T(128)S(1)} %get-tuple-element.60), channel_id=1, replica_groups=mesh['dp'=8,'sp'=4] {'sp'}, use_global_device_ids=true, to_apply=%region_7.8 | all-reduce | flops 8 | bytes 64 | tf_op jit(solution)/shard_map/psum | solution.py:62
  70.9 31.6 %all_gather.3 = bf16[64,896]{1,0:T(8,128)(2,1)S(1)} all-gather(bf16[8,896]{1,0:T(8,128)(2,1)S(1)} %divide_convert_fusion.2), channel_id=1, replica_groups=mesh['dp'=8,'sp'=4] {'dp'}, dimensions={0}, use_global_device_ids=true | all-gather | bytes 129024 | tf_op jit(solution)/shard_map/all_gather | solution.py:65
  102.7 5.7 %psum.22 = f32[8,64]{1,0:T(8,128)S(1)} all-reduce(f32[8,64]{1,0:T(8,128)S(1)} %fusion.21), channel_id=1, replica_groups=mesh['dp'=8,'sp'=4] {'sp'}, use_global_device_ids=true, to_apply=%region_8.9 | all-reduce | flops 512 | bytes 4096 | tf_op jit(solution)/shard_map/psum | solution.py:69
  108.7 1.1 fusion.18
  109.9 0.6 dynamic-slice
  111.1 69.9 %all-reduce.3.cloned.1.call-done = f32[64,896]{1,0:T(8,128)} async-done(((f32[64,896]{1,0:T(8,128)}), f32[64,896]{1,0:T(8,128)}) %all-reduce.3.cloned.1.call-update) | async-done | bytes 229392
  181.0 1.1 fusion.10
  182.1 5.7 %psum.23 = f32[8]{0:T(128)S(1)} all-reduce(f32[8]{0:T(128)S(1)} %get-tuple-element.62), channel_id=1, replica_groups=mesh['dp'=8,'sp'=4] {'sp'}, use_global_device_ids=true, to_apply=%region_13.14 | all-reduce | flops 8 | bytes 64 | tf_op jit(solution)/shard_map/psum | solution.py:87
  187.7 0.7 fusion.12
  (51 shorter events, 5.4 us)
Async XLA Ops:
  7.2 6.2 %copy-start.1 = (bf16[128,3584]{1,0:T(8,128)(2,1)S(1)}, bf16[128,3584]{1,0:T(8,128)(2,1)}, u32[]{:S(2)}) copy-start(bf16[128,3584]{1,0:T(8,128)(2,1)} %param.7) | copy-start | bytes 2752516
  9.1 28.7 %all-to-all-start.1 = ((bf16[2,128,512]{1,0,2:T(2,128)(2,1)}), bf16[2,128,512]{1,0,2:T(2,128)(2,1)S(1)}, u32[]{:S(2)}, u32[]{:S(2)}) async-start(bf16[2,128,512]{1,0,2:T(2,128)(2,1)} %copy.28), calls=%async_computation.1 | async-start | bytes 524288 | tf_op jit(solution)/shard_map/all_to_all | solution.py:54
  16.3 21.3 %copy-start.4 = (s32[1,8]{1,0:T(1,128)S(1)}, s32[1,8]{1,0:T(1,128)}, u32[]{:S(2)}) copy-start(s32[1,8]{1,0:T(1,128)} %param.10) | copy-start | bytes 100
  37.8 16.5 %all-to-all-start = ((bf16[4,2,57344]{2,1,0:T(2,128)(2,1)}), bf16[4,2,57344]{2,1,0:T(2,128)(2,1)S(1)}, u32[]{:S(2)}, u32[]{:S(2)}) async-start(bf16[4,2,57344]{2,1,0:T(2,128)(2,1)} %reshape.59), calls=%async_computation | async-start | bytes 1835008 | tf_op jit(solution)/shard_map/all_to_all | solution.py:53
  41.3 139.6 %all-reduce.3.cloned.1.call-start = ((), (), s32[]{:S(2)}) async-start(), calls=%async_computation.2 | async-start | bytes 458752
  55.4 1.5 copy-start
  63.8 44.9 %copy-start.3 = (s32[8]{0:T(128)S(1)}, s32[8]{0:T(128)}, u32[]{:S(2)}) copy-start(s32[8]{0:T(128)} %param.11) | copy-start | bytes 100
  63.8 46.0 %copy-start.5 = (u32[32]{0:T(128)S(1)}, u32[32]{0:T(128)}, u32[]{:S(2)}) copy-start(u32[32]{0:T(128)} %constant.46) | copy-start | bytes 388
  70.9 117.5 %copy-start.2 = (bf16[8,896]{1,0:T(8,128)(2,1)}, bf16[8,896]{1,0:T(8,128)(2,1)S(1)}, u32[]{:S(2)}) copy-start(bf16[8,896]{1,0:T(8,128)(2,1)S(1)} %divide_convert_fusion.2) | copy-start | bytes 43012
Sparse Core Ops, SparseCore 0:
  110.0 70.9 all-reduce.2
where the time goes:
time: 196 us; the launch traced here: 195 us
  waiting for transfers between devices  81.7 us (42%)
  blocking collectives  48.7 us (25%)
  other arithmetic  23.6 us (12%)
  between operations  14.9 us (8%)
  local copies, waits for them, and re-layouts  10.5 us (5%)
  matrix products  7.95 us (4%)
  starting transfers between devices  7.75 us (4%)
    unnamed x2, waiting for transfers between devices  69.9 us
    all_gather x1, blocking collectives, per_device(): every = lax.all_gather(embeddings, 'dp', axis=0, tiled=True)  31.6 us
    unnamed x1, other arithmetic  19.7 us
    all_to_all x1, waiting for transfers between devices, per_device(): lax.all_to_all(queries[None], 'sp', split_axis=2, concat_axis=1, tiled=True)  11.8 us
    psum x1, blocking collectives, per_device(): squares = lax.psum(jnp.sum(pooled * pooled, axis=1), 'sp')  5.76 us
    psum x1, blocking collectives, per_device(): along = lax.psum(jnp.sum(own_wide * embedding_gradient, axis=1), 'sp')  5.66 us
    psum x1, blocking collectives, per_device(): score_logits = lax.psum(partial_scores, 'sp') / SOFTMAX_TEMP  5.65 us
    all_to_all x1, starting transfers between devices, per_device(): lax.all_to_all(stacked, 'sp', split_axis=2, concat_axis=1, tiled=True)  4.21 us
  transfers between devices with their start and end apart: 3, of which 2 were waited for; matrix products, arithmetic and copies ran while one was open for 13% of the time, Pallas kernels for 0%

commit v1 on v0

v1 whole, which is shorter than its diff:
```python
import functools
import math

import jax
import jax.numpy as jnp
from jax import lax
from jax.experimental import pallas as pl
from jax.experimental.pallas import tpu as pltpu
from jax.sharding import PartitionSpec as P

QUERY_HEADS = 28
KEY_VALUE_HEADS = 4
HEAD_SIZE = 128
HEAD_GROUP = QUERY_HEADS // KEY_VALUE_HEADS
GROUP_WIDTH = HEAD_GROUP * HEAD_SIZE
PAIR = 2
DOCS = 8
SOFTMAX_TEMP = 0.02
VMEM_LIMIT = 48 * 1024 * 1024

VMEM = pl.BlockSpec(memory_space=pltpu.VMEM)
HBM = pl.BlockSpec(memory_space=pltpu.HBM)


def segments(lengths_ref, places):
    end = lengths_ref[0, 0]
    segment = (places >= end).astype(jnp.int32)
    for d in range(1, DOCS):
        end = end + lengths_ref[0, d]
        segment = segment + (places >= end).astype(jnp.int32)
    return segment


def plan_kernel(parts, lengths_hbm, pairs_hbm, q_hbm, k_hbm, v_hbm, *refs):
    q_out, k_out, v_out, near_out, k_far_out, v_far_out, bias_ref, doc_ref, partner_ref, lengths_ref, pairs_ref, sem, small_sem = refs
    span = k_hbm.shape[0]
    me = lax.axis_index("sp")
    core = lax.rem(me, PAIR)
    small = [
        pltpu.make_async_copy(lengths_hbm, lengths_ref, small_sem.at[0]),
        pltpu.make_async_copy(pairs_hbm, pairs_ref, small_sem.at[1]),
    ]
    for copy in small:
        copy.start()
    copies = []

    def cut(source, other, target, start):
        width = source.shape[1] // KEY_VALUE_HEADS
        for p in range(PAIR):
            first = pl.multiple_of((PAIR * p + (core ^ other)) * width, HEAD_SIZE)
            copies.append(
                pltpu.make_async_copy(
                    source.at[:, pl.ds(first, width)],
                    target.at[:, start + p * width : start + (p + 1) * width],
                    sem.at[len(copies)],
                )
            )

    pair_width = PAIR * HEAD_SIZE
    cut(k_hbm, 0, k_out, 0)
    cut(k_hbm, 1, k_far_out, 0)
    cut(k_hbm, 1, near_out, PAIR * GROUP_WIDTH)
    cut(q_hbm, 1, near_out, 0)
    cut(v_hbm, 1, near_out, PAIR * GROUP_WIDTH + pair_width)
    cut(v_hbm, 0, v_out, 0)
    cut(v_hbm, 1, v_far_out, 0)
    cut(q_hbm, 0, q_out, 0)
    for copy in copies:
        copy.start()
    for copy in small:
        copy.wait()
    doc = lax.broadcasted_iota(jnp.int32, (DOCS, span), 0)
    weight = jnp.zeros((DOCS, span), jnp.float32)
    for d in range(DOCS):
        weight = jnp.where(doc == d, 1.0 / lengths_ref[0, d].astype(jnp.float32), weight)
    row_segments = [
        segments(lengths_ref, (me ^ r) * span + lax.broadcasted_iota(jnp.int32, (span, 1), 0)) for r in range(PAIR)
    ]
    for r in range(parts):
        columns = slice(r * span, (r + 1) * span)
        key_segment = segments(lengths_ref, (me ^ r) * span + lax.broadcasted_iota(jnp.int32, (1, span), 1))
        for t in range(PAIR):
            bias_ref[t * span : (t + 1) * span, columns] = jnp.where(row_segments[t] == key_segment, 0.0, -1e30)
        doc_ref[:, columns] = jnp.where(key_segment == doc, weight, 0.0)
    own = lax.axis_index("dp")
    own_row = lax.broadcasted_iota(jnp.int32, partner_ref.shape, 0)
    own_column = lax.broadcasted_iota(jnp.int32, partner_ref.shape, 1)
    place = jnp.zeros(partner_ref.shape, jnp.int32)
    for d in range(DOCS):
        pair = pairs_ref[d]
        place = jnp.where(own_row == d, ((pair // DOCS) ^ own) * DOCS + lax.rem(pair, DOCS), place)
    partner_ref[...] = jnp.where(own_column == place, 2.0, 0.0)
    for copy in copies:
        copy.wait()


def scores_kernel(bias_ref, q_own, k_own, near, k_far, k_last, sums_ref):
    scale = HEAD_SIZE ** (-0.5) * math.log2(math.e)
    for p in range(PAIR):
        here = slice(p * HEAD_SIZE, (p + 1) * HEAD_SIZE)
        beside = PAIR * GROUP_WIDTH + p * HEAD_SIZE
        key_head = jnp.concatenate(
            [k_own[:, here], near[:, beside : beside + HEAD_SIZE], k_far[:, here], k_last[:, here]], axis=0
        )
        for h in range(HEAD_GROUP):
            place = (p * HEAD_GROUP + h) * HEAD_SIZE
            total = None
            for t, q_ref in enumerate((q_own, near)):
                query = q_ref[:, place : place + HEAD_SIZE]
                rows = query.shape[0]
                scores = lax.dot_general(
                    query, key_head, (((1,), (1,)), ((), ())), preferred_element_type=jnp.float32
                )
                scores = scores + bias_ref[t * rows : (t + 1) * rows]
                largest = jnp.max(scores, axis=1, keepdims=True)
                weights = jnp.exp2((scores - largest) * scale)
                probs = weights * (1.0 / jnp.sum(weights, axis=1, keepdims=True))
                summed = jnp.sum(probs, axis=0, keepdims=True)
                total = summed if total is None else total + summed
            row = p * HEAD_GROUP + h
            sums_ref[row : row + 1] = total


def values_kernel(sums_ref, doc_ref, v_own, near, v_far, v_last, out_ref, sent_ref):
    for p in range(PAIR):
        here = slice(p * HEAD_SIZE, (p + 1) * HEAD_SIZE)
        beside = PAIR * (GROUP_WIDTH + HEAD_SIZE) + p * HEAD_SIZE
        value_head = jnp.concatenate(
            [v_own[:, here], near[:, beside : beside + HEAD_SIZE], v_far[:, here], v_last[:, here]], axis=0
        )
        rows = range(p * HEAD_GROUP, (p + 1) * HEAD_GROUP)
        spread = jnp.concatenate([sums_ref[row : row + 1] * doc_ref[...] for row in rows], axis=0)
        high = spread.astype(jnp.bfloat16)
        low = (spread - high.astype(jnp.float32)).astype(jnp.bfloat16)
        summed = jnp.dot(high, value_head, preferred_element_type=jnp.float32) + jnp.dot(
            low, value_head, preferred_element_type=jnp.float32
        )
        for h, row in enumerate(rows):
            out_ref[:, row * HEAD_SIZE : (row + 1) * HEAD_SIZE] = summed[h * DOCS : (h + 1) * DOCS]
    sent_ref[...] = out_ref[...].astype(jnp.bfloat16)


def pool_kernel(one_ref, two_ref, pooled_ref, sent_ref):
    pooled = one_ref[...] + two_ref[...].astype(jnp.float32)
    pooled_ref[...] = pooled
    sent_ref[...] = pooled.astype(jnp.bfloat16)


def join_kernel(*refs):
    refs[-1][...] = jnp.concatenate([ref[...] for ref in in_order(refs[:-1])], axis=0)


def in_order(refs):
    return (refs[0], *refs[:0:-1])


def gram_kernel(*refs):
    every = jnp.concatenate([ref[...] for ref in in_order(refs[:-1])], axis=0)
    refs[-1][...] = lax.dot_general(every, every, (((1,), (1,)), ((), ())), preferred_element_type=jnp.float32)


def grads_kernel(partner_ref, pooled_ref, gram_one, gram_two, *refs):
    every_refs, (emb_ref, grads_ref) = refs[:-2], refs[-2:]
    gram = gram_one[...] + gram_two[...]
    docs = gram.shape[0]
    columns = pl.ds(pl.multiple_of((lax.axis_index("sp") // PAIR) * GROUP_WIDTH, HEAD_SIZE), GROUP_WIDTH)
    row = lax.broadcasted_iota(jnp.int32, (docs, docs), 0)
    column = lax.broadcasted_iota(jnp.int32, (docs, docs), 1)
    diagonal = row == column
    square = jnp.where(diagonal, gram, 0.0)
    inverse_column = lax.rsqrt(jnp.sum(square, axis=1, keepdims=True) + 1e-6)
    inverse_row = lax.rsqrt(jnp.sum(square, axis=0, keepdims=True) + 1e-6)
    cosine = gram * inverse_column * inverse_row
    logits = jnp.where(diagonal, -jnp.inf, cosine * (1.0 / SOFTMAX_TEMP))
    own = logits[:DOCS]
    largest = jnp.max(own, axis=1, keepdims=True)
    weights = jnp.exp(own - largest)
    probs = weights / jnp.sum(weights, axis=1, keepdims=True)
    largest_row = jnp.max(logits, axis=0, keepdims=True)
    total_row = jnp.sum(jnp.exp(logits - largest_row), axis=0, keepdims=True)
    probs = probs + jnp.exp(own - largest_row) / total_row
    both = probs - partner_ref[...]
    along = jnp.sum(both * cosine[:DOCS], axis=1, keepdims=True) * (1.0 / SOFTMAX_TEMP)
    weighted = both * inverse_row * (1.0 / SOFTMAX_TEMP)
    high = weighted.astype(jnp.bfloat16)
    low = (weighted - high.astype(jnp.float32)).astype(jnp.bfloat16)
    every = jnp.concatenate([ref[:, columns] for ref in in_order(every_refs)], axis=0)
    gradient = jnp.dot(high, every, preferred_element_type=jnp.float32) + jnp.dot(
        low, every, preferred_element_type=jnp.float32
    )
    inverse = inverse_column[:DOCS]
    embeddings = (pooled_ref[:, columns] * inverse).astype(jnp.bfloat16)
    emb_ref[...] = embeddings
    grads_ref[...] = (gradient - embeddings.astype(jnp.float32) * along) * inverse


def call(kernel, out_shape, in_specs, scratch_shapes=(), flops=0, moved=0):
    return pl.pallas_call(
        kernel,
        out_shape=out_shape,
        in_specs=in_specs,
        out_specs=jax.tree.map(lambda _: VMEM, out_shape),
        scratch_shapes=scratch_shapes,
        compiler_params=pltpu.CompilerParams(vmem_limit_bytes=VMEM_LIMIT),
        cost_estimate=pl.CostEstimate(flops=flops, bytes_accessed=moved, transcendentals=0),
    )


def swap(block, axis, size, distance):
    return lax.ppermute(block, axis, [(s, s ^ distance) for s in range(size)])


def gather_pairs(block, axis, size):
    have, blocks = 1, [block]
    while have < size:
        if have > 1:
            shape = (len(blocks) * block.shape[0], block.shape[1])
            block = call(join_kernel, jax.ShapeDtypeStruct(shape, block.dtype), [VMEM] * len(blocks))(*blocks)
        radix = PAIR if have == 1 else min(4, size // have)
        blocks = [block] + [swap(block, axis, size, r * have) for r in reversed(range(1, radix))]
        have *= radix
    return blocks


def per_device(sizes, queries, keys, values, document_lengths, pair_ids):
    replicas, parts = sizes
    tokens, features = queries.shape
    width = features // PAIR
    kv_width = keys.shape[1] // PAIR
    docs = DOCS * replicas
    f32, bf16 = jnp.float32, jnp.bfloat16
    struct = jax.ShapeDtypeStruct
    query_own, key_own, value_own, near, key_send, value_send, bias, of_doc, partner = call(
        functools.partial(plan_kernel, parts),
        (
            struct((tokens, width), bf16),
            struct((tokens, kv_width), bf16),
            struct((tokens, kv_width), bf16),
            struct((tokens, width + 2 * kv_width), bf16),
            struct((tokens, kv_width), bf16),
            struct((tokens, kv_width), bf16),
            struct((PAIR * tokens, parts * tokens), f32),
            struct((DOCS, parts * tokens), f32),
            struct((DOCS, docs), f32),
        ),
        [HBM] * 5,
        [
            pltpu.SMEM((1, DOCS), jnp.int32),
            pltpu.SMEM((DOCS,), jnp.int32),
            pltpu.SemaphoreType.DMA((8 * PAIR,)),
            pltpu.SemaphoreType.DMA((2,)),
        ],
        moved=2 * tokens * features + 4 * keys.size,
    )(*(pltpu.with_memory_space_constraint(x, pltpu.HBM) for x in (document_lengths, pair_ids, queries, keys, values)))
    near = swap(near, "sp", parts, 1)
    value_far = swap(value_own, "sp", parts, 2)
    value_last = swap(value_send, "sp", parts, 3)
    key_far = swap(key_own, "sp", parts, 2)
    key_last = swap(key_send, "sp", parts, 3)
    sums = call(
        scores_kernel,
        struct((PAIR * HEAD_GROUP, parts * tokens), f32),
        [VMEM] * 6,
        flops=tokens * features * tokens * parts,
        moved=2 * queries.size + 4 * parts * keys.size,
    )(bias, query_own, key_own, near, key_far, key_last)
    partial, rounded = call(
        values_kernel, (struct((DOCS, width), f32), struct((DOCS, width), bf16)), [VMEM] * 6
    )(sums, of_doc, value_own, near, value_far, value_last)
    pooled, sent = call(
        pool_kernel, (struct((DOCS, width), f32), struct((DOCS, width), bf16)), [VMEM] * 2
    )(partial, swap(rounded, "sp", parts, 2))
    blocks = gather_pairs(sent, "dp", replicas)
    gram = call(gram_kernel, struct((docs, docs), f32), [VMEM] * len(blocks))(*blocks)
    return call(
        grads_kernel,
        (struct((DOCS, features // parts), bf16), struct((DOCS, features // parts), f32)),
        [VMEM] * (4 + len(blocks)),
    )(partner, pooled, gram, swap(gram, "sp", parts, 1), *blocks)


def solution(mesh):
    sizes = (mesh.shape["dp"], mesh.shape["sp"])
    return jax.shard_map(
        functools.partial(per_device, sizes),
        mesh=mesh,
        in_specs=(
            P(("dp", "sp"), None),
            P(("dp", "sp"), None),
            P(("dp", "sp"), None),
            P("dp", None),
            P("dp"),
        ),
        out_specs=(P("dp", "sp"), P("dp", "sp")),
        check_vma=False,
    )
```

time: 196 us -> 31.7 us (0.16)
  waiting for transfers between devices: 81.7 us -> 13.1 us
  blocking collectives: 48.7 us -> 0 us
  other arithmetic: 23.6 us -> 0 us
  between operations: 14.9 us -> 0.69 us
  local copies, waits for them, and re-layouts: 10.5 us -> 0 us
  matrix products: 7.95 us -> 0 us
  Pallas kernels: 0 us -> 5.34 us
  starting transfers between devices: 7.75 us -> 12.4 us
    unnamed x2 -> x0, waiting for transfers between devices: 69.9 us -> none
    all_gather x1 -> x0, blocking collectives: 31.6 us -> none  [per_device(): every = lax.all_gather(embeddings, 'dp', axis=0, tiled=True)]
    unnamed x1 -> x0, other arithmetic: 19.7 us -> none
    psum x3 -> x0, blocking collectives: 17.1 us -> none  [the longest x1 5.76 us: per_device(): squares = lax.psum(jnp.sum(pooled * pooled, axis=1), 'sp')]
    ppermute x0 -> x11, waiting for transfers between devices: none -> 13.1 us  [swap(): return lax.ppermute(block, axis, [(s, s ^ distance) for s in range(size)])]
    ppermute x0 -> x11, starting transfers between devices: none -> 12.4 us  [swap(): return lax.ppermute(block, axis, [(s, s ^ distance) for s in range(size)])]
    all_to_all x2 -> x0, waiting for transfers between devices: 11.8 us -> none  [the longest x1 11.8 us: per_device(): lax.all_to_all(queries[None], 'sp', split_axis=2, concat_axis=1, tiled=True)]
    dot_general x18 -> x0, matrix products: 7.95 us -> none  [the longest x7 3.01 us: one_block(): jnp.dot(probs, value_head, preferred_element_type=jnp.float32)]
  transfers between devices with their start and end apart: 3 -> 11, of which waited for: 2 -> 8; matrix products, arithmetic and copies ran while one was open for 13% -> 0% of each run, Pallas kernels for 0% -> 7%
where the time goes in v1:
time: 31.7 us; the launch traced here: 31.5 us
  waiting for transfers between devices  13.1 us (41%)
  starting transfers between devices  12.4 us (39%)
  Pallas kernels  5.34 us (17%)
  between operations  0.69 us (2%)
    ppermute x11, waiting for transfers between devices, swap(): return lax.ppermute(block, axis, [(s, s ^ distance) for s in range(size)])  13.1 us
    ppermute x11, starting transfers between devices, swap(): return lax.ppermute(block, axis, [(s, s ^ distance) for s in range(size)])  12.4 us
    pallas_call x1, Pallas kernels, per_device(): call(scores_kernel, struct((PAIR * HEAD_GROUP, parts * tokens), f32), [VM...  2.3 us
    pallas_call x1, Pallas kernels, per_device(): call(functools.partial(plan_kernel, parts), (struct((tokens, width), bf16...  1.59 us
    pallas_call x1, Pallas kernels, per_device(): call(grads_kernel, (struct((DOCS, features // parts), bf16), struct((DOCS...  1.02 us
  transfers between devices with their start and end apart: 11, of which 8 were waited for; matrix products, arithmetic and copies ran while one was open for 0% of the time, Pallas kernels for 7%

profile of v1, /device:TPU:0, one launch (start us, length us, event | category | flops | bytes accessed | tf_op | source)
XLA Modules:
  0.0 31.5 jit_solution(4107520355337600518)
XLA Ops:
  0.6 1.6 %shard_map.68 = (bf16[128,1792]{1,0:T(8,128)(2,1)S(1)}, bf16[128,256]{1,0:T(8,128)(2,1)S(1)}, bf16[128,256]{1,0:T(8,128)(2,1)S(1)}, bf16[128,2304]{1,0:T(8,128)(...) custom-call(s32[1,8]{1,0:T(1,128)} %lengths_hbm.1, ...), custom_call_target="tpu_custom_call" | custom-call | bytes 1179648 | tf_op jit(solution)/shard_map/pallas_call | solution.py:233
  2.2 0.5 %collective-permute-start = (bf16[128,2304]{1,0:T(8,128)(2,1)S(1)}, bf16[128,2304]{1,0:T(8,128)(2,1)S(1)}, u32[]{:S(2)}, u32[]{:S(2)}) collective-permute-start(bf16[128,2304]{1,0:T(8,128)(2,1)S(1)} %get-tuple-element.19), channel_id=1, source_target_pairs={{0,1},{1,0},{2,3},{3,2},{4,5},{5,4},{6,7},{7,6},{8,9},{9,8},{10,11... | collective-permute-start | bytes 1769480 | tf_op jit(solution)/shard_map/ppermute | solution.py:210
  2.7 2.6 %collective-permute-start.1 = (bf16[128,256]{1,0:T(8,128)(2,1)S(1)}, bf16[128,256]{1,0:T(8,128)(2,1)S(1)}, u32[]{:S(2)}, u32[]{:S(2)}) collective-permute-start(bf16[128,256]{1,0:T(8,128)(2,1)S(1)} %get-tuple-element.18.k_own), channel_id=1, source_target_pairs={{0,2},{1,3},{2,0},{3,1},{4,6},{5,7},{6,4},{7,5},{8,10},{9,11},{10,... | collective-permute-start | bytes 196616 | tf_op jit(solution)/shard_map/ppermute | solution.py:210
  5.3 0.1 collective-permute-start.2
  5.4 1.7 %collective-permute-start.3 = (bf16[128,256]{1,0:T(8,128)(2,1)S(1)}, bf16[128,256]{1,0:T(8,128)(2,1)S(1)}, u32[]{:S(2)}, u32[]{:S(2)}) collective-permute-start(bf16[128,256]{1,0:T(8,128)(2,1)S(1)} %get-tuple-element.22.v_own), channel_id=1, source_target_pairs={{0,2},{1,3},{2,0},{3,1},{4,6},{5,7},{6,4},{7,5},{8,10},{9,11},{10,... | collective-permute-start | bytes 196616 | tf_op jit(solution)/shard_map/ppermute | solution.py:210
  7.1 0.0 collective-permute-start.4
  7.1 0.9 %collective-permute-done.1.k_far = bf16[128,256]{1,0:T(8,128)(2,1)S(1)} collective-permute-done((bf16[128,256]{1,0:T(8,128)(2,1)S(1)}, bf16[128,256]{1,0:T(8,128)(2,1)S(1)}, u32[]{:S(2)}, u32[]{:S(2)}) %collective-permute-start.1) | collective-permute-done | bytes 65568 | tf_op jit(solution)/shard_map/ppermute | solution.py:210
  8.0 1.4 %collective-permute-done.2.k_last = bf16[128,256]{1,0:T(8,128)(2,1)S(1)} collective-permute-done((bf16[128,256]{1,0:T(8,128)(2,1)S(1)}, bf16[128,256]{1,0:T(8,128)(2,1)S(1)}, u32[]{:S(2)}, u32[]{:S(2)}) %collective-permute-start.2) | collective-permute-done | bytes 65568 | tf_op jit(solution)/shard_map/ppermute | solution.py:210
  9.4 0.0 collective-permute-done.near
  9.4 2.3 %shard_map.69.sums_ref = f32[14,512]{1,0:T(8,128)S(1)} custom-call(f32[256,512]{1,0:T(8,128)S(1)} %get-tuple-element.16.bias_ref, bf16[128,1792]{1,0:T(8,128)(2,1)S(1)} %get-tuple-element.17.q_own, bf16[128,256]{1,0:T(8,128)(2,1)S(1)} %get-tuple-element.18.k_own, bf16[128,2304]{1,0:T(8,128)(2,1)S(1)} %collective-permute-done.near, ...), custom_call_target="tpu_custom_call" | custom-call | flops 234881024 | bytes 1966080 | tf_op jit(solution)/shard_map/pallas_call | solution.py:260
  11.7 0.0 collective-permute-done.3.v_far
  11.7 0.5 %collective-permute-done.4.v_last = bf16[128,256]{1,0:T(8,128)(2,1)S(1)} collective-permute-done((bf16[128,256]{1,0:T(8,128)(2,1)S(1)}, bf16[128,256]{1,0:T(8,128)(2,1)S(1)}, u32[]{:S(2)}, u32[]{:S(2)}) %collective-permute-start.4) | collective-permute-done | bytes 65568 | tf_op jit(solution)/shard_map/ppermute | solution.py:210
  12.2 0.2 shard_map.70
  12.4 1.4 %collective-permute-start.5 = (bf16[8,1792]{1,0:T(8,128)(2,1)S(1)}, bf16[8,1792]{1,0:T(8,128)(2,1)S(1)}, u32[]{:S(2)}, u32[]{:S(2)}) collective-permute-start(bf16[8,1792]{1,0:T(8,128)(2,1)S(1)} %get-tuple-element.25), channel_id=1, source_target_pairs={{0,2},{1,3},{2,0},{3,1},{4,6},{5,7},{6,4},{7,5},{8,10},{9,11},{10,... | collective-permute-start | bytes 86024 | tf_op jit(solution)/shard_map/ppermute | solution.py:210
  13.8 2.5 %collective-permute-done.5.two_ref = bf16[8,1792]{1,0:T(8,128)(2,1)S(1)} collective-permute-done((bf16[8,1792]{1,0:T(8,128)(2,1)S(1)}, bf16[8,1792]{1,0:T(8,128)(2,1)S(1)}, u32[]{:S(2)}, u32[]{:S(2)}) %collective-permute-start.5) | collective-permute-done | bytes 28704 | tf_op jit(solution)/shard_map/ppermute | solution.py:210
  16.3 1.6 %collective-permute-start.6 = (bf16[8,1792]{1,0:T(8,128)(2,1)S(1)}, bf16[8,1792]{1,0:T(8,128)(2,1)S(1)}, u32[]{:S(2)}, u32[]{:S(2)}) collective-permute-start(bf16[8,1792]{1,0:T(8,128)(2,1)S(1)} %get-tuple-element.27.refs_0_), channel_id=1, source_target_pairs={{0,4},{4,0},{8,12},{12,8},{16,20},{20,16},{24,28},{28,24},{1,5},{5... | collective-permute-start | bytes 86024 | tf_op jit(solution)/shard_map/ppermute | solution.py:210
  17.9 2.4 %collective-permute-done.6.refs_1_ = bf16[8,1792]{1,0:T(8,128)(2,1)S(1)} collective-permute-done((bf16[8,1792]{1,0:T(8,128)(2,1)S(1)}, bf16[8,1792]{1,0:T(8,128)(2,1)S(1)}, u32[]{:S(2)}, u32[]{:S(2)}) %collective-permute-start.6) | collective-permute-done | bytes 28704 | tf_op jit(solution)/shard_map/ppermute | solution.py:210
  20.3 3.7 %collective-permute-start.7 = (bf16[16,1792]{1,0:T(8,128)(2,1)S(1)}, bf16[16,1792]{1,0:T(8,128)(2,1)S(1)}, u32[]{:S(2)}, u32[]{:S(2)}) collective-permute-start(bf16[16,1792]{1,0:T(8,128)(2,1)S(1)} %shard_map.72.refs_0_), channel_id=1, source_target_pairs={{0,24},{4,28},{8,16},{12,20},{16,8},{20,12},{24,0},{28,4},{1,25},{... | collective-permute-start | bytes 172040 | tf_op jit(solution)/shard_map/ppermute | solution.py:210
  24.0 0.0 collective-permute-start.8
  24.0 0.8 %collective-permute-start.9 = (bf16[16,1792]{1,0:T(8,128)(2,1)S(1)}, bf16[16,1792]{1,0:T(8,128)(2,1)S(1)}, u32[]{:S(2)}, u32[]{:S(2)}) collective-permute-start(bf16[16,1792]{1,0:T(8,128)(2,1)S(1)} %shard_map.72.refs_0_), channel_id=1, source_target_pairs={{0,8},{4,12},{8,0},{12,4},{16,24},{20,28},{24,16},{28,20},{1,9},{5... | collective-permute-start | bytes 172040 | tf_op jit(solution)/shard_map/ppermute | solution.py:210
  24.7 1.8 %collective-permute-done.7.refs_1_ = bf16[16,1792]{1,0:T(8,128)(2,1)S(1)} collective-permute-done((bf16[16,1792]{1,0:T(8,128)(2,1)S(1)}, bf16[16,1792]{1,0:T(8,128)(2,1)S(1)}, u32[]{:S(2)}, u32[]{:S(2)}) %collective-permute-start.7) | collective-permute-done | bytes 57376 | tf_op jit(solution)/shard_map/ppermute | solution.py:210
  26.5 2.5 %collective-permute-done.8.refs_2_ = bf16[16,1792]{1,0:T(8,128)(2,1)S(1)} collective-permute-done((bf16[16,1792]{1,0:T(8,128)(2,1)S(1)}, bf16[16,1792]{1,0:T(8,128)(2,1)S(1)}, u32[]{:S(2)}, u32[]{:S(2)}) %collective-permute-start.8) | collective-permute-done | bytes 57376 | tf_op jit(solution)/shard_map/ppermute | solution.py:210
  29.0 0.0 collective-permute-done.9.refs_3_
  29.0 0.2 shard_map.73.gram_one
  29.2 0.1 collective-permute-start.10
  29.3 1.2 %collective-permute-done.10.gram_two = f32[64,64]{1,0:T(8,128)S(1)} collective-permute-done((f32[64,64]{1,0:T(8,128)S(1)}, f32[64,64]{1,0:T(8,128)S(1)}, u32[]{:S(2)}, u32[]{:S(2)}) %collective-permute-start.10) | collective-permute-done | bytes 16416 | tf_op jit(solution)/shard_map/ppermute | solution.py:210
  30.5 1.0 %shard_map.74 = (bf16[8,896]{1,0:T(8,128)(2,1)}, f32[8,896]{1,0:T(8,128)}) custom-call(f32[8,64]{1,0:T(8,128)S(1)} %get-tuple-element.15.partner_ref, f32[8,1792]{1,0:T(8,128)S(1)} %get-tuple-element.26.pooled_ref, f32[64,64]{1,0:T(8,128)S(1)} %shard_map.73.gram_one, f32[64,64]{1,0:T(8,128)S(1)} %collective-permute-done.10.gram_two, ...), custom_call_target="tpu_custom_call" | custom-call | tf_op jit(solution)/shard_map/pallas_call | solution.py:275
  (2 shorter events, 0.0 us)
Async XLA Ops:
  2.2 7.1 %collective-permute-start = (bf16[128,2304]{1,0:T(8,128)(2,1)S(1)}, bf16[128,2304]{1,0:T(8,128)(2,1)S(1)}, u32[]{:S(2)}, u32[]{:S(2)}) collective-permute-start(bf16[128,2304]{1,0:T(8,128)(2,1)S(1)} %get-tuple-element.19), channel_id=1, source_target_pairs={{0,1},{1,0},{2,3},{3,2},{4,5},{5,4},{6,7},{7,6},{8,9},{9,8},{10,11... | collective-permute-start | bytes 1769480 | tf_op jit(solution)/shard_map/ppermute | solution.py:210
  2.7 5.3 %collective-permute-start.1 = (bf16[128,256]{1,0:T(8,128)(2,1)S(1)}, bf16[128,256]{1,0:T(8,128)(2,1)S(1)}, u32[]{:S(2)}, u32[]{:S(2)}) collective-permute-start(bf16[128,256]{1,0:T(8,128)(2,1)S(1)} %get-tuple-element.18.k_own), channel_id=1, source_target_pairs={{0,2},{1,3},{2,0},{3,1},{4,6},{5,7},{6,4},{7,5},{8,10},{9,11},{10,... | collective-permute-start | bytes 196616 | tf_op jit(solution)/shard_map/ppermute | solution.py:210
  5.3 4.0 %collective-permute-start.2 = (bf16[128,256]{1,0:T(8,128)(2,1)S(1)}, bf16[128,256]{1,0:T(8,128)(2,1)S(1)}, u32[]{:S(2)}, u32[]{:S(2)}) collective-permute-start(bf16[128,256]{1,0:T(8,128)(2,1)S(1)} %get-tuple-element.20), channel_id=1, source_target_pairs={{0,3},{1,2},{2,1},{3,0},{4,7},{5,6},{6,5},{7,4},{8,11},{9,10},{10,... | collective-permute-start | bytes 196616 | tf_op jit(solution)/shard_map/ppermute | solution.py:210
  5.4 6.3 %collective-permute-start.3 = (bf16[128,256]{1,0:T(8,128)(2,1)S(1)}, bf16[128,256]{1,0:T(8,128)(2,1)S(1)}, u32[]{:S(2)}, u32[]{:S(2)}) collective-permute-start(bf16[128,256]{1,0:T(8,128)(2,1)S(1)} %get-tuple-element.22.v_own), channel_id=1, source_target_pairs={{0,2},{1,3},{2,0},{3,1},{4,6},{5,7},{6,4},{7,5},{8,10},{9,11},{10,... | collective-permute-start | bytes 196616 | tf_op jit(solution)/shard_map/ppermute | solution.py:210
  7.1 5.0 %collective-permute-start.4 = (bf16[128,256]{1,0:T(8,128)(2,1)S(1)}, bf16[128,256]{1,0:T(8,128)(2,1)S(1)}, u32[]{:S(2)}, u32[]{:S(2)}) collective-permute-start(bf16[128,256]{1,0:T(8,128)(2,1)S(1)} %get-tuple-element.23), channel_id=1, source_target_pairs={{0,3},{1,2},{2,1},{3,0},{4,7},{5,6},{6,5},{7,4},{8,11},{9,10},{10,... | collective-permute-start | bytes 196616 | tf_op jit(solution)/shard_map/ppermute | solution.py:210
  12.4 3.9 %collective-permute-start.5 = (bf16[8,1792]{1,0:T(8,128)(2,1)S(1)}, bf16[8,1792]{1,0:T(8,128)(2,1)S(1)}, u32[]{:S(2)}, u32[]{:S(2)}) collective-permute-start(bf16[8,1792]{1,0:T(8,128)(2,1)S(1)} %get-tuple-element.25), channel_id=1, source_target_pairs={{0,2},{1,3},{2,0},{3,1},{4,6},{5,7},{6,4},{7,5},{8,10},{9,11},{10,... | collective-permute-start | bytes 86024 | tf_op jit(solution)/shard_map/ppermute | solution.py:210
  16.3 3.9 %collective-permute-start.6 = (bf16[8,1792]{1,0:T(8,128)(2,1)S(1)}, bf16[8,1792]{1,0:T(8,128)(2,1)S(1)}, u32[]{:S(2)}, u32[]{:S(2)}) collective-permute-start(bf16[8,1792]{1,0:T(8,128)(2,1)S(1)} %get-tuple-element.27.refs_0_), channel_id=1, source_target_pairs={{0,4},{4,0},{8,12},{12,8},{16,20},{20,16},{24,28},{28,24},{1,5},{5... | collective-permute-start | bytes 86024 | tf_op jit(solution)/shard_map/ppermute | solution.py:210
  20.3 6.2 %collective-permute-start.7 = (bf16[16,1792]{1,0:T(8,128)(2,1)S(1)}, bf16[16,1792]{1,0:T(8,128)(2,1)S(1)}, u32[]{:S(2)}, u32[]{:S(2)}) collective-permute-start(bf16[16,1792]{1,0:T(8,128)(2,1)S(1)} %shard_map.72.refs_0_), channel_id=1, source_target_pairs={{0,24},{4,28},{8,16},{12,20},{16,8},{20,12},{24,0},{28,4},{1,25},{... | collective-permute-start | bytes 172040 | tf_op jit(solution)/shard_map/ppermute | solution.py:210
  24.0 5.1 %collective-permute-start.8 = (bf16[16,1792]{1,0:T(8,128)(2,1)S(1)}, bf16[16,1792]{1,0:T(8,128)(2,1)S(1)}, u32[]{:S(2)}, u32[]{:S(2)}) collective-permute-start(bf16[16,1792]{1,0:T(8,128)(2,1)S(1)} %shard_map.72.refs_0_), channel_id=1, source_target_pairs={{0,16},{4,20},{8,24},{12,28},{16,0},{20,4},{24,8},{28,12},{1,17},{... | collective-permute-start | bytes 172040 | tf_op jit(solution)/shard_map/ppermute | solution.py:210
  24.0 5.1 %collective-permute-start.9 = (bf16[16,1792]{1,0:T(8,128)(2,1)S(1)}, bf16[16,1792]{1,0:T(8,128)(2,1)S(1)}, u32[]{:S(2)}, u32[]{:S(2)}) collective-permute-start(bf16[16,1792]{1,0:T(8,128)(2,1)S(1)} %shard_map.72.refs_0_), channel_id=1, source_target_pairs={{0,8},{4,12},{8,0},{12,4},{16,24},{20,28},{24,16},{28,20},{1,9},{5... | collective-permute-start | bytes 172040 | tf_op jit(solution)/shard_map/ppermute | solution.py:210
  29.2 1.3 %collective-permute-start.10 = (f32[64,64]{1,0:T(8,128)S(1)}, f32[64,64]{1,0:T(8,128)S(1)}, u32[]{:S(2)}, u32[]{:S(2)}) collective-permute-start(f32[64,64]{1,0:T(8,128)S(1)} %shard_map.73.gram_one), channel_id=1, source_target_pairs={{0,1},{1,0},{2,3},{3,2},{4,5},{5,4},{6,7},{7,6},{8,9},{9,8},{10,11... | collective-permute-start | bytes 49160 | tf_op jit(solution)/shard_map/ppermute | solution.py:210

commit v2 on v1

--- a/solution.py
+++ b/solution.py
@@ -31,11 +31,15 @@
     return segment
 
 
+def group_of(p, role):
+    return role if p == 0 else KEY_VALUE_HEADS - 1 - role
+
+
 def plan_kernel(parts, lengths_hbm, pairs_hbm, q_hbm, k_hbm, v_hbm, *refs):
     q_out, k_out, v_out, near_out, k_far_out, v_far_out, bias_ref, doc_ref, partner_ref, lengths_ref, pairs_ref, sem, small_sem = refs
     span = k_hbm.shape[0]
     me = lax.axis_index("sp")
-    core = lax.rem(me, PAIR)
+    role = lax.rem(me, PAIR) ^ (me // PAIR)
     small = [
         pltpu.make_async_copy(lengths_hbm, lengths_ref, small_sem.at[0]),
         pltpu.make_async_copy(pairs_hbm, pairs_ref, small_sem.at[1]),
@@ -47,7 +51,7 @@
     def cut(source, other, target, start):
         width = source.shape[1] // KEY_VALUE_HEADS
         for p in range(PAIR):
-            first = pl.multiple_of((PAIR * p + (core ^ other)) * width, HEAD_SIZE)
+            first = pl.multiple_of(group_of(p, role ^ other) * width, HEAD_SIZE)
             copies.append(
                 pltpu.make_async_copy(
                     source.at[:, pl.ds(first, width)],
@@ -253,10 +257,10 @@
         moved=2 * tokens * features + 4 * keys.size,
     )(*(pltpu.with_memory_space_constraint(x, pltpu.HBM) for x in (document_lengths, pair_ids, queries, keys, values)))
     near = swap(near, "sp", parts, 1)
-    value_far = swap(value_own, "sp", parts, 2)
-    value_last = swap(value_send, "sp", parts, 3)
-    key_far = swap(key_own, "sp", parts, 2)
-    key_last = swap(key_send, "sp", parts, 3)
+    value_far = swap(value_send, "sp", parts, 2)
+    value_last = swap(value_own, "sp", parts, 3)
+    key_far = swap(key_send, "sp", parts, 2)
+    key_last = swap(key_own, "sp", parts, 3)
     sums = call(
         scores_kernel,
         struct((PAIR * HEAD_GROUP, parts * tokens), f32),
@@ -269,7 +273,7 @@
     )(sums, of_doc, value_own, near, value_far, value_last)
     pooled, sent = call(
         pool_kernel, (struct((DOCS, width), f32), struct((DOCS, width), bf16)), [VMEM] * 2
-    )(partial, swap(rounded, "sp", parts, 2))
+    )(partial, swap(rounded, "sp", parts, 3))
     blocks = gather_pairs(sent, "dp", replicas)
     gram = call(gram_kernel, struct((docs, docs), f32), [VMEM] * len(blocks))(*blocks)
     return call(

time: 31.7 us -> 31.9 us (level)
  waiting for transfers between devices: 13.1 us -> 13.5 us
    ppermute x11, waiting for transfers between devices: 13.1 us -> 13.5 us  [swap(): return lax.ppermute(block, axis, [(s, s ^ distance) for s in range(size)])]
  transfers between devices with their start and end apart: 11 -> 11, of which waited for: 8 -> 7; matrix products, arithmetic and copies ran while one was open for 0% -> 0% of each run, Pallas kernels for 7% -> 7%
where the time goes in v2:
time: 31.9 us; the launch traced here: 31.7 us
  waiting for transfers between devices  13.5 us (42%)
  starting transfers between devices  12.2 us (38%)
  Pallas kernels  5.35 us (17%)
  between operations  0.7 us (2%)
    ppermute x11, waiting for transfers between devices, swap(): return lax.ppermute(block, axis, [(s, s ^ distance) for s in range(size)])  13.5 us
    ppermute x11, starting transfers between devices, swap(): return lax.ppermute(block, axis, [(s, s ^ distance) for s in range(size)])  12.2 us
    pallas_call x1, Pallas kernels, per_device(): call(scores_kernel, struct((PAIR * HEAD_GROUP, parts * tokens), f32), [VM...  2.3 us
    pallas_call x1, Pallas kernels, per_device(): call(functools.partial(plan_kernel, parts), (struct((tokens, width), bf16...  1.59 us
    pallas_call x1, Pallas kernels, per_device(): call(grads_kernel, (struct((DOCS, features // parts), bf16), struct((DOCS...  1.02 us
  transfers between devices with their start and end apart: 11, of which 7 were waited for; matrix products, arithmetic and copies ran while one was open for 0% of the time, Pallas kernels for 7%

profile of v2, /device:TPU:0, one launch (start us, length us, event | category | flops | bytes accessed | tf_op | source)
XLA Modules:
  0.0 31.7 jit_solution(14117105771254962281)
XLA Ops:
  0.6 1.6 %shard_map.68 = (bf16[128,1792]{1,0:T(8,128)(2,1)S(1)}, bf16[128,256]{1,0:T(8,128)(2,1)S(1)}, bf16[128,256]{1,0:T(8,128)(2,1)S(1)}, bf16[128,2304]{1,0:T(8,128)(...) custom-call(s32[1,8]{1,0:T(1,128)} %lengths_hbm.1, ...), custom_call_target="tpu_custom_call" | custom-call | bytes 1179648 | tf_op jit(solution)/shard_map/pallas_call | solution.py:237
  2.2 0.5 %collective-permute-start = (bf16[128,2304]{1,0:T(8,128)(2,1)S(1)}, bf16[128,2304]{1,0:T(8,128)(2,1)S(1)}, u32[]{:S(2)}, u32[]{:S(2)}) collective-permute-start(bf16[128,2304]{1,0:T(8,128)(2,1)S(1)} %get-tuple-element.19), channel_id=1, source_target_pairs={{0,1},{1,0},{2,3},{3,2},{4,5},{5,4},{6,7},{7,6},{8,9},{9,8},{10,11... | collective-permute-start | bytes 1769480 | tf_op jit(solution)/shard_map/ppermute | solution.py:214
  2.8 2.6 %collective-permute-start.2 = (bf16[128,256]{1,0:T(8,128)(2,1)S(1)}, bf16[128,256]{1,0:T(8,128)(2,1)S(1)}, u32[]{:S(2)}, u32[]{:S(2)}) collective-permute-start(bf16[128,256]{1,0:T(8,128)(2,1)S(1)} %get-tuple-element.18.k_own), channel_id=1, source_target_pairs={{0,3},{1,2},{2,1},{3,0},{4,7},{5,6},{6,5},{7,4},{8,11},{9,10},{10,... | collective-permute-start | bytes 196616 | tf_op jit(solution)/shard_map/ppermute | solution.py:214
  5.4 0.0 collective-permute-start.1
  5.4 1.4 %collective-permute-start.4 = (bf16[128,256]{1,0:T(8,128)(2,1)S(1)}, bf16[128,256]{1,0:T(8,128)(2,1)S(1)}, u32[]{:S(2)}, u32[]{:S(2)}) collective-permute-start(bf16[128,256]{1,0:T(8,128)(2,1)S(1)} %get-tuple-element.22.v_own), channel_id=1, source_target_pairs={{0,3},{1,2},{2,1},{3,0},{4,7},{5,6},{6,5},{7,4},{8,11},{9,10},{10,... | collective-permute-start | bytes 196616 | tf_op jit(solution)/shard_map/ppermute | solution.py:214
  6.8 0.6 %collective-permute-start.3 = (bf16[128,256]{1,0:T(8,128)(2,1)S(1)}, bf16[128,256]{1,0:T(8,128)(2,1)S(1)}, u32[]{:S(2)}, u32[]{:S(2)}) collective-permute-start(bf16[128,256]{1,0:T(8,128)(2,1)S(1)} %get-tuple-element.23), channel_id=1, source_target_pairs={{0,2},{1,3},{2,0},{3,1},{4,6},{5,7},{6,4},{7,5},{8,10},{9,11},{10,... | collective-permute-start | bytes 196616 | tf_op jit(solution)/shard_map/ppermute | solution.py:214
  7.4 0.4 %collective-permute-done.2.k_last = bf16[128,256]{1,0:T(8,128)(2,1)S(1)} collective-permute-done((bf16[128,256]{1,0:T(8,128)(2,1)S(1)}, bf16[128,256]{1,0:T(8,128)(2,1)S(1)}, u32[]{:S(2)}, u32[]{:S(2)}) %collective-permute-start.2) | collective-permute-done | bytes 65568 | tf_op jit(solution)/shard_map/ppermute | solution.py:214
  7.8 2.3 %collective-permute-done.1.k_far = bf16[128,256]{1,0:T(8,128)(2,1)S(1)} collective-permute-done((bf16[128,256]{1,0:T(8,128)(2,1)S(1)}, bf16[128,256]{1,0:T(8,128)(2,1)S(1)}, u32[]{:S(2)}, u32[]{:S(2)}) %collective-permute-start.1) | collective-permute-done | bytes 65568 | tf_op jit(solution)/shard_map/ppermute | solution.py:214
  10.1 0.0 collective-permute-done.near
  10.1 2.3 %shard_map.69.sums_ref = f32[14,512]{1,0:T(8,128)S(1)} custom-call(f32[256,512]{1,0:T(8,128)S(1)} %get-tuple-element.16.bias_ref, bf16[128,1792]{1,0:T(8,128)(2,1)S(1)} %get-tuple-element.17.q_own, bf16[128,256]{1,0:T(8,128)(2,1)S(1)} %get-tuple-element.18.k_own, bf16[128,2304]{1,0:T(8,128)(2,1)S(1)} %collective-permute-done.near, ...), custom_call_target="tpu_custom_call" | custom-call | flops 234881024 | bytes 1966080 | tf_op jit(solution)/shard_map/pallas_call | solution.py:264
  12.4 0.0 collective-permute-done.4.v_last
  12.5 0.0 collective-permute-done.3.v_far
  12.5 0.2 shard_map.70
  12.7 0.7 %collective-permute-start.5 = (bf16[8,1792]{1,0:T(8,128)(2,1)S(1)}, bf16[8,1792]{1,0:T(8,128)(2,1)S(1)}, u32[]{:S(2)}, u32[]{:S(2)}) collective-permute-start(bf16[8,1792]{1,0:T(8,128)(2,1)S(1)} %get-tuple-element.25), channel_id=1, source_target_pairs={{0,3},{1,2},{2,1},{3,0},{4,7},{5,6},{6,5},{7,4},{8,11},{9,10},{10,... | collective-permute-start | bytes 86024 | tf_op jit(solution)/shard_map/ppermute | solution.py:214
  13.4 2.9 %collective-permute-done.5.two_ref = bf16[8,1792]{1,0:T(8,128)(2,1)S(1)} collective-permute-done((bf16[8,1792]{1,0:T(8,128)(2,1)S(1)}, bf16[8,1792]{1,0:T(8,128)(2,1)S(1)}, u32[]{:S(2)}, u32[]{:S(2)}) %collective-permute-start.5) | collective-permute-done | bytes 28704 | tf_op jit(solution)/shard_map/ppermute | solution.py:214
  16.3 1.8 %collective-permute-start.6 = (bf16[8,1792]{1,0:T(8,128)(2,1)S(1)}, bf16[8,1792]{1,0:T(8,128)(2,1)S(1)}, u32[]{:S(2)}, u32[]{:S(2)}) collective-permute-start(bf16[8,1792]{1,0:T(8,128)(2,1)S(1)} %get-tuple-element.27.refs_0_), channel_id=1, source_target_pairs={{0,4},{4,0},{8,12},{12,8},{16,20},{20,16},{24,28},{28,24},{1,5},{5... | collective-permute-start | bytes 86024 | tf_op jit(solution)/shard_map/ppermute | solution.py:214
  18.0 2.2 %collective-permute-done.6.refs_1_ = bf16[8,1792]{1,0:T(8,128)(2,1)S(1)} collective-permute-done((bf16[8,1792]{1,0:T(8,128)(2,1)S(1)}, bf16[8,1792]{1,0:T(8,128)(2,1)S(1)}, u32[]{:S(2)}, u32[]{:S(2)}) %collective-permute-start.6) | collective-permute-done | bytes 28704 | tf_op jit(solution)/shard_map/ppermute | solution.py:214
  20.2 3.9 %collective-permute-start.7 = (bf16[16,1792]{1,0:T(8,128)(2,1)S(1)}, bf16[16,1792]{1,0:T(8,128)(2,1)S(1)}, u32[]{:S(2)}, u32[]{:S(2)}) collective-permute-start(bf16[16,1792]{1,0:T(8,128)(2,1)S(1)} %shard_map.72.refs_0_), channel_id=1, source_target_pairs={{0,24},{4,28},{8,16},{12,20},{16,8},{20,12},{24,0},{28,4},{1,25},{... | collective-permute-start | bytes 172040 | tf_op jit(solution)/shard_map/ppermute | solution.py:214
  24.1 0.0 collective-permute-start.8
  24.1 0.6 %collective-permute-start.9 = (bf16[16,1792]{1,0:T(8,128)(2,1)S(1)}, bf16[16,1792]{1,0:T(8,128)(2,1)S(1)}, u32[]{:S(2)}, u32[]{:S(2)}) collective-permute-start(bf16[16,1792]{1,0:T(8,128)(2,1)S(1)} %shard_map.72.refs_0_), channel_id=1, source_target_pairs={{0,8},{4,12},{8,0},{12,4},{16,24},{20,28},{24,16},{28,20},{1,9},{5... | collective-permute-start | bytes 172040 | tf_op jit(solution)/shard_map/ppermute | solution.py:214
  24.7 1.8 %collective-permute-done.7.refs_1_ = bf16[16,1792]{1,0:T(8,128)(2,1)S(1)} collective-permute-done((bf16[16,1792]{1,0:T(8,128)(2,1)S(1)}, bf16[16,1792]{1,0:T(8,128)(2,1)S(1)}, u32[]{:S(2)}, u32[]{:S(2)}) %collective-permute-start.7) | collective-permute-done | bytes 57376 | tf_op jit(solution)/shard_map/ppermute | solution.py:214
  26.5 2.7 %collective-permute-done.8.refs_2_ = bf16[16,1792]{1,0:T(8,128)(2,1)S(1)} collective-permute-done((bf16[16,1792]{1,0:T(8,128)(2,1)S(1)}, bf16[16,1792]{1,0:T(8,128)(2,1)S(1)}, u32[]{:S(2)}, u32[]{:S(2)}) %collective-permute-start.8) | collective-permute-done | bytes 57376 | tf_op jit(solution)/shard_map/ppermute | solution.py:214
  29.2 0.0 collective-permute-done.9.refs_3_
  29.2 0.2 shard_map.73.gram_one
  29.4 0.1 collective-permute-start.10
  29.5 1.2 %collective-permute-done.10.gram_two = f32[64,64]{1,0:T(8,128)S(1)} collective-permute-done((f32[64,64]{1,0:T(8,128)S(1)}, f32[64,64]{1,0:T(8,128)S(1)}, u32[]{:S(2)}, u32[]{:S(2)}) %collective-permute-start.10) | collective-permute-done | bytes 16416 | tf_op jit(solution)/shard_map/ppermute | solution.py:214
  30.7 1.0 %shard_map.74 = (bf16[8,896]{1,0:T(8,128)(2,1)}, f32[8,896]{1,0:T(8,128)}) custom-call(f32[8,64]{1,0:T(8,128)S(1)} %get-tuple-element.15.partner_ref, f32[8,1792]{1,0:T(8,128)S(1)} %get-tuple-element.26.pooled_ref, f32[64,64]{1,0:T(8,128)S(1)} %shard_map.73.gram_one, f32[64,64]{1,0:T(8,128)S(1)} %collective-permute-done.10.gram_two, ...), custom_call_target="tpu_custom_call" | custom-call | tf_op jit(solution)/shard_map/pallas_call | solution.py:279
  (2 shorter events, 0.0 us)
Async XLA Ops:
  2.2 7.9 %collective-permute-start = (bf16[128,2304]{1,0:T(8,128)(2,1)S(1)}, bf16[128,2304]{1,0:T(8,128)(2,1)S(1)}, u32[]{:S(2)}, u32[]{:S(2)}) collective-permute-start(bf16[128,2304]{1,0:T(8,128)(2,1)S(1)} %get-tuple-element.19), channel_id=1, source_target_pairs={{0,1},{1,0},{2,3},{3,2},{4,5},{5,4},{6,7},{7,6},{8,9},{9,8},{10,11... | collective-permute-start | bytes 1769480 | tf_op jit(solution)/shard_map/ppermute | solution.py:214
  2.8 5.0 %collective-permute-start.2 = (bf16[128,256]{1,0:T(8,128)(2,1)S(1)}, bf16[128,256]{1,0:T(8,128)(2,1)S(1)}, u32[]{:S(2)}, u32[]{:S(2)}) collective-permute-start(bf16[128,256]{1,0:T(8,128)(2,1)S(1)} %get-tuple-element.18.k_own), channel_id=1, source_target_pairs={{0,3},{1,2},{2,1},{3,0},{4,7},{5,6},{6,5},{7,4},{8,11},{9,10},{10,... | collective-permute-start | bytes 196616 | tf_op jit(solution)/shard_map/ppermute | solution.py:214
  5.4 4.8 %collective-permute-start.1 = (bf16[128,256]{1,0:T(8,128)(2,1)S(1)}, bf16[128,256]{1,0:T(8,128)(2,1)S(1)}, u32[]{:S(2)}, u32[]{:S(2)}) collective-permute-start(bf16[128,256]{1,0:T(8,128)(2,1)S(1)} %get-tuple-element.20), channel_id=1, source_target_pairs={{0,2},{1,3},{2,0},{3,1},{4,6},{5,7},{6,4},{7,5},{8,10},{9,11},{10,... | collective-permute-start | bytes 196616 | tf_op jit(solution)/shard_map/ppermute | solution.py:214
  5.4 7.0 %collective-permute-start.4 = (bf16[128,256]{1,0:T(8,128)(2,1)S(1)}, bf16[128,256]{1,0:T(8,128)(2,1)S(1)}, u32[]{:S(2)}, u32[]{:S(2)}) collective-permute-start(bf16[128,256]{1,0:T(8,128)(2,1)S(1)} %get-tuple-element.22.v_own), channel_id=1, source_target_pairs={{0,3},{1,2},{2,1},{3,0},{4,7},{5,6},{6,5},{7,4},{8,11},{9,10},{10,... | collective-permute-start | bytes 196616 | tf_op jit(solution)/shard_map/ppermute | solution.py:214
  6.8 5.7 %collective-permute-start.3 = (bf16[128,256]{1,0:T(8,128)(2,1)S(1)}, bf16[128,256]{1,0:T(8,128)(2,1)S(1)}, u32[]{:S(2)}, u32[]{:S(2)}) collective-permute-start(bf16[128,256]{1,0:T(8,128)(2,1)S(1)} %get-tuple-element.23), channel_id=1, source_target_pairs={{0,2},{1,3},{2,0},{3,1},{4,6},{5,7},{6,4},{7,5},{8,10},{9,11},{10,... | collective-permute-start | bytes 196616 | tf_op jit(solution)/shard_map/ppermute | solution.py:214
  12.7 3.6 %collective-permute-start.5 = (bf16[8,1792]{1,0:T(8,128)(2,1)S(1)}, bf16[8,1792]{1,0:T(8,128)(2,1)S(1)}, u32[]{:S(2)}, u32[]{:S(2)}) collective-permute-start(bf16[8,1792]{1,0:T(8,128)(2,1)S(1)} %get-tuple-element.25), channel_id=1, source_target_pairs={{0,3},{1,2},{2,1},{3,0},{4,7},{5,6},{6,5},{7,4},{8,11},{9,10},{10,... | collective-permute-start | bytes 86024 | tf_op jit(solution)/shard_map/ppermute | solution.py:214
  16.3 3.9 %collective-permute-start.6 = (bf16[8,1792]{1,0:T(8,128)(2,1)S(1)}, bf16[8,1792]{1,0:T(8,128)(2,1)S(1)}, u32[]{:S(2)}, u32[]{:S(2)}) collective-permute-start(bf16[8,1792]{1,0:T(8,128)(2,1)S(1)} %get-tuple-element.27.refs_0_), channel_id=1, source_target_pairs={{0,4},{4,0},{8,12},{12,8},{16,20},{20,16},{24,28},{28,24},{1,5},{5... | collective-permute-start | bytes 86024 | tf_op jit(solution)/shard_map/ppermute | solution.py:214
  20.2 6.3 %collective-permute-start.7 = (bf16[16,1792]{1,0:T(8,128)(2,1)S(1)}, bf16[16,1792]{1,0:T(8,128)(2,1)S(1)}, u32[]{:S(2)}, u32[]{:S(2)}) collective-permute-start(bf16[16,1792]{1,0:T(8,128)(2,1)S(1)} %shard_map.72.refs_0_), channel_id=1, source_target_pairs={{0,24},{4,28},{8,16},{12,20},{16,8},{20,12},{24,0},{28,4},{1,25},{... | collective-permute-start | bytes 172040 | tf_op jit(solution)/shard_map/ppermute | solution.py:214
  24.1 5.1 %collective-permute-start.8 = (bf16[16,1792]{1,0:T(8,128)(2,1)S(1)}, bf16[16,1792]{1,0:T(8,128)(2,1)S(1)}, u32[]{:S(2)}, u32[]{:S(2)}) collective-permute-start(bf16[16,1792]{1,0:T(8,128)(2,1)S(1)} %shard_map.72.refs_0_), channel_id=1, source_target_pairs={{0,16},{4,20},{8,24},{12,28},{16,0},{20,4},{24,8},{28,12},{1,17},{... | collective-permute-start | bytes 172040 | tf_op jit(solution)/shard_map/ppermute | solution.py:214
  24.1 5.1 %collective-permute-start.9 = (bf16[16,1792]{1,0:T(8,128)(2,1)S(1)}, bf16[16,1792]{1,0:T(8,128)(2,1)S(1)}, u32[]{:S(2)}, u32[]{:S(2)}) collective-permute-start(bf16[16,1792]{1,0:T(8,128)(2,1)S(1)} %shard_map.72.refs_0_), channel_id=1, source_target_pairs={{0,8},{4,12},{8,0},{12,4},{16,24},{20,28},{24,16},{28,20},{1,9},{5... | collective-permute-start | bytes 172040 | tf_op jit(solution)/shard_map/ppermute | solution.py:214
  29.4 1.3 %collective-permute-start.10 = (f32[64,64]{1,0:T(8,128)S(1)}, f32[64,64]{1,0:T(8,128)S(1)}, u32[]{:S(2)}, u32[]{:S(2)}) collective-permute-start(f32[64,64]{1,0:T(8,128)S(1)} %shard_map.73.gram_one), channel_id=1, source_target_pairs={{0,1},{1,0},{2,3},{3,2},{4,5},{5,4},{6,7},{7,6},{8,9},{9,8},{10,11... | collective-permute-start | bytes 49160 | tf_op jit(solution)/shard_map/ppermute | solution.py:214

commit v3 on v1

--- a/solution.py
+++ b/solution.py
@@ -140,18 +140,18 @@
     sent_ref[...] = out_ref[...].astype(jnp.bfloat16)
 
 
-def pool_kernel(one_ref, two_ref, pooled_ref, sent_ref):
-    pooled = one_ref[...] + two_ref[...].astype(jnp.float32)
-    pooled_ref[...] = pooled
-    sent_ref[...] = pooled.astype(jnp.bfloat16)
+def pool_kernel(corner_ref, far_ref, next_ref, own_ref, sent_ref):
+    pooled = own_ref[...] + far_ref[...].astype(jnp.float32)
+    beside = next_ref[...].astype(jnp.float32) + corner_ref[...].astype(jnp.float32)
+    sent_ref[...] = jnp.concatenate([pooled, beside], axis=0).astype(jnp.bfloat16)
+
+
+def in_order(refs):
+    return (refs[-1], *refs[-3::-1], refs[-2])
 
 
 def join_kernel(*refs):
     refs[-1][...] = jnp.concatenate([ref[...] for ref in in_order(refs[:-1])], axis=0)
-
-
-def in_order(refs):
-    return (refs[0], *refs[:0:-1])
 
 
 def gram_kernel(*refs):
@@ -159,8 +159,8 @@
     refs[-1][...] = lax.dot_general(every, every, (((1,), (1,)), ((), ())), preferred_element_type=jnp.float32)
 
 
-def grads_kernel(partner_ref, pooled_ref, gram_one, gram_two, *refs):
-    every_refs, (emb_ref, grads_ref) = refs[:-2], refs[-2:]
+def grads_kernel(partner_ref, gram_one, gram_two, *refs):
+    every_refs, (own_ref, far_ref, emb_ref, grads_ref) = refs[:-4], refs[-4:]
     gram = gram_one[...] + gram_two[...]
     docs = gram.shape[0]
     columns = pl.ds(pl.multiple_of((lax.axis_index("sp") // PAIR) * GROUP_WIDTH, HEAD_SIZE), GROUP_WIDTH)
@@ -189,7 +189,8 @@
         low, every, preferred_element_type=jnp.float32
     )
     inverse = inverse_column[:DOCS]
-    embeddings = (pooled_ref[:, columns] * inverse).astype(jnp.bfloat16)
+    pooled = own_ref[:, columns] + far_ref[:, columns].astype(jnp.float32)
+    embeddings = (pooled * inverse).astype(jnp.bfloat16)
     emb_ref[...] = embeddings
     grads_ref[...] = (gradient - embeddings.astype(jnp.float32) * along) * inverse
 
@@ -211,13 +212,13 @@
 
 
 def gather_pairs(block, axis, size):
-    have, blocks = 1, [block]
+    have, blocks = PAIR, [block]
     while have < size:
-        if have > 1:
+        if have > PAIR:
             shape = (len(blocks) * block.shape[0], block.shape[1])
             block = call(join_kernel, jax.ShapeDtypeStruct(shape, block.dtype), [VMEM] * len(blocks))(*blocks)
-        radix = PAIR if have == 1 else min(4, size // have)
-        blocks = [block] + [swap(block, axis, size, r * have) for r in reversed(range(1, radix))]
+        radix = min(4, size // have)
+        blocks = [swap(block, axis, size, r * have) for r in (*range(radix - 2, 0, -1), radix - 1)] + [block]
         have *= radix
     return blocks
 
@@ -267,16 +268,17 @@
     partial, rounded = call(
         values_kernel, (struct((DOCS, width), f32), struct((DOCS, width), bf16)), [VMEM] * 6
     )(sums, of_doc, value_own, near, value_far, value_last)
-    pooled, sent = call(
-        pool_kernel, (struct((DOCS, width), f32), struct((DOCS, width), bf16)), [VMEM] * 2
-    )(partial, swap(rounded, "sp", parts, 2))
+    corner = swap(rounded, ("dp", "sp"), replicas * parts, parts + 2)
+    far = swap(rounded, "sp", parts, 2)
+    beside = swap(rounded, "dp", replicas, 1)
+    sent = call(pool_kernel, struct((PAIR * DOCS, width), bf16), [VMEM] * 4)(corner, far, beside, partial)
     blocks = gather_pairs(sent, "dp", replicas)
     gram = call(gram_kernel, struct((docs, docs), f32), [VMEM] * len(blocks))(*blocks)
     return call(
         grads_kernel,
         (struct((DOCS, features // parts), bf16), struct((DOCS, features // parts), f32)),
-        [VMEM] * (4 + len(blocks)),
-    )(partner, pooled, gram, swap(gram, "sp", parts, 1), *blocks)
+        [VMEM] * (5 + len(blocks)),
+    )(partner, gram, swap(gram, "sp", parts, 1), *blocks, partial, far)
 
 
 def solution(mesh):

time: 31.7 us -> 30.7 us (0.968)
  waiting for transfers between devices: 13.1 us -> 11.6 us
  starting transfers between devices: 12.4 us -> 13 us
    ppermute x11 -> x12, waiting for transfers between devices: 13.1 us -> 11.6 us  [swap(): return lax.ppermute(block, axis, [(s, s ^ distance) for s in range(size)])]
    ppermute x11 -> x12, starting transfers between devices: 12.4 us -> 13 us  [swap(): return lax.ppermute(block, axis, [(s, s ^ distance) for s in range(size)])]
  transfers between devices with their start and end apart: 11 -> 12, of which waited for: 8 -> 9; matrix products, arithmetic and copies ran while one was open for 0% -> 0% of each run, Pallas kernels for 7% -> 8%
where the time goes in v3:
time: 30.7 us; the launch traced here: 30.6 us
  starting transfers between devices  13 us (42%)
  waiting for transfers between devices  11.6 us (38%)
  Pallas kernels  5.35 us (17%)
  between operations  0.69 us (2%)
    ppermute x12, starting transfers between devices, swap(): return lax.ppermute(block, axis, [(s, s ^ distance) for s in range(size)])  13 us
    ppermute x12, waiting for transfers between devices, swap(): return lax.ppermute(block, axis, [(s, s ^ distance) for s in range(size)])  11.6 us
    pallas_call x1, Pallas kernels, per_device(): call(scores_kernel, struct((PAIR * HEAD_GROUP, parts * tokens), f32), [VM...  2.3 us
    pallas_call x1, Pallas kernels, per_device(): call(functools.partial(plan_kernel, parts), (struct((tokens, width), bf16...  1.59 us
    pallas_call x1, Pallas kernels, per_device(): call(grads_kernel, (struct((DOCS, features // parts), bf16), struct((DOCS...  1.02 us
  transfers between devices with their start and end apart: 12, of which 9 were waited for; matrix products, arithmetic and copies ran while one was open for 0% of the time, Pallas kernels for 8%

profile of v3, /device:TPU:0, one launch (start us, length us, event | category | flops | bytes accessed | tf_op | source)
XLA Modules:
  0.0 30.6 jit_solution(3389983113676299229)
XLA Ops:
  0.6 1.6 %shard_map.68 = (bf16[128,1792]{1,0:T(8,128)(2,1)S(1)}, bf16[128,256]{1,0:T(8,128)(2,1)S(1)}, bf16[128,256]{1,0:T(8,128)(2,1)S(1)}, bf16[128,2304]{1,0:T(8,128)(...) custom-call(s32[1,8]{1,0:T(1,128)} %lengths_hbm.1, ...), custom_call_target="tpu_custom_call" | custom-call | bytes 1179648 | tf_op jit(solution)/shard_map/pallas_call | solution.py:234
  2.2 0.5 %collective-permute-start = (bf16[128,2304]{1,0:T(8,128)(2,1)S(1)}, bf16[128,2304]{1,0:T(8,128)(2,1)S(1)}, u32[]{:S(2)}, u32[]{:S(2)}) collective-permute-start(bf16[128,2304]{1,0:T(8,128)(2,1)S(1)} %get-tuple-element.17), channel_id=1, source_target_pairs={{0,1},{1,0},{2,3},{3,2},{4,5},{5,4},{6,7},{7,6},{8,9},{9,8},{10,11... | collective-permute-start | bytes 1769480 | tf_op jit(solution)/shard_map/ppermute | solution.py:211
  2.7 2.6 %collective-permute-start.1 = (bf16[128,256]{1,0:T(8,128)(2,1)S(1)}, bf16[128,256]{1,0:T(8,128)(2,1)S(1)}, u32[]{:S(2)}, u32[]{:S(2)}) collective-permute-start(bf16[128,256]{1,0:T(8,128)(2,1)S(1)} %get-tuple-element.16.k_own), channel_id=1, source_target_pairs={{0,2},{1,3},{2,0},{3,1},{4,6},{5,7},{6,4},{7,5},{8,10},{9,11},{10,... | collective-permute-start | bytes 196616 | tf_op jit(solution)/shard_map/ppermute | solution.py:211
  5.3 0.1 collective-permute-start.2
  5.4 1.7 %collective-permute-start.3 = (bf16[128,256]{1,0:T(8,128)(2,1)S(1)}, bf16[128,256]{1,0:T(8,128)(2,1)S(1)}, u32[]{:S(2)}, u32[]{:S(2)}) collective-permute-start(bf16[128,256]{1,0:T(8,128)(2,1)S(1)} %get-tuple-element.20.v_own), channel_id=1, source_target_pairs={{0,2},{1,3},{2,0},{3,1},{4,6},{5,7},{6,4},{7,5},{8,10},{9,11},{10,... | collective-permute-start | bytes 196616 | tf_op jit(solution)/shard_map/ppermute | solution.py:211
  7.1 0.0 collective-permute-start.4
  7.1 0.9 %collective-permute-done.1.k_far = bf16[128,256]{1,0:T(8,128)(2,1)S(1)} collective-permute-done((bf16[128,256]{1,0:T(8,128)(2,1)S(1)}, bf16[128,256]{1,0:T(8,128)(2,1)S(1)}, u32[]{:S(2)}, u32[]{:S(2)}) %collective-permute-start.1) | collective-permute-done | bytes 65568 | tf_op jit(solution)/shard_map/ppermute | solution.py:211
  8.0 1.4 %collective-permute-done.2.k_last = bf16[128,256]{1,0:T(8,128)(2,1)S(1)} collective-permute-done((bf16[128,256]{1,0:T(8,128)(2,1)S(1)}, bf16[128,256]{1,0:T(8,128)(2,1)S(1)}, u32[]{:S(2)}, u32[]{:S(2)}) %collective-permute-start.2) | collective-permute-done | bytes 65568 | tf_op jit(solution)/shard_map/ppermute | solution.py:211
  9.4 0.0 collective-permute-done.near
  9.4 2.3 %shard_map.69.sums_ref = f32[14,512]{1,0:T(8,128)S(1)} custom-call(f32[256,512]{1,0:T(8,128)S(1)} %get-tuple-element.14.bias_ref, bf16[128,1792]{1,0:T(8,128)(2,1)S(1)} %get-tuple-element.15.q_own, bf16[128,256]{1,0:T(8,128)(2,1)S(1)} %get-tuple-element.16.k_own, bf16[128,2304]{1,0:T(8,128)(2,1)S(1)} %collective-permute-done.near, ...), custom_call_target="tpu_custom_call" | custom-call | flops 234881024 | bytes 1966080 | tf_op jit(solution)/shard_map/pallas_call | solution.py:261
  11.7 0.0 collective-permute-done.3.v_far
  11.7 0.5 %collective-permute-done.4.v_last = bf16[128,256]{1,0:T(8,128)(2,1)S(1)} collective-permute-done((bf16[128,256]{1,0:T(8,128)(2,1)S(1)}, bf16[128,256]{1,0:T(8,128)(2,1)S(1)}, u32[]{:S(2)}, u32[]{:S(2)}) %collective-permute-start.4) | collective-permute-done | bytes 65568 | tf_op jit(solution)/shard_map/ppermute | solution.py:211
  12.2 0.2 shard_map.70
  12.4 2.4 %collective-permute-start.5 = (bf16[8,1792]{1,0:T(8,128)(2,1)S(1)}, bf16[8,1792]{1,0:T(8,128)(2,1)S(1)}, u32[]{:S(2)}, u32[]{:S(2)}) collective-permute-start(bf16[8,1792]{1,0:T(8,128)(2,1)S(1)} %get-tuple-element.22), channel_id=1, source_target_pairs={{0,6},{1,7},{2,4},{3,5},{4,2},{5,3},{6,0},{7,1},{8,14},{9,15},{10,... | collective-permute-start | bytes 86024 | tf_op jit(solution)/shard_map/ppermute | solution.py:211
  14.8 0.7 %collective-permute-start.6 = (bf16[8,1792]{1,0:T(8,128)(2,1)S(1)}, bf16[8,1792]{1,0:T(8,128)(2,1)S(1)}, u32[]{:S(2)}, u32[]{:S(2)}) collective-permute-start(bf16[8,1792]{1,0:T(8,128)(2,1)S(1)} %get-tuple-element.22), channel_id=1, source_target_pairs={{0,2},{1,3},{2,0},{3,1},{4,6},{5,7},{6,4},{7,5},{8,10},{9,11},{10,... | collective-permute-start | bytes 86024 | tf_op jit(solution)/shard_map/ppermute | solution.py:211
  15.4 0.5 %collective-permute-start.7 = (bf16[8,1792]{1,0:T(8,128)(2,1)S(1)}, bf16[8,1792]{1,0:T(8,128)(2,1)S(1)}, u32[]{:S(2)}, u32[]{:S(2)}) collective-permute-start(bf16[8,1792]{1,0:T(8,128)(2,1)S(1)} %get-tuple-element.22), channel_id=1, source_target_pairs={{0,4},{4,0},{8,12},{12,8},{16,20},{20,16},{24,28},{28,24},{1,5},{5... | collective-permute-start | bytes 86024 | tf_op jit(solution)/shard_map/ppermute | solution.py:211
  15.9 1.3 %collective-permute-done.5.corner_ref = bf16[8,1792]{1,0:T(8,128)(2,1)S(1)} collective-permute-done((bf16[8,1792]{1,0:T(8,128)(2,1)S(1)}, bf16[8,1792]{1,0:T(8,128)(2,1)S(1)}, u32[]{:S(2)}, u32[]{:S(2)}) %collective-permute-start.5) | collective-permute-done | bytes 28704 | tf_op jit(solution)/shard_map/ppermute | solution.py:211
  17.2 1.4 %collective-permute-done.6.far_ref.refs_5_ = bf16[8,1792]{1,0:T(8,128)(2,1)S(1)} collective-permute-done((bf16[8,1792]{1,0:T(8,128)(2,1)S(1)}, bf16[8,1792]{1,0:T(8,128)(2,1)S(1)}, u32[]{:S(2)}, u32[]{:S(2)}) %collective-permute-start.6) | collective-permute-done | bytes 28704 | tf_op jit(solution)/shard_map/ppermute | solution.py:211
  18.6 0.7 %collective-permute-done.7.next_ref = bf16[8,1792]{1,0:T(8,128)(2,1)S(1)} collective-permute-done((bf16[8,1792]{1,0:T(8,128)(2,1)S(1)}, bf16[8,1792]{1,0:T(8,128)(2,1)S(1)}, u32[]{:S(2)}, u32[]{:S(2)}) %collective-permute-start.7) | collective-permute-done | bytes 28704 | tf_op jit(solution)/shard_map/ppermute | solution.py:211
  19.3 3.7 %collective-permute-start.10 = (bf16[16,1792]{1,0:T(8,128)(2,1)S(1)}, bf16[16,1792]{1,0:T(8,128)(2,1)S(1)}, u32[]{:S(2)}, u32[]{:S(2)}) collective-permute-start(bf16[16,1792]{1,0:T(8,128)(2,1)S(1)} %shard_map.71.refs_3_), channel_id=1, source_target_pairs={{0,24},{4,28},{8,16},{12,20},{16,8},{20,12},{24,0},{28,4},{1,25},{... | collective-permute-start | bytes 172040 | tf_op jit(solution)/shard_map/ppermute | solution.py:211
  23.0 0.0 collective-permute-start.8
  23.0 0.8 %collective-permute-start.9 = (bf16[16,1792]{1,0:T(8,128)(2,1)S(1)}, bf16[16,1792]{1,0:T(8,128)(2,1)S(1)}, u32[]{:S(2)}, u32[]{:S(2)}) collective-permute-start(bf16[16,1792]{1,0:T(8,128)(2,1)S(1)} %shard_map.71.refs_3_), channel_id=1, source_target_pairs={{0,8},{4,12},{8,0},{12,4},{16,24},{20,28},{24,16},{28,20},{1,9},{5... | collective-permute-start | bytes 172040 | tf_op jit(solution)/shard_map/ppermute | solution.py:211
  23.8 1.7 %collective-permute-done.10.refs_2_ = bf16[16,1792]{1,0:T(8,128)(2,1)S(1)} collective-permute-done((bf16[16,1792]{1,0:T(8,128)(2,1)S(1)}, bf16[16,1792]{1,0:T(8,128)(2,1)S(1)}, u32[]{:S(2)}, u32[]{:S(2)}) %collective-permute-start.10) | collective-permute-done | bytes 57376 | tf_op jit(solution)/shard_map/ppermute | solution.py:211
  25.5 2.6 %collective-permute-done.8.refs_0_ = bf16[16,1792]{1,0:T(8,128)(2,1)S(1)} collective-permute-done((bf16[16,1792]{1,0:T(8,128)(2,1)S(1)}, bf16[16,1792]{1,0:T(8,128)(2,1)S(1)}, u32[]{:S(2)}, u32[]{:S(2)}) %collective-permute-start.8) | collective-permute-done | bytes 57376 | tf_op jit(solution)/shard_map/ppermute | solution.py:211
  28.1 0.0 collective-permute-done.9.refs_1_
  28.1 0.2 shard_map.72.gram_one
  28.3 0.1 collective-permute-start.11
  28.4 1.2 %collective-permute-done.11.gram_two = f32[64,64]{1,0:T(8,128)S(1)} collective-permute-done((f32[64,64]{1,0:T(8,128)S(1)}, f32[64,64]{1,0:T(8,128)S(1)}, u32[]{:S(2)}, u32[]{:S(2)}) %collective-permute-start.11) | collective-permute-done | bytes 16416 | tf_op jit(solution)/shard_map/ppermute | solution.py:211
  29.6 1.0 %shard_map.73 = (bf16[8,896]{1,0:T(8,128)(2,1)}, f32[8,896]{1,0:T(8,128)}) custom-call(f32[8,64]{1,0:T(8,128)S(1)} %get-tuple-element.13.partner_ref, f32[64,64]{1,0:T(8,128)S(1)} %shard_map.72.gram_one, f32[64,64]{1,0:T(8,128)S(1)} %collective-permute-done.11.gram_two, bf16[16,1792]{1,0:T(8,128)(2,1)S(1)} %collective-permute-done.8.refs_0_, ...), custom_call_target="tpu_custom_call" | custom-call | tf_op jit(solution)/shard_map/pallas_call | solution.py:277
  (1 shorter events, 0.0 us)
Async XLA Ops:
  2.2 7.1 %collective-permute-start = (bf16[128,2304]{1,0:T(8,128)(2,1)S(1)}, bf16[128,2304]{1,0:T(8,128)(2,1)S(1)}, u32[]{:S(2)}, u32[]{:S(2)}) collective-permute-start(bf16[128,2304]{1,0:T(8,128)(2,1)S(1)} %get-tuple-element.17), channel_id=1, source_target_pairs={{0,1},{1,0},{2,3},{3,2},{4,5},{5,4},{6,7},{7,6},{8,9},{9,8},{10,11... | collective-permute-start | bytes 1769480 | tf_op jit(solution)/shard_map/ppermute | solution.py:211
  2.7 5.3 %collective-permute-start.1 = (bf16[128,256]{1,0:T(8,128)(2,1)S(1)}, bf16[128,256]{1,0:T(8,128)(2,1)S(1)}, u32[]{:S(2)}, u32[]{:S(2)}) collective-permute-start(bf16[128,256]{1,0:T(8,128)(2,1)S(1)} %get-tuple-element.16.k_own), channel_id=1, source_target_pairs={{0,2},{1,3},{2,0},{3,1},{4,6},{5,7},{6,4},{7,5},{8,10},{9,11},{10,... | collective-permute-start | bytes 196616 | tf_op jit(solution)/shard_map/ppermute | solution.py:211
  5.3 4.0 %collective-permute-start.2 = (bf16[128,256]{1,0:T(8,128)(2,1)S(1)}, bf16[128,256]{1,0:T(8,128)(2,1)S(1)}, u32[]{:S(2)}, u32[]{:S(2)}) collective-permute-start(bf16[128,256]{1,0:T(8,128)(2,1)S(1)} %get-tuple-element.18), channel_id=1, source_target_pairs={{0,3},{1,2},{2,1},{3,0},{4,7},{5,6},{6,5},{7,4},{8,11},{9,10},{10,... | collective-permute-start | bytes 196616 | tf_op jit(solution)/shard_map/ppermute | solution.py:211
  5.4 6.3 %collective-permute-start.3 = (bf16[128,256]{1,0:T(8,128)(2,1)S(1)}, bf16[128,256]{1,0:T(8,128)(2,1)S(1)}, u32[]{:S(2)}, u32[]{:S(2)}) collective-permute-start(bf16[128,256]{1,0:T(8,128)(2,1)S(1)} %get-tuple-element.20.v_own), channel_id=1, source_target_pairs={{0,2},{1,3},{2,0},{3,1},{4,6},{5,7},{6,4},{7,5},{8,10},{9,11},{10,... | collective-permute-start | bytes 196616 | tf_op jit(solution)/shard_map/ppermute | solution.py:211
  7.1 5.0 %collective-permute-start.4 = (bf16[128,256]{1,0:T(8,128)(2,1)S(1)}, bf16[128,256]{1,0:T(8,128)(2,1)S(1)}, u32[]{:S(2)}, u32[]{:S(2)}) collective-permute-start(bf16[128,256]{1,0:T(8,128)(2,1)S(1)} %get-tuple-element.21), channel_id=1, source_target_pairs={{0,3},{1,2},{2,1},{3,0},{4,7},{5,6},{6,5},{7,4},{8,11},{9,10},{10,... | collective-permute-start | bytes 196616 | tf_op jit(solution)/shard_map/ppermute | solution.py:211
  12.4 4.8 %collective-permute-start.5 = (bf16[8,1792]{1,0:T(8,128)(2,1)S(1)}, bf16[8,1792]{1,0:T(8,128)(2,1)S(1)}, u32[]{:S(2)}, u32[]{:S(2)}) collective-permute-start(bf16[8,1792]{1,0:T(8,128)(2,1)S(1)} %get-tuple-element.22), channel_id=1, source_target_pairs={{0,6},{1,7},{2,4},{3,5},{4,2},{5,3},{6,0},{7,1},{8,14},{9,15},{10,... | collective-permute-start | bytes 86024 | tf_op jit(solution)/shard_map/ppermute | solution.py:211
  14.8 3.9 %collective-permute-start.6 = (bf16[8,1792]{1,0:T(8,128)(2,1)S(1)}, bf16[8,1792]{1,0:T(8,128)(2,1)S(1)}, u32[]{:S(2)}, u32[]{:S(2)}) collective-permute-start(bf16[8,1792]{1,0:T(8,128)(2,1)S(1)} %get-tuple-element.22), channel_id=1, source_target_pairs={{0,2},{1,3},{2,0},{3,1},{4,6},{5,7},{6,4},{7,5},{8,10},{9,11},{10,... | collective-permute-start | bytes 86024 | tf_op jit(solution)/shard_map/ppermute | solution.py:211
  15.4 3.9 %collective-permute-start.7 = (bf16[8,1792]{1,0:T(8,128)(2,1)S(1)}, bf16[8,1792]{1,0:T(8,128)(2,1)S(1)}, u32[]{:S(2)}, u32[]{:S(2)}) collective-permute-start(bf16[8,1792]{1,0:T(8,128)(2,1)S(1)} %get-tuple-element.22), channel_id=1, source_target_pairs={{0,4},{4,0},{8,12},{12,8},{16,20},{20,16},{24,28},{28,24},{1,5},{5... | collective-permute-start | bytes 86024 | tf_op jit(solution)/shard_map/ppermute | solution.py:211
  19.3 6.1 %collective-permute-start.10 = (bf16[16,1792]{1,0:T(8,128)(2,1)S(1)}, bf16[16,1792]{1,0:T(8,128)(2,1)S(1)}, u32[]{:S(2)}, u32[]{:S(2)}) collective-permute-start(bf16[16,1792]{1,0:T(8,128)(2,1)S(1)} %shard_map.71.refs_3_), channel_id=1, source_target_pairs={{0,24},{4,28},{8,16},{12,20},{16,8},{20,12},{24,0},{28,4},{1,25},{... | collective-permute-start | bytes 172040 | tf_op jit(solution)/shard_map/ppermute | solution.py:211
  23.0 5.1 %collective-permute-start.8 = (bf16[16,1792]{1,0:T(8,128)(2,1)S(1)}, bf16[16,1792]{1,0:T(8,128)(2,1)S(1)}, u32[]{:S(2)}, u32[]{:S(2)}) collective-permute-start(bf16[16,1792]{1,0:T(8,128)(2,1)S(1)} %shard_map.71.refs_3_), channel_id=1, source_target_pairs={{0,16},{4,20},{8,24},{12,28},{16,0},{20,4},{24,8},{28,12},{1,17},{... | collective-permute-start | bytes 172040 | tf_op jit(solution)/shard_map/ppermute | solution.py:211
  23.0 5.1 %collective-permute-start.9 = (bf16[16,1792]{1,0:T(8,128)(2,1)S(1)}, bf16[16,1792]{1,0:T(8,128)(2,1)S(1)}, u32[]{:S(2)}, u32[]{:S(2)}) collective-permute-start(bf16[16,1792]{1,0:T(8,128)(2,1)S(1)} %shard_map.71.refs_3_), channel_id=1, source_target_pairs={{0,8},{4,12},{8,0},{12,4},{16,24},{20,28},{24,16},{28,20},{1,9},{5... | collective-permute-start | bytes 172040 | tf_op jit(solution)/shard_map/ppermute | solution.py:211
  28.3 1.3 %collective-permute-start.11 = (f32[64,64]{1,0:T(8,128)S(1)}, f32[64,64]{1,0:T(8,128)S(1)}, u32[]{:S(2)}, u32[]{:S(2)}) collective-permute-start(f32[64,64]{1,0:T(8,128)S(1)} %shard_map.72.gram_one), channel_id=1, source_target_pairs={{0,1},{1,0},{2,3},{3,2},{4,5},{5,4},{6,7},{7,6},{8,9},{9,8},{10,11... | collective-permute-start | bytes 49160 | tf_op jit(solution)/shard_map/ppermute | solution.py:211

commit v4 on v3

--- a/solution.py
+++ b/solution.py
@@ -31,41 +31,49 @@
     return segment
 
 
-def plan_kernel(parts, lengths_hbm, pairs_hbm, q_hbm, k_hbm, v_hbm, *refs):
-    q_out, k_out, v_out, near_out, k_far_out, v_far_out, bias_ref, doc_ref, partner_ref, lengths_ref, pairs_ref, sem, small_sem = refs
-    span = k_hbm.shape[0]
+def group_columns(ref, group):
+    width = ref.shape[1] // KEY_VALUE_HEADS
+    return ref.at[:, pl.ds(pl.multiple_of(group * width, HEAD_SIZE), width)]
+
+
+def cut_kernel(k_hbm, v_hbm, k_out, v_out, near_out, k_far_out, v_far_out, sem):
+    core = lax.rem(lax.axis_index("sp"), PAIR)
+    plans = [(k_hbm, 0, k_out, 0), (k_hbm, 1, k_far_out, 0), (k_hbm, 1, near_out, 0)]
+    plans += [(v_hbm, 1, near_out, PAIR), (v_hbm, 0, v_out, 0), (v_hbm, 1, v_far_out, 0)]
+    copies = []
+    for source, other, target, start in plans:
+        for p in range(PAIR):
+            first = (start + p) * HEAD_SIZE
+            copies.append(
+                pltpu.make_async_copy(
+                    group_columns(source, PAIR * p + (core ^ other)),
+                    target.at[:, first : first + HEAD_SIZE],
+                    sem.at[len(copies)],
+                )
+            )
+    for copy in copies:
+        copy.start()
+    for copy in copies:
+        copy.wait()
+
+
+def plan_kernel(parts, lengths_hbm, pairs_hbm, q_hbm, q_out, bias_ref, doc_ref, partner_ref, lengths_ref, pairs_ref, sem):
+    span = q_hbm.shape[0]
     me = lax.axis_index("sp")
     core = lax.rem(me, PAIR)
     small = [
-        pltpu.make_async_copy(lengths_hbm, lengths_ref, small_sem.at[0]),
-        pltpu.make_async_copy(pairs_hbm, pairs_ref, small_sem.at[1]),
+        pltpu.make_async_copy(lengths_hbm, lengths_ref, sem.at[PAIR]),
+        pltpu.make_async_copy(pairs_hbm, pairs_ref, sem.at[PAIR + 1]),
     ]
-    for copy in small:
-        copy.start()
-    copies = []
-
-    def cut(source, other, target, start):
-        width = source.shape[1] // KEY_VALUE_HEADS
-        for p in range(PAIR):
-            first = pl.multiple_of((PAIR * p + (core ^ other)) * width, HEAD_SIZE)
-            copies.append(
-                pltpu.make_async_copy(
-                    source.at[:, pl.ds(first, width)],
-                    target.at[:, start + p * width : start + (p + 1) * width],
-                    sem.at[len(copies)],
-                )
-            )
-
-    pair_width = PAIR * HEAD_SIZE
-    cut(k_hbm, 0, k_out, 0)
-    cut(k_hbm, 1, k_far_out, 0)
-    cut(k_hbm, 1, near_out, PAIR * GROUP_WIDTH)
-    cut(q_hbm, 1, near_out, 0)
-    cut(v_hbm, 1, near_out, PAIR * GROUP_WIDTH + pair_width)
-    cut(v_hbm, 0, v_out, 0)
-    cut(v_hbm, 1, v_far_out, 0)
-    cut(q_hbm, 0, q_out, 0)
-    for copy in copies:
+    copies = [
+        pltpu.make_async_copy(
+            group_columns(q_hbm, PAIR * p + core),
+            q_out.at[:, p * GROUP_WIDTH : (p + 1) * GROUP_WIDTH],
+            sem.at[p],
+        )
+        for p in range(PAIR)
+    ]
+    for copy in small + copies:
         copy.start()
     for copy in small:
         copy.wait()
@@ -94,19 +102,17 @@
         copy.wait()
 
 
-def scores_kernel(bias_ref, q_own, k_own, near, k_far, k_last, sums_ref):
+def scores_kernel(bias_ref, q_own, q_near, k_own, near, k_far, k_last, sums_ref):
+    core = lax.rem(lax.axis_index("sp"), PAIR)
     scale = HEAD_SIZE ** (-0.5) * math.log2(math.e)
     for p in range(PAIR):
         here = slice(p * HEAD_SIZE, (p + 1) * HEAD_SIZE)
-        beside = PAIR * GROUP_WIDTH + p * HEAD_SIZE
-        key_head = jnp.concatenate(
-            [k_own[:, here], near[:, beside : beside + HEAD_SIZE], k_far[:, here], k_last[:, here]], axis=0
-        )
+        key_head = jnp.concatenate([k[:, here] for k in (k_own, near, k_far, k_last)], axis=0)
         for h in range(HEAD_GROUP):
             place = (p * HEAD_GROUP + h) * HEAD_SIZE
+            beside = pl.multiple_of((PAIR * p + core) * GROUP_WIDTH + h * HEAD_SIZE, HEAD_SIZE)
             total = None
-            for t, q_ref in enumerate((q_own, near)):
-                query = q_ref[:, place : place + HEAD_SIZE]
+            for t, query in enumerate((q_own[:, place : place + HEAD_SIZE], q_near[:, pl.ds(beside, HEAD_SIZE)])):
                 rows = query.shape[0]
                 scores = lax.dot_general(
                     query, key_head, (((1,), (1,)), ((), ())), preferred_element_type=jnp.float32
@@ -124,7 +130,7 @@
 def values_kernel(sums_ref, doc_ref, v_own, near, v_far, v_last, out_ref, sent_ref):
     for p in range(PAIR):
         here = slice(p * HEAD_SIZE, (p + 1) * HEAD_SIZE)
-        beside = PAIR * (GROUP_WIDTH + HEAD_SIZE) + p * HEAD_SIZE
+        beside = (PAIR + p) * HEAD_SIZE
         value_head = jnp.concatenate(
             [v_own[:, here], near[:, beside : beside + HEAD_SIZE], v_far[:, here], v_last[:, here]], axis=0
         )
@@ -147,7 +153,7 @@
 
 
 def in_order(refs):
-    return (refs[-1], *refs[-3::-1], refs[-2])
+    return (refs[-1], refs[0], *refs[-2:0:-1])
 
 
 def join_kernel(*refs):
@@ -218,7 +224,7 @@
             shape = (len(blocks) * block.shape[0], block.shape[1])
             block = call(join_kernel, jax.ShapeDtypeStruct(shape, block.dtype), [VMEM] * len(blocks))(*blocks)
         radix = min(4, size // have)
-        blocks = [swap(block, axis, size, r * have) for r in (*range(radix - 2, 0, -1), radix - 1)] + [block]
+        blocks = [swap(block, axis, size, r * have) for r in (1, *range(radix - 1, 1, -1))] + [block]
         have *= radix
     return blocks
 
@@ -231,40 +237,44 @@
     docs = DOCS * replicas
     f32, bf16 = jnp.float32, jnp.bfloat16
     struct = jax.ShapeDtypeStruct
-    query_own, key_own, value_own, near, key_send, value_send, bias, of_doc, partner = call(
+    query_near = swap(queries, "sp", parts, 1)
+    near_cut = struct((tokens, kv_width), bf16)
+    arguments = [pltpu.with_memory_space_constraint(x, pltpu.HBM) for x in (document_lengths, pair_ids, queries, keys, values)]
+    key_own, value_own, near, key_send, value_send = call(
+        cut_kernel,
+        (near_cut, near_cut, struct((tokens, 2 * kv_width), bf16), near_cut, near_cut),
+        [HBM] * 2,
+        [pltpu.SemaphoreType.DMA((6 * PAIR,))],
+        moved=8 * keys.size,
+    )(*arguments[3:])
+    query_own, bias, of_doc, partner = call(
         functools.partial(plan_kernel, parts),
         (
             struct((tokens, width), bf16),
-            struct((tokens, kv_width), bf16),
-            struct((tokens, kv_width), bf16),
-            struct((tokens, width + 2 * kv_width), bf16),
-            struct((tokens, kv_width), bf16),
-            struct((tokens, kv_width), bf16),
             struct((PAIR * tokens, parts * tokens), f32),
             struct((DOCS, parts * tokens), f32),
             struct((DOCS, docs), f32),
         ),
-        [HBM] * 5,
+        [HBM] * 3,
         [
             pltpu.SMEM((1, DOCS), jnp.int32),
             pltpu.SMEM((DOCS,), jnp.int32),
-            pltpu.SemaphoreType.DMA((8 * PAIR,)),
-            pltpu.SemaphoreType.DMA((2,)),
+            pltpu.SemaphoreType.DMA((PAIR + 2,)),
         ],
-        moved=2 * tokens * features + 4 * keys.size,
-    )(*(pltpu.with_memory_space_constraint(x, pltpu.HBM) for x in (document_lengths, pair_ids, queries, keys, values)))
+        moved=2 * tokens * features,
+    )(*arguments[:3])
     near = swap(near, "sp", parts, 1)
+    key_far = swap(key_own, "sp", parts, 2)
+    key_last = swap(key_send, "sp", parts, 3)
     value_far = swap(value_own, "sp", parts, 2)
     value_last = swap(value_send, "sp", parts, 3)
-    key_far = swap(key_own, "sp", parts, 2)
-    key_last = swap(key_send, "sp", parts, 3)
     sums = call(
         scores_kernel,
         struct((PAIR * HEAD_GROUP, parts * tokens), f32),
-        [VMEM] * 6,
+        [VMEM] * 7,
         flops=tokens * features * tokens * parts,
         moved=2 * queries.size + 4 * parts * keys.size,
-    )(bias, query_own, key_own, near, key_far, key_last)
+    )(bias, query_own, query_near, key_own, near, key_far, key_last)
     partial, rounded = call(
         values_kernel, (struct((DOCS, width), f32), struct((DOCS, width), bf16)), [VMEM] * 6
     )(sums, of_doc, value_own, near, value_far, value_last)

time: 30.7 us -> 31 us (level)
  waiting for transfers between devices: 11.6 us -> 10.6 us
  starting transfers between devices: 13 us -> 13.6 us
  Pallas kernels: 5.35 us -> 5.91 us
    pallas_call x0 -> x1, Pallas kernels: none -> 1.04 us  [per_device(): call(cut_kernel, (near_cut, near_cut, struct((tokens, 2 * kv_width), bf16...]
    ppermute x12 -> x13, waiting for transfers between devices: 11.6 us -> 10.6 us  [swap(): return lax.ppermute(block, axis, [(s, s ^ distance) for s in range(size)])]
    ppermute x12 -> x13, starting transfers between devices: 13 us -> 13.6 us  [swap(): return lax.ppermute(block, axis, [(s, s ^ distance) for s in range(size)])]
    pallas_call x1, Pallas kernels: 1.59 us -> 1.08 us  [per_device(): call(functools.partial(plan_kernel, parts), (struct((tokens, width), bf16...]
  transfers between devices with their start and end apart: 12 -> 13, of which waited for: 9 -> 8; matrix products, arithmetic and copies ran while one was open for 0% -> 0% of each run, Pallas kernels for 8% -> 14%
where the time goes in v4:
time: 31 us; the launch traced here: 30.8 us
  starting transfers between devices  13.6 us (44%)
  waiting for transfers between devices  10.6 us (34%)
  Pallas kernels  5.91 us (19%)
  between operations  0.7 us (2%)
    ppermute x13, starting transfers between devices, swap(): return lax.ppermute(block, axis, [(s, s ^ distance) for s in range(size)])  13.6 us
    ppermute x13, waiting for transfers between devices, swap(): return lax.ppermute(block, axis, [(s, s ^ distance) for s in range(size)])  10.6 us
    pallas_call x1, Pallas kernels, per_device(): call(scores_kernel, struct((PAIR * HEAD_GROUP, parts * tokens), f32), [VM...  2.32 us
    pallas_call x1, Pallas kernels, per_device(): call(functools.partial(plan_kernel, parts), (struct((tokens, width), bf16...  1.08 us
    pallas_call x1, Pallas kernels, per_device(): call(cut_kernel, (near_cut, near_cut, struct((tokens, 2 * kv_width), bf16...  1.04 us
    pallas_call x1, Pallas kernels, per_device(): call(grads_kernel, (struct((DOCS, features // parts), bf16), struct((DOCS...  1.02 us
  transfers between devices with their start and end apart: 13, of which 8 were waited for; matrix products, arithmetic and copies ran while one was open for 0% of the time, Pallas kernels for 14%

profile of v4, /device:TPU:0, one launch (start us, length us, event | category | flops | bytes accessed | tf_op | source)
XLA Modules:
  0.0 30.8 jit_solution(13748359568762367339)
XLA Ops:
  0.6 0.5 %collective-permute-start = (bf16[128,3584]{1,0:T(8,128)(2,1)}, bf16[128,3584]{1,0:T(8,128)(2,1)S(1)}, u32[]{:S(2)}, u32[]{:S(2)}) collective-permute-start(bf16[128,3584]{1,0:T(8,128)(2,1)} %q_hbm.1), channel_id=1, source_target_pairs={{0,1},{1,0},{2,3},{3,2},{4,5},{5,4},{6,7},{7,6},{8,9},{9,8},{10,11... | collective-permute-start | bytes 2752520 | tf_op jit(solution)/shard_map/ppermute | solution.py:217
  1.1 1.0 %shard_map.69 = (bf16[128,256]{1,0:T(8,128)(2,1)S(1)}, bf16[128,256]{1,0:T(8,128)(2,1)S(1)}, bf16[128,512]{1,0:T(8,128)(2,1)S(1)}, bf16[128,256]{1,0:T(8,128)(2,1)S(1)}, bf16[128,256]{1,0:T(8,128)(2,1)S(1)}) custom-call(bf16[128,512]{1,0:T(8,128)(2,1)} %k_hbm.1, bf16[128,512]{1,0:T(8,128)(2,1)} %v_hbm.1), custom_call_target="tpu_custom_call" | custom-call | bytes 524288 | tf_op jit(solution)/shard_map/pallas_call | solution.py:243
  2.2 0.1 collective-permute-start.1
  2.3 2.9 %collective-permute-start.2 = (bf16[128,256]{1,0:T(8,128)(2,1)S(1)}, bf16[128,256]{1,0:T(8,128)(2,1)S(1)}, u32[]{:S(2)}, u32[]{:S(2)}) collective-permute-start(bf16[128,256]{1,0:T(8,128)(2,1)S(1)} %get-tuple-element.16.k_own), channel_id=1, source_target_pairs={{0,2},{1,3},{2,0},{3,1},{4,6},{5,7},{6,4},{7,5},{8,10},{9,11},{10,... | collective-permute-start | bytes 196616 | tf_op jit(solution)/shard_map/ppermute | solution.py:217
  5.3 0.0 collective-permute-start.3
  5.3 1.4 %collective-permute-start.4 = (bf16[128,256]{1,0:T(8,128)(2,1)S(1)}, bf16[128,256]{1,0:T(8,128)(2,1)S(1)}, u32[]{:S(2)}, u32[]{:S(2)}) collective-permute-start(bf16[128,256]{1,0:T(8,128)(2,1)S(1)} %get-tuple-element.20.v_own), channel_id=1, source_target_pairs={{0,2},{1,3},{2,0},{3,1},{4,6},{5,7},{6,4},{7,5},{8,10},{9,11},{10,... | collective-permute-start | bytes 196616 | tf_op jit(solution)/shard_map/ppermute | solution.py:217
  6.7 0.9 %collective-permute-done.2.k_far = bf16[128,256]{1,0:T(8,128)(2,1)S(1)} collective-permute-done((bf16[128,256]{1,0:T(8,128)(2,1)S(1)}, bf16[128,256]{1,0:T(8,128)(2,1)S(1)}, u32[]{:S(2)}, u32[]{:S(2)}) %collective-permute-start.2) | collective-permute-done | bytes 65568 | tf_op jit(solution)/shard_map/ppermute | solution.py:217
  7.6 0.5 %collective-permute-start.5 = (bf16[128,256]{1,0:T(8,128)(2,1)S(1)}, bf16[128,256]{1,0:T(8,128)(2,1)S(1)}, u32[]{:S(2)}, u32[]{:S(2)}) collective-permute-start(bf16[128,256]{1,0:T(8,128)(2,1)S(1)} %get-tuple-element.21), channel_id=1, source_target_pairs={{0,3},{1,2},{2,1},{3,0},{4,7},{5,6},{6,5},{7,4},{8,11},{9,10},{10,... | collective-permute-start | bytes 196616 | tf_op jit(solution)/shard_map/ppermute | solution.py:217
  8.1 1.1 %shard_map.68 = (bf16[128,1792]{1,0:T(8,128)(2,1)S(1)}, f32[256,512]{1,0:T(8,128)S(1)}, f32[8,512]{1,0:T(8,128)S(1)}, f32[8,64]{1,0:T(8,128)S(1)}) custom-call(s32[1,8]{1,0:T(1,128)} %lengths_hbm.1, s32[8]{0:T(128)} %pairs_hbm.1, bf16[128,3584]{1,0:T(8,128)(2,1)} %q_hbm.1), custom_call_target="tpu_custom_call" | custom-call | bytes 917504 | tf_op jit(solution)/shard_map/pallas_call | solution.py:250
  9.2 0.5 %collective-permute-done.3.k_last = bf16[128,256]{1,0:T(8,128)(2,1)S(1)} collective-permute-done((bf16[128,256]{1,0:T(8,128)(2,1)S(1)}, bf16[128,256]{1,0:T(8,128)(2,1)S(1)}, u32[]{:S(2)}, u32[]{:S(2)}) %collective-permute-start.3) | collective-permute-done | bytes 65568 | tf_op jit(solution)/shard_map/ppermute | solution.py:217
  9.7 0.0 collective-permute-done.1.near
  9.7 0.0 collective-permute-done.q_near
  9.7 2.3 %shard_map.70.sums_ref = f32[14,512]{1,0:T(8,128)S(1)} custom-call(f32[256,512]{1,0:T(8,128)S(1)} %get-tuple-element.14.bias_ref, bf16[128,1792]{1,0:T(8,128)(2,1)S(1)} %get-tuple-element.15.q_own, bf16[128,3584]{1,0:T(8,128)(2,1)S(1)} %collective-permute-done.q_near, bf16[128,256]{1,0:T(8,128)(2,1)S(1)} %get-tuple-element.16.k_own, ...), custom_call_target="tpu_custom_call" | custom-call | flops 234881024 | bytes 1966080 | tf_op jit(solution)/shard_map/pallas_call | solution.py:271
  12.0 0.0 collective-permute-done.4.v_far
  12.0 0.0 collective-permute-done.5.v_last
  12.0 0.2 shard_map.71
  12.2 2.9 %collective-permute-start.6 = (bf16[8,1792]{1,0:T(8,128)(2,1)S(1)}, bf16[8,1792]{1,0:T(8,128)(2,1)S(1)}, u32[]{:S(2)}, u32[]{:S(2)}) collective-permute-start(bf16[8,1792]{1,0:T(8,128)(2,1)S(1)} %get-tuple-element.22), channel_id=1, source_target_pairs={{0,6},{1,7},{2,4},{3,5},{4,2},{5,3},{6,0},{7,1},{8,14},{9,15},{10,... | collective-permute-start | bytes 86024 | tf_op jit(solution)/shard_map/ppermute | solution.py:217
  15.2 0.1 collective-permute-start.7
  15.3 0.5 %collective-permute-start.8 = (bf16[8,1792]{1,0:T(8,128)(2,1)S(1)}, bf16[8,1792]{1,0:T(8,128)(2,1)S(1)}, u32[]{:S(2)}, u32[]{:S(2)}) collective-permute-start(bf16[8,1792]{1,0:T(8,128)(2,1)S(1)} %get-tuple-element.22), channel_id=1, source_target_pairs={{0,4},{4,0},{8,12},{12,8},{16,20},{20,16},{24,28},{28,24},{1,5},{5... | collective-permute-start | bytes 86024 | tf_op jit(solution)/shard_map/ppermute | solution.py:217
  15.8 1.3 %collective-permute-done.6.corner_ref = bf16[8,1792]{1,0:T(8,128)(2,1)S(1)} collective-permute-done((bf16[8,1792]{1,0:T(8,128)(2,1)S(1)}, bf16[8,1792]{1,0:T(8,128)(2,1)S(1)}, u32[]{:S(2)}, u32[]{:S(2)}) %collective-permute-start.6) | collective-permute-done | bytes 28704 | tf_op jit(solution)/shard_map/ppermute | solution.py:217
  17.1 2.0 %collective-permute-done.7.far_ref.refs_5_ = bf16[8,1792]{1,0:T(8,128)(2,1)S(1)} collective-permute-done((bf16[8,1792]{1,0:T(8,128)(2,1)S(1)}, bf16[8,1792]{1,0:T(8,128)(2,1)S(1)}, u32[]{:S(2)}, u32[]{:S(2)}) %collective-permute-start.7) | collective-permute-done | bytes 28704 | tf_op jit(solution)/shard_map/ppermute | solution.py:217
  19.0 0.1 collective-permute-done.8.next_ref
  19.2 3.7 %collective-permute-start.10 = (bf16[16,1792]{1,0:T(8,128)(2,1)S(1)}, bf16[16,1792]{1,0:T(8,128)(2,1)S(1)}, u32[]{:S(2)}, u32[]{:S(2)}) collective-permute-start(bf16[16,1792]{1,0:T(8,128)(2,1)S(1)} %shard_map.72.refs_3_), channel_id=1, source_target_pairs={{0,24},{4,28},{8,16},{12,20},{16,8},{20,12},{24,0},{28,4},{1,25},{... | collective-permute-start | bytes 172040 | tf_op jit(solution)/shard_map/ppermute | solution.py:217
  22.9 0.0 collective-permute-start.11
  22.9 0.8 %collective-permute-start.9 = (bf16[16,1792]{1,0:T(8,128)(2,1)S(1)}, bf16[16,1792]{1,0:T(8,128)(2,1)S(1)}, u32[]{:S(2)}, u32[]{:S(2)}) collective-permute-start(bf16[16,1792]{1,0:T(8,128)(2,1)S(1)} %shard_map.72.refs_3_), channel_id=1, source_target_pairs={{0,8},{4,12},{8,0},{12,4},{16,24},{20,28},{24,16},{28,20},{1,9},{5... | collective-permute-start | bytes 172040 | tf_op jit(solution)/shard_map/ppermute | solution.py:217
  23.7 1.8 %collective-permute-done.10.refs_1_ = bf16[16,1792]{1,0:T(8,128)(2,1)S(1)} collective-permute-done((bf16[16,1792]{1,0:T(8,128)(2,1)S(1)}, bf16[16,1792]{1,0:T(8,128)(2,1)S(1)}, u32[]{:S(2)}, u32[]{:S(2)}) %collective-permute-start.10) | collective-permute-done | bytes 57376 | tf_op jit(solution)/shard_map/ppermute | solution.py:217
  25.4 2.8 %collective-permute-done.11.refs_2_ = bf16[16,1792]{1,0:T(8,128)(2,1)S(1)} collective-permute-done((bf16[16,1792]{1,0:T(8,128)(2,1)S(1)}, bf16[16,1792]{1,0:T(8,128)(2,1)S(1)}, u32[]{:S(2)}, u32[]{:S(2)}) %collective-permute-start.11) | collective-permute-done | bytes 57376 | tf_op jit(solution)/shard_map/ppermute | solution.py:217
  28.2 0.0 collective-permute-done.9.refs_0_
  28.3 0.2 shard_map.73.gram_one
  28.5 0.1 collective-permute-start.12
  28.5 1.2 %collective-permute-done.12.gram_two = f32[64,64]{1,0:T(8,128)S(1)} collective-permute-done((f32[64,64]{1,0:T(8,128)S(1)}, f32[64,64]{1,0:T(8,128)S(1)}, u32[]{:S(2)}, u32[]{:S(2)}) %collective-permute-start.12) | collective-permute-done | bytes 16416 | tf_op jit(solution)/shard_map/ppermute | solution.py:217
  29.7 1.0 %shard_map.74 = (bf16[8,896]{1,0:T(8,128)(2,1)}, f32[8,896]{1,0:T(8,128)}) custom-call(f32[8,64]{1,0:T(8,128)S(1)} %get-tuple-element.13.partner_ref, f32[64,64]{1,0:T(8,128)S(1)} %shard_map.73.gram_one, f32[64,64]{1,0:T(8,128)S(1)} %collective-permute-done.12.gram_two, bf16[16,1792]{1,0:T(8,128)(2,1)S(1)} %collective-permute-done.9.refs_0_, ...), custom_call_target="tpu_custom_call" | custom-call | tf_op jit(solution)/shard_map/pallas_call | solution.py:287
  (1 shorter events, 0.0 us)
Async XLA Ops:
  0.6 9.0 %collective-permute-start = (bf16[128,3584]{1,0:T(8,128)(2,1)}, bf16[128,3584]{1,0:T(8,128)(2,1)S(1)}, u32[]{:S(2)}, u32[]{:S(2)}) collective-permute-start(bf16[128,3584]{1,0:T(8,128)(2,1)} %q_hbm.1), channel_id=1, source_target_pairs={{0,1},{1,0},{2,3},{3,2},{4,5},{5,4},{6,7},{7,6},{8,9},{9,8},{10,11... | collective-permute-start | bytes 2752520 | tf_op jit(solution)/shard_map/ppermute | solution.py:217
  2.2 7.5 %collective-permute-start.1 = (bf16[128,512]{1,0:T(8,128)(2,1)S(1)}, bf16[128,512]{1,0:T(8,128)(2,1)S(1)}, u32[]{:S(2)}, u32[]{:S(2)}) collective-permute-start(bf16[128,512]{1,0:T(8,128)(2,1)S(1)} %get-tuple-element.17), channel_id=1, source_target_pairs={{0,1},{1,0},{2,3},{3,2},{4,5},{5,4},{6,7},{7,6},{8,9},{9,8},{10,11... | collective-permute-start | bytes 393224 | tf_op jit(solution)/shard_map/ppermute | solution.py:217
  2.3 5.3 %collective-permute-start.2 = (bf16[128,256]{1,0:T(8,128)(2,1)S(1)}, bf16[128,256]{1,0:T(8,128)(2,1)S(1)}, u32[]{:S(2)}, u32[]{:S(2)}) collective-permute-start(bf16[128,256]{1,0:T(8,128)(2,1)S(1)} %get-tuple-element.16.k_own), channel_id=1, source_target_pairs={{0,2},{1,3},{2,0},{3,1},{4,6},{5,7},{6,4},{7,5},{8,10},{9,11},{10,... | collective-permute-start | bytes 196616 | tf_op jit(solution)/shard_map/ppermute | solution.py:217
  5.3 4.4 %collective-permute-start.3 = (bf16[128,256]{1,0:T(8,128)(2,1)S(1)}, bf16[128,256]{1,0:T(8,128)(2,1)S(1)}, u32[]{:S(2)}, u32[]{:S(2)}) collective-permute-start(bf16[128,256]{1,0:T(8,128)(2,1)S(1)} %get-tuple-element.18), channel_id=1, source_target_pairs={{0,3},{1,2},{2,1},{3,0},{4,7},{5,6},{6,5},{7,4},{8,11},{9,10},{10,... | collective-permute-start | bytes 196616 | tf_op jit(solution)/shard_map/ppermute | solution.py:217
  5.3 6.7 %collective-permute-start.4 = (bf16[128,256]{1,0:T(8,128)(2,1)S(1)}, bf16[128,256]{1,0:T(8,128)(2,1)S(1)}, u32[]{:S(2)}, u32[]{:S(2)}) collective-permute-start(bf16[128,256]{1,0:T(8,128)(2,1)S(1)} %get-tuple-element.20.v_own), channel_id=1, source_target_pairs={{0,2},{1,3},{2,0},{3,1},{4,6},{5,7},{6,4},{7,5},{8,10},{9,11},{10,... | collective-permute-start | bytes 196616 | tf_op jit(solution)/shard_map/ppermute | solution.py:217
  7.6 4.4 %collective-permute-start.5 = (bf16[128,256]{1,0:T(8,128)(2,1)S(1)}, bf16[128,256]{1,0:T(8,128)(2,1)S(1)}, u32[]{:S(2)}, u32[]{:S(2)}) collective-permute-start(bf16[128,256]{1,0:T(8,128)(2,1)S(1)} %get-tuple-element.21), channel_id=1, source_target_pairs={{0,3},{1,2},{2,1},{3,0},{4,7},{5,6},{6,5},{7,4},{8,11},{9,10},{10,... | collective-permute-start | bytes 196616 | tf_op jit(solution)/shard_map/ppermute | solution.py:217
  12.2 4.8 %collective-permute-start.6 = (bf16[8,1792]{1,0:T(8,128)(2,1)S(1)}, bf16[8,1792]{1,0:T(8,128)(2,1)S(1)}, u32[]{:S(2)}, u32[]{:S(2)}) collective-permute-start(bf16[8,1792]{1,0:T(8,128)(2,1)S(1)} %get-tuple-element.22), channel_id=1, source_target_pairs={{0,6},{1,7},{2,4},{3,5},{4,2},{5,3},{6,0},{7,1},{8,14},{9,15},{10,... | collective-permute-start | bytes 86024 | tf_op jit(solution)/shard_map/ppermute | solution.py:217
  15.2 3.9 %collective-permute-start.7 = (bf16[8,1792]{1,0:T(8,128)(2,1)S(1)}, bf16[8,1792]{1,0:T(8,128)(2,1)S(1)}, u32[]{:S(2)}, u32[]{:S(2)}) collective-permute-start(bf16[8,1792]{1,0:T(8,128)(2,1)S(1)} %get-tuple-element.22), channel_id=1, source_target_pairs={{0,2},{1,3},{2,0},{3,1},{4,6},{5,7},{6,4},{7,5},{8,10},{9,11},{10,... | collective-permute-start | bytes 86024 | tf_op jit(solution)/shard_map/ppermute | solution.py:217
  15.3 3.9 %collective-permute-start.8 = (bf16[8,1792]{1,0:T(8,128)(2,1)S(1)}, bf16[8,1792]{1,0:T(8,128)(2,1)S(1)}, u32[]{:S(2)}, u32[]{:S(2)}) collective-permute-start(bf16[8,1792]{1,0:T(8,128)(2,1)S(1)} %get-tuple-element.22), channel_id=1, source_target_pairs={{0,4},{4,0},{8,12},{12,8},{16,20},{20,16},{24,28},{28,24},{1,5},{5... | collective-permute-start | bytes 86024 | tf_op jit(solution)/shard_map/ppermute | solution.py:217
  19.2 6.2 %collective-permute-start.10 = (bf16[16,1792]{1,0:T(8,128)(2,1)S(1)}, bf16[16,1792]{1,0:T(8,128)(2,1)S(1)}, u32[]{:S(2)}, u32[]{:S(2)}) collective-permute-start(bf16[16,1792]{1,0:T(8,128)(2,1)S(1)} %shard_map.72.refs_3_), channel_id=1, source_target_pairs={{0,24},{4,28},{8,16},{12,20},{16,8},{20,12},{24,0},{28,4},{1,25},{... | collective-permute-start | bytes 172040 | tf_op jit(solution)/shard_map/ppermute | solution.py:217
  22.9 5.4 %collective-permute-start.11 = (bf16[16,1792]{1,0:T(8,128)(2,1)S(1)}, bf16[16,1792]{1,0:T(8,128)(2,1)S(1)}, u32[]{:S(2)}, u32[]{:S(2)}) collective-permute-start(bf16[16,1792]{1,0:T(8,128)(2,1)S(1)} %shard_map.72.refs_3_), channel_id=1, source_target_pairs={{0,16},{4,20},{8,24},{12,28},{16,0},{20,4},{24,8},{28,12},{1,17},{... | collective-permute-start | bytes 172040 | tf_op jit(solution)/shard_map/ppermute | solution.py:217
  22.9 5.4 %collective-permute-start.9 = (bf16[16,1792]{1,0:T(8,128)(2,1)S(1)}, bf16[16,1792]{1,0:T(8,128)(2,1)S(1)}, u32[]{:S(2)}, u32[]{:S(2)}) collective-permute-start(bf16[16,1792]{1,0:T(8,128)(2,1)S(1)} %shard_map.72.refs_3_), channel_id=1, source_target_pairs={{0,8},{4,12},{8,0},{12,4},{16,24},{20,28},{24,16},{28,20},{1,9},{5... | collective-permute-start | bytes 172040 | tf_op jit(solution)/shard_map/ppermute | solution.py:217
  28.5 1.3 %collective-permute-start.12 = (f32[64,64]{1,0:T(8,128)S(1)}, f32[64,64]{1,0:T(8,128)S(1)}, u32[]{:S(2)}, u32[]{:S(2)}) collective-permute-start(f32[64,64]{1,0:T(8,128)S(1)} %shard_map.73.gram_one), channel_id=1, source_target_pairs={{0,1},{1,0},{2,3},{3,2},{4,5},{5,4},{6,7},{7,6},{8,9},{9,8},{10,11... | collective-permute-start | bytes 49160 | tf_op jit(solution)/shard_map/ppermute | solution.py:217

commit v5 on v4

--- a/solution.py
+++ b/solution.py
@@ -57,7 +57,7 @@
         copy.wait()
 
 
-def plan_kernel(parts, lengths_hbm, pairs_hbm, q_hbm, q_out, bias_ref, doc_ref, partner_ref, lengths_ref, pairs_ref, sem):
+def plan_kernel(parts, lengths_hbm, pairs_hbm, q_hbm, q_out, bias_ref, doc_ref, partner_ref, far_ref, lengths_ref, pairs_ref, sem):
     span = q_hbm.shape[0]
     me = lax.axis_index("sp")
     core = lax.rem(me, PAIR)
@@ -90,6 +90,17 @@
         for t in range(PAIR):
             bias_ref[t * span : (t + 1) * span, columns] = jnp.where(row_segments[t] == key_segment, 0.0, -1e30)
         doc_ref[:, columns] = jnp.where(key_segment == doc, weight, 0.0)
+    firsts = [segments(lengths_ref, (me ^ r) * span) for r in range(parts)]
+    lasts = [segments(lengths_ref, (me ^ r) * span + span - 1) for r in range(parts)]
+    needs = []
+    for t in range(PAIR):
+        shared = [
+            (jnp.maximum(firsts[t], firsts[r]) <= jnp.minimum(lasts[t], lasts[r])).astype(jnp.int32)
+            for r in range(PAIR, parts)
+        ]
+        needs.append((shared[0] + 2 * shared[1]).astype(jnp.float32))
+    flag_row = lax.broadcasted_iota(jnp.int32, far_ref.shape, 0)
+    far_ref[...] = jnp.where(flag_row == 0, needs[0], needs[1])
     own = lax.axis_index("dp")
     own_row = lax.broadcasted_iota(jnp.int32, partner_ref.shape, 0)
     own_column = lax.broadcasted_iota(jnp.int32, partner_ref.shape, 1)
@@ -102,29 +113,42 @@
         copy.wait()
 
 
-def scores_kernel(bias_ref, q_own, q_near, k_own, near, k_far, k_last, sums_ref):
+def scores_kernel(far_ref, bias_ref, q_own, q_near, k_own, near, k_far, k_last, sums_ref):
     core = lax.rem(lax.axis_index("sp"), PAIR)
     scale = HEAD_SIZE ** (-0.5) * math.log2(math.e)
-    for p in range(PAIR):
-        here = slice(p * HEAD_SIZE, (p + 1) * HEAD_SIZE)
-        key_head = jnp.concatenate([k[:, here] for k in (k_own, near, k_far, k_last)], axis=0)
-        for h in range(HEAD_GROUP):
-            place = (p * HEAD_GROUP + h) * HEAD_SIZE
-            beside = pl.multiple_of((PAIR * p + core) * GROUP_WIDTH + h * HEAD_SIZE, HEAD_SIZE)
-            total = None
-            for t, query in enumerate((q_own[:, place : place + HEAD_SIZE], q_near[:, pl.ds(beside, HEAD_SIZE)])):
-                rows = query.shape[0]
+    blocks = (k_own, near, k_far, k_last)
+    span = k_own.shape[0]
+
+    def attend(t, used):
+        rows = slice(t * span, (t + 1) * span)
+        bias = jnp.concatenate([bias_ref[rows, r * span : (r + 1) * span] for r in used], axis=1)
+        for p in range(PAIR):
+            here = slice(p * HEAD_SIZE, (p + 1) * HEAD_SIZE)
+            key_head = jnp.concatenate([blocks[r][:, here] for r in used], axis=0)
+            for h in range(HEAD_GROUP):
+                row = p * HEAD_GROUP + h
+                if t == 0:
+                    query = q_own[:, row * HEAD_SIZE : (row + 1) * HEAD_SIZE]
+                else:
+                    first = (PAIR * p + core) * GROUP_WIDTH + h * HEAD_SIZE
+                    query = q_near[:, pl.ds(pl.multiple_of(first, HEAD_SIZE), HEAD_SIZE)]
                 scores = lax.dot_general(
                     query, key_head, (((1,), (1,)), ((), ())), preferred_element_type=jnp.float32
                 )
-                scores = scores + bias_ref[t * rows : (t + 1) * rows]
+                scores = scores + bias
                 largest = jnp.max(scores, axis=1, keepdims=True)
                 weights = jnp.exp2((scores - largest) * scale)
                 probs = weights * (1.0 / jnp.sum(weights, axis=1, keepdims=True))
                 summed = jnp.sum(probs, axis=0, keepdims=True)
-                total = summed if total is None else total + summed
-            row = p * HEAD_GROUP + h
-            sums_ref[row : row + 1] = total
+                for i, r in enumerate(used):
+                    place = (slice(row, row + 1), slice(r * span, (r + 1) * span))
+                    sums_ref[place] = sums_ref[place] + summed[:, i * span : (i + 1) * span]
+
+    sums_ref[...] = jnp.zeros_like(sums_ref)
+    for t in range(PAIR):
+        need = jnp.max(far_ref[t : t + 1])
+        for code, used in enumerate(((0, 1), (0, 1, 2), (0, 1, 3), (0, 1, 2, 3))):
+            pl.when(need == code)(functools.partial(attend, t, used))
 
 
 def values_kernel(sums_ref, doc_ref, v_own, near, v_far, v_last, out_ref, sent_ref):
@@ -247,13 +271,14 @@
         [pltpu.SemaphoreType.DMA((6 * PAIR,))],
         moved=8 * keys.size,
     )(*arguments[3:])
-    query_own, bias, of_doc, partner = call(
+    query_own, bias, of_doc, partner, far_needs = call(
         functools.partial(plan_kernel, parts),
         (
             struct((tokens, width), bf16),
             struct((PAIR * tokens, parts * tokens), f32),
             struct((DOCS, parts * tokens), f32),
             struct((DOCS, docs), f32),
+            struct((8, 128), f32),
         ),
         [HBM] * 3,
         [
@@ -266,15 +291,16 @@
     near = swap(near, "sp", parts, 1)
     key_far = swap(key_own, "sp", parts, 2)
     key_last = swap(key_send, "sp", parts, 3)
-    value_far = swap(value_own, "sp", parts, 2)
+    value_send, value_to_far, near = lax.optimization_barrier((value_send, value_own, near))
+    value_far = swap(value_to_far, "sp", parts, 2)
     value_last = swap(value_send, "sp", parts, 3)
     sums = call(
         scores_kernel,
         struct((PAIR * HEAD_GROUP, parts * tokens), f32),
-        [VMEM] * 7,
+        [VMEM] * 8,
         flops=tokens * features * tokens * parts,
         moved=2 * queries.size + 4 * parts * keys.size,
-    )(bias, query_own, query_near, key_own, near, key_far, key_last)
+    )(far_needs, bias, query_own, query_near, key_own, near, key_far, key_last)
     partial, rounded = call(
         values_kernel, (struct((DOCS, width), f32), struct((DOCS, width), bf16)), [VMEM] * 6
     )(sums, of_doc, value_own, near, value_far, value_last)

time: 31 us -> 31.2 us (level)
  transfers between devices with their start and end apart: 13 -> 13, of which waited for: 8 -> 8; matrix products, arithmetic and copies ran while one was open for 0% -> 0% of each run, Pallas kernels for 14% -> 15%
where the time goes in v5:
time: 31.2 us; the launch traced here: 30.9 us
  starting transfers between devices  13.4 us (43%)
  waiting for transfers between devices  10.8 us (35%)
  Pallas kernels  5.97 us (19%)
  between operations  0.7 us (2%)
    ppermute x13, starting transfers between devices, swap(): return lax.ppermute(block, axis, [(s, s ^ distance) for s in range(size)])  13.4 us
    ppermute x13, waiting for transfers between devices, swap(): return lax.ppermute(block, axis, [(s, s ^ distance) for s in range(size)])  10.8 us
    pallas_call x1, Pallas kernels, per_device(): call(scores_kernel, struct((PAIR * HEAD_GROUP, parts * tokens), f32), [VM...  2.38 us
    pallas_call x1, Pallas kernels, per_device(): call(functools.partial(plan_kernel, parts), (struct((tokens, width), bf16...  1.08 us
    pallas_call x1, Pallas kernels, per_device(): call(cut_kernel, (near_cut, near_cut, struct((tokens, 2 * kv_width), bf16...  1.04 us
    pallas_call x1, Pallas kernels, per_device(): call(grads_kernel, (struct((DOCS, features // parts), bf16), struct((DOCS...  1.02 us
  transfers between devices with their start and end apart: 13, of which 8 were waited for; matrix products, arithmetic and copies ran while one was open for 0% of the time, Pallas kernels for 15%

profile of v5, /device:TPU:0, one launch (start us, length us, event | category | flops | bytes accessed | tf_op | source)
XLA Modules:
  0.0 30.9 jit_solution(5536521997975113144)
XLA Ops:
  0.6 0.5 %collective-permute-start = (bf16[128,3584]{1,0:T(8,128)(2,1)}, bf16[128,3584]{1,0:T(8,128)(2,1)S(1)}, u32[]{:S(2)}, u32[]{:S(2)}) collective-permute-start(bf16[128,3584]{1,0:T(8,128)(2,1)} %q_hbm.1), channel_id=1, source_target_pairs={{0,1},{1,0},{2,3},{3,2},{4,5},{5,4},{6,7},{7,6},{8,9},{9,8},{10,11... | collective-permute-start | bytes 2752520 | tf_op jit(solution)/shard_map/ppermute | solution.py:241
  1.1 1.0 %shard_map.69 = (bf16[128,256]{1,0:T(8,128)(2,1)S(1)}, bf16[128,256]{1,0:T(8,128)(2,1)S(1)}, bf16[128,512]{1,0:T(8,128)(2,1)S(1)}, bf16[128,256]{1,0:T(8,128)(2,1)S(1)}, bf16[128,256]{1,0:T(8,128)(2,1)S(1)}) custom-call(bf16[128,512]{1,0:T(8,128)(2,1)} %k_hbm.1, bf16[128,512]{1,0:T(8,128)(2,1)} %v_hbm.1), custom_call_target="tpu_custom_call" | custom-call | bytes 524288 | tf_op jit(solution)/shard_map/pallas_call | solution.py:267
  2.2 0.1 collective-permute-start.1
  2.3 2.9 %collective-permute-start.2 = (bf16[128,256]{1,0:T(8,128)(2,1)S(1)}, bf16[128,256]{1,0:T(8,128)(2,1)S(1)}, u32[]{:S(2)}, u32[]{:S(2)}) collective-permute-start(bf16[128,256]{1,0:T(8,128)(2,1)S(1)} %get-tuple-element.21.k_own), channel_id=1, source_target_pairs={{0,2},{1,3},{2,0},{3,1},{4,6},{5,7},{6,4},{7,5},{8,10},{9,11},{10,... | collective-permute-start | bytes 196616 | tf_op jit(solution)/shard_map/ppermute | solution.py:241
  5.3 0.0 collective-permute-start.3
  5.3 0.0 collective-permute-done.1.near
  5.3 1.4 %collective-permute-start.4 = (bf16[128,256]{1,0:T(8,128)(2,1)S(1)}, bf16[128,256]{1,0:T(8,128)(2,1)S(1)}, u32[]{:S(2)}, u32[]{:S(2)}) collective-permute-start(bf16[128,256]{1,0:T(8,128)(2,1)S(1)} %get-tuple-element.28.v_own), channel_id=1, source_target_pairs={{0,2},{1,3},{2,0},{3,1},{4,6},{5,7},{6,4},{7,5},{8,10},{9,11},{10,... | collective-permute-start | bytes 196616 | tf_op jit(solution)/shard_map/ppermute | solution.py:241
  6.7 0.3 %collective-permute-start.5 = (bf16[128,256]{1,0:T(8,128)(2,1)S(1)}, bf16[128,256]{1,0:T(8,128)(2,1)S(1)}, u32[]{:S(2)}, u32[]{:S(2)}) collective-permute-start(bf16[128,256]{1,0:T(8,128)(2,1)S(1)} %get-tuple-element.29), channel_id=1, source_target_pairs={{0,3},{1,2},{2,1},{3,0},{4,7},{5,6},{6,5},{7,4},{8,11},{9,10},{10,... | collective-permute-start | bytes 196616 | tf_op jit(solution)/shard_map/ppermute | solution.py:241
  7.0 1.1 %shard_map.68 = (bf16[128,1792]{1,0:T(8,128)(2,1)S(1)}, f32[256,512]{1,0:T(8,128)S(1)}, f32[8,512]{1,0:T(8,128)S(1)}, f32[8,64]{1,0:T(8,128)S(1)}, f32[8,128]{1,0:T(8,128)S(1)}) custom-call(s32[1,8]{1,0:T(1,128)} %lengths_hbm.1, s32[8]{0:T(128)} %pairs_hbm.1, bf16[128,3584]{1,0:T(8,128)(2,1)} %q_hbm.1), custom_call_target="tpu_custom_call" | custom-call | bytes 917504 | tf_op jit(solution)/shard_map/pallas_call | solution.py:274
  8.1 0.0 collective-permute-done.2.k_far
  8.1 1.5 %collective-permute-done.3.k_last = bf16[128,256]{1,0:T(8,128)(2,1)S(1)} collective-permute-done((bf16[128,256]{1,0:T(8,128)(2,1)S(1)}, bf16[128,256]{1,0:T(8,128)(2,1)S(1)}, u32[]{:S(2)}, u32[]{:S(2)}) %collective-permute-start.3) | collective-permute-done | bytes 65568 | tf_op jit(solution)/shard_map/ppermute | solution.py:241
  9.7 0.0 collective-permute-done.q_near
  9.7 2.4 %shard_map.70.sums_ref = f32[14,512]{1,0:T(8,128)S(1)} custom-call(f32[8,128]{1,0:T(8,128)S(1)} %get-tuple-element.18.far_ref, f32[256,512]{1,0:T(8,128)S(1)} %get-tuple-element.19.bias_ref, bf16[128,1792]{1,0:T(8,128)(2,1)S(1)} %get-tuple-element.20.q_own, bf16[128,3584]{1,0:T(8,128)(2,1)S(1)} %collective-permute-done.q_near, ...), custom_call_target="tpu_custom_call" | custom-call | flops 234881024 | bytes 1966080 | tf_op jit(solution)/shard_map/pallas_call | solution.py:297
  12.0 0.0 collective-permute-done.4.v_far
  12.1 0.4 %collective-permute-done.5.v_last = bf16[128,256]{1,0:T(8,128)(2,1)S(1)} collective-permute-done((bf16[128,256]{1,0:T(8,128)(2,1)S(1)}, bf16[128,256]{1,0:T(8,128)(2,1)S(1)}, u32[]{:S(2)}, u32[]{:S(2)}) %collective-permute-start.5) | collective-permute-done | bytes 65568 | tf_op jit(solution)/shard_map/ppermute | solution.py:241
  12.4 0.2 shard_map.71
  12.7 1.6 %collective-permute-start.6 = (bf16[8,1792]{1,0:T(8,128)(2,1)S(1)}, bf16[8,1792]{1,0:T(8,128)(2,1)S(1)}, u32[]{:S(2)}, u32[]{:S(2)}) collective-permute-start(bf16[8,1792]{1,0:T(8,128)(2,1)S(1)} %get-tuple-element.30), channel_id=1, source_target_pairs={{0,6},{1,7},{2,4},{3,5},{4,2},{5,3},{6,0},{7,1},{8,14},{9,15},{10,... | collective-permute-start | bytes 86024 | tf_op jit(solution)/shard_map/ppermute | solution.py:241
  14.3 1.5 %collective-permute-start.7 = (bf16[8,1792]{1,0:T(8,128)(2,1)S(1)}, bf16[8,1792]{1,0:T(8,128)(2,1)S(1)}, u32[]{:S(2)}, u32[]{:S(2)}) collective-permute-start(bf16[8,1792]{1,0:T(8,128)(2,1)S(1)} %get-tuple-element.30), channel_id=1, source_target_pairs={{0,2},{1,3},{2,0},{3,1},{4,6},{5,7},{6,4},{7,5},{8,10},{9,11},{10,... | collective-permute-start | bytes 86024 | tf_op jit(solution)/shard_map/ppermute | solution.py:241
  15.7 0.5 %collective-permute-start.8 = (bf16[8,1792]{1,0:T(8,128)(2,1)S(1)}, bf16[8,1792]{1,0:T(8,128)(2,1)S(1)}, u32[]{:S(2)}, u32[]{:S(2)}) collective-permute-start(bf16[8,1792]{1,0:T(8,128)(2,1)S(1)} %get-tuple-element.30), channel_id=1, source_target_pairs={{0,4},{4,0},{8,12},{12,8},{16,20},{20,16},{24,28},{28,24},{1,5},{5... | collective-permute-start | bytes 86024 | tf_op jit(solution)/shard_map/ppermute | solution.py:241
  16.2 1.3 %collective-permute-done.6.corner_ref = bf16[8,1792]{1,0:T(8,128)(2,1)S(1)} collective-permute-done((bf16[8,1792]{1,0:T(8,128)(2,1)S(1)}, bf16[8,1792]{1,0:T(8,128)(2,1)S(1)}, u32[]{:S(2)}, u32[]{:S(2)}) %collective-permute-start.6) | collective-permute-done | bytes 28704 | tf_op jit(solution)/shard_map/ppermute | solution.py:241
  17.5 0.6 %collective-permute-done.7.far_ref.refs_5_ = bf16[8,1792]{1,0:T(8,128)(2,1)S(1)} collective-permute-done((bf16[8,1792]{1,0:T(8,128)(2,1)S(1)}, bf16[8,1792]{1,0:T(8,128)(2,1)S(1)}, u32[]{:S(2)}, u32[]{:S(2)}) %collective-permute-start.7) | collective-permute-done | bytes 28704 | tf_op jit(solution)/shard_map/ppermute | solution.py:241
  18.1 1.5 %collective-permute-done.8.next_ref = bf16[8,1792]{1,0:T(8,128)(2,1)S(1)} collective-permute-done((bf16[8,1792]{1,0:T(8,128)(2,1)S(1)}, bf16[8,1792]{1,0:T(8,128)(2,1)S(1)}, u32[]{:S(2)}, u32[]{:S(2)}) %collective-permute-start.8) | collective-permute-done | bytes 28704 | tf_op jit(solution)/shard_map/ppermute | solution.py:241
  19.6 3.7 %collective-permute-start.10 = (bf16[16,1792]{1,0:T(8,128)(2,1)S(1)}, bf16[16,1792]{1,0:T(8,128)(2,1)S(1)}, u32[]{:S(2)}, u32[]{:S(2)}) collective-permute-start(bf16[16,1792]{1,0:T(8,128)(2,1)S(1)} %shard_map.72.refs_3_), channel_id=1, source_target_pairs={{0,24},{4,28},{8,16},{12,20},{16,8},{20,12},{24,0},{28,4},{1,25},{... | collective-permute-start | bytes 172040 | tf_op jit(solution)/shard_map/ppermute | solution.py:241
  23.3 0.0 collective-permute-start.11
  23.3 0.8 %collective-permute-start.9 = (bf16[16,1792]{1,0:T(8,128)(2,1)S(1)}, bf16[16,1792]{1,0:T(8,128)(2,1)S(1)}, u32[]{:S(2)}, u32[]{:S(2)}) collective-permute-start(bf16[16,1792]{1,0:T(8,128)(2,1)S(1)} %shard_map.72.refs_3_), channel_id=1, source_target_pairs={{0,8},{4,12},{8,0},{12,4},{16,24},{20,28},{24,16},{28,20},{1,9},{5... | collective-permute-start | bytes 172040 | tf_op jit(solution)/shard_map/ppermute | solution.py:241
  24.1 1.7 %collective-permute-done.10.refs_1_ = bf16[16,1792]{1,0:T(8,128)(2,1)S(1)} collective-permute-done((bf16[16,1792]{1,0:T(8,128)(2,1)S(1)}, bf16[16,1792]{1,0:T(8,128)(2,1)S(1)}, u32[]{:S(2)}, u32[]{:S(2)}) %collective-permute-start.10) | collective-permute-done | bytes 57376 | tf_op jit(solution)/shard_map/ppermute | solution.py:241
  25.7 2.7 %collective-permute-done.11.refs_2_ = bf16[16,1792]{1,0:T(8,128)(2,1)S(1)} collective-permute-done((bf16[16,1792]{1,0:T(8,128)(2,1)S(1)}, bf16[16,1792]{1,0:T(8,128)(2,1)S(1)}, u32[]{:S(2)}, u32[]{:S(2)}) %collective-permute-start.11) | collective-permute-done | bytes 57376 | tf_op jit(solution)/shard_map/ppermute | solution.py:241
  28.4 0.0 collective-permute-done.9.refs_0_
  28.4 0.2 shard_map.73.gram_one
  28.7 0.1 collective-permute-start.12
  28.7 1.2 %collective-permute-done.12.gram_two = f32[64,64]{1,0:T(8,128)S(1)} collective-permute-done((f32[64,64]{1,0:T(8,128)S(1)}, f32[64,64]{1,0:T(8,128)S(1)}, u32[]{:S(2)}, u32[]{:S(2)}) %collective-permute-start.12) | collective-permute-done | bytes 16416 | tf_op jit(solution)/shard_map/ppermute | solution.py:241
  29.9 1.0 %shard_map.74 = (bf16[8,896]{1,0:T(8,128)(2,1)}, f32[8,896]{1,0:T(8,128)}) custom-call(f32[8,64]{1,0:T(8,128)S(1)} %get-tuple-element.17.partner_ref, f32[64,64]{1,0:T(8,128)S(1)} %shard_map.73.gram_one, f32[64,64]{1,0:T(8,128)S(1)} %collective-permute-done.12.gram_two, bf16[16,1792]{1,0:T(8,128)(2,1)S(1)} %collective-permute-done.9.refs_0_, ...), custom_call_target="tpu_custom_call" | custom-call | tf_op jit(solution)/shard_map/pallas_call | solution.py:313
  (1 shorter events, 0.0 us)
Async XLA Ops:
  0.6 9.0 %collective-permute-start = (bf16[128,3584]{1,0:T(8,128)(2,1)}, bf16[128,3584]{1,0:T(8,128)(2,1)S(1)}, u32[]{:S(2)}, u32[]{:S(2)}) collective-permute-start(bf16[128,3584]{1,0:T(8,128)(2,1)} %q_hbm.1), channel_id=1, source_target_pairs={{0,1},{1,0},{2,3},{3,2},{4,5},{5,4},{6,7},{7,6},{8,9},{9,8},{10,11... | collective-permute-start | bytes 2752520 | tf_op jit(solution)/shard_map/ppermute | solution.py:241
  2.2 3.1 %collective-permute-start.1 = (bf16[128,512]{1,0:T(8,128)(2,1)S(1)}, bf16[128,512]{1,0:T(8,128)(2,1)S(1)}, u32[]{:S(2)}, u32[]{:S(2)}) collective-permute-start(bf16[128,512]{1,0:T(8,128)(2,1)S(1)} %get-tuple-element.24), channel_id=1, source_target_pairs={{0,1},{1,0},{2,3},{3,2},{4,5},{5,4},{6,7},{7,6},{8,9},{9,8},{10,11... | collective-permute-start | bytes 393224 | tf_op jit(solution)/shard_map/ppermute | solution.py:241
  2.3 5.8 %collective-permute-start.2 = (bf16[128,256]{1,0:T(8,128)(2,1)S(1)}, bf16[128,256]{1,0:T(8,128)(2,1)S(1)}, u32[]{:S(2)}, u32[]{:S(2)}) collective-permute-start(bf16[128,256]{1,0:T(8,128)(2,1)S(1)} %get-tuple-element.21.k_own), channel_id=1, source_target_pairs={{0,2},{1,3},{2,0},{3,1},{4,6},{5,7},{6,4},{7,5},{8,10},{9,11},{10,... | collective-permute-start | bytes 196616 | tf_op jit(solution)/shard_map/ppermute | solution.py:241
  5.3 4.4 %collective-permute-start.3 = (bf16[128,256]{1,0:T(8,128)(2,1)S(1)}, bf16[128,256]{1,0:T(8,128)(2,1)S(1)}, u32[]{:S(2)}, u32[]{:S(2)}) collective-permute-start(bf16[128,256]{1,0:T(8,128)(2,1)S(1)} %get-tuple-element.26), channel_id=1, source_target_pairs={{0,3},{1,2},{2,1},{3,0},{4,7},{5,6},{6,5},{7,4},{8,11},{9,10},{10,... | collective-permute-start | bytes 196616 | tf_op jit(solution)/shard_map/ppermute | solution.py:241
  5.3 6.8 %collective-permute-start.4 = (bf16[128,256]{1,0:T(8,128)(2,1)S(1)}, bf16[128,256]{1,0:T(8,128)(2,1)S(1)}, u32[]{:S(2)}, u32[]{:S(2)}) collective-permute-start(bf16[128,256]{1,0:T(8,128)(2,1)S(1)} %get-tuple-element.28.v_own), channel_id=1, source_target_pairs={{0,2},{1,3},{2,0},{3,1},{4,6},{5,7},{6,4},{7,5},{8,10},{9,11},{10,... | collective-permute-start | bytes 196616 | tf_op jit(solution)/shard_map/ppermute | solution.py:241
  6.7 5.7 %collective-permute-start.5 = (bf16[128,256]{1,0:T(8,128)(2,1)S(1)}, bf16[128,256]{1,0:T(8,128)(2,1)S(1)}, u32[]{:S(2)}, u32[]{:S(2)}) collective-permute-start(bf16[128,256]{1,0:T(8,128)(2,1)S(1)} %get-tuple-element.29), channel_id=1, source_target_pairs={{0,3},{1,2},{2,1},{3,0},{4,7},{5,6},{6,5},{7,4},{8,11},{9,10},{10,... | collective-permute-start | bytes 196616 | tf_op jit(solution)/shard_map/ppermute | solution.py:241
  12.7 4.8 %collective-permute-start.6 = (bf16[8,1792]{1,0:T(8,128)(2,1)S(1)}, bf16[8,1792]{1,0:T(8,128)(2,1)S(1)}, u32[]{:S(2)}, u32[]{:S(2)}) collective-permute-start(bf16[8,1792]{1,0:T(8,128)(2,1)S(1)} %get-tuple-element.30), channel_id=1, source_target_pairs={{0,6},{1,7},{2,4},{3,5},{4,2},{5,3},{6,0},{7,1},{8,14},{9,15},{10,... | collective-permute-start | bytes 86024 | tf_op jit(solution)/shard_map/ppermute | solution.py:241
  14.3 3.9 %collective-permute-start.7 = (bf16[8,1792]{1,0:T(8,128)(2,1)S(1)}, bf16[8,1792]{1,0:T(8,128)(2,1)S(1)}, u32[]{:S(2)}, u32[]{:S(2)}) collective-permute-start(bf16[8,1792]{1,0:T(8,128)(2,1)S(1)} %get-tuple-element.30), channel_id=1, source_target_pairs={{0,2},{1,3},{2,0},{3,1},{4,6},{5,7},{6,4},{7,5},{8,10},{9,11},{10,... | collective-permute-start | bytes 86024 | tf_op jit(solution)/shard_map/ppermute | solution.py:241
  15.7 3.9 %collective-permute-start.8 = (bf16[8,1792]{1,0:T(8,128)(2,1)S(1)}, bf16[8,1792]{1,0:T(8,128)(2,1)S(1)}, u32[]{:S(2)}, u32[]{:S(2)}) collective-permute-start(bf16[8,1792]{1,0:T(8,128)(2,1)S(1)} %get-tuple-element.30), channel_id=1, source_target_pairs={{0,4},{4,0},{8,12},{12,8},{16,20},{20,16},{24,28},{28,24},{1,5},{5... | collective-permute-start | bytes 86024 | tf_op jit(solution)/shard_map/ppermute | solution.py:241
  19.6 6.1 %collective-permute-start.10 = (bf16[16,1792]{1,0:T(8,128)(2,1)S(1)}, bf16[16,1792]{1,0:T(8,128)(2,1)S(1)}, u32[]{:S(2)}, u32[]{:S(2)}) collective-permute-start(bf16[16,1792]{1,0:T(8,128)(2,1)S(1)} %shard_map.72.refs_3_), channel_id=1, source_target_pairs={{0,24},{4,28},{8,16},{12,20},{16,8},{20,12},{24,0},{28,4},{1,25},{... | collective-permute-start | bytes 172040 | tf_op jit(solution)/shard_map/ppermute | solution.py:241
  23.3 5.2 %collective-permute-start.11 = (bf16[16,1792]{1,0:T(8,128)(2,1)S(1)}, bf16[16,1792]{1,0:T(8,128)(2,1)S(1)}, u32[]{:S(2)}, u32[]{:S(2)}) collective-permute-start(bf16[16,1792]{1,0:T(8,128)(2,1)S(1)} %shard_map.72.refs_3_), channel_id=1, source_target_pairs={{0,16},{4,20},{8,24},{12,28},{16,0},{20,4},{24,8},{28,12},{1,17},{... | collective-permute-start | bytes 172040 | tf_op jit(solution)/shard_map/ppermute | solution.py:241
  23.3 5.2 %collective-permute-start.9 = (bf16[16,1792]{1,0:T(8,128)(2,1)S(1)}, bf16[16,1792]{1,0:T(8,128)(2,1)S(1)}, u32[]{:S(2)}, u32[]{:S(2)}) collective-permute-start(bf16[16,1792]{1,0:T(8,128)(2,1)S(1)} %shard_map.72.refs_3_), channel_id=1, source_target_pairs={{0,8},{4,12},{8,0},{12,4},{16,24},{20,28},{24,16},{28,20},{1,9},{5... | collective-permute-start | bytes 172040 | tf_op jit(solution)/shard_map/ppermute | solution.py:241
  28.7 1.3 %collective-permute-start.12 = (f32[64,64]{1,0:T(8,128)S(1)}, f32[64,64]{1,0:T(8,128)S(1)}, u32[]{:S(2)}, u32[]{:S(2)}) collective-permute-start(f32[64,64]{1,0:T(8,128)S(1)} %shard_map.73.gram_one), channel_id=1, source_target_pairs={{0,1},{1,0},{2,3},{3,2},{4,5},{5,4},{6,7},{7,6},{8,9},{9,8},{10,11... | collective-permute-start | bytes 49160 | tf_op jit(solution)/shard_map/ppermute | solution.py:241

commit v6 on v3

--- a/solution.py
+++ b/solution.py
@@ -85,10 +85,13 @@
     own = lax.axis_index("dp")
     own_row = lax.broadcasted_iota(jnp.int32, partner_ref.shape, 0)
     own_column = lax.broadcasted_iota(jnp.int32, partner_ref.shape, 1)
+    half = partner_ref.shape[1] // (PAIR * DOCS)
     place = jnp.zeros(partner_ref.shape, jnp.int32)
     for d in range(DOCS):
         pair = pairs_ref[d]
-        place = jnp.where(own_row == d, ((pair // DOCS) ^ own) * DOCS + lax.rem(pair, DOCS), place)
+        far = (pair // DOCS) ^ own
+        block = PAIR * lax.rem(far, half) + far // half
+        place = jnp.where(own_row == d, block * DOCS + lax.rem(pair, DOCS), place)
     partner_ref[...] = jnp.where(own_column == place, 2.0, 0.0)
     for copy in copies:
         copy.wait()
@@ -140,7 +143,7 @@
     sent_ref[...] = out_ref[...].astype(jnp.bfloat16)
 
 
-def pool_kernel(corner_ref, far_ref, next_ref, own_ref, sent_ref):
+def pool_kernel(corner_ref, next_ref, far_ref, own_ref, sent_ref):
     pooled = own_ref[...] + far_ref[...].astype(jnp.float32)
     beside = next_ref[...].astype(jnp.float32) + corner_ref[...].astype(jnp.float32)
     sent_ref[...] = jnp.concatenate([pooled, beside], axis=0).astype(jnp.bfloat16)
@@ -212,12 +215,12 @@
 
 
 def gather_pairs(block, axis, size):
-    have, blocks = PAIR, [block]
-    while have < size:
-        if have > PAIR:
+    have, blocks = 1, [block]
+    while PAIR * have < size:
+        if have > 1:
             shape = (len(blocks) * block.shape[0], block.shape[1])
             block = call(join_kernel, jax.ShapeDtypeStruct(shape, block.dtype), [VMEM] * len(blocks))(*blocks)
-        radix = min(4, size // have)
+        radix = min(4, size // (PAIR * have))
         blocks = [swap(block, axis, size, r * have) for r in (*range(radix - 2, 0, -1), radix - 1)] + [block]
         have *= radix
     return blocks
@@ -268,10 +271,10 @@
     partial, rounded = call(
         values_kernel, (struct((DOCS, width), f32), struct((DOCS, width), bf16)), [VMEM] * 6
     )(sums, of_doc, value_own, near, value_far, value_last)
-    corner = swap(rounded, ("dp", "sp"), replicas * parts, parts + 2)
+    corner = swap(rounded, ("dp", "sp"), replicas * parts, replicas // PAIR * parts + 2)
     far = swap(rounded, "sp", parts, 2)
-    beside = swap(rounded, "dp", replicas, 1)
-    sent = call(pool_kernel, struct((PAIR * DOCS, width), bf16), [VMEM] * 4)(corner, far, beside, partial)
+    beside = swap(rounded, "dp", replicas, replicas // PAIR)
+    sent = call(pool_kernel, struct((PAIR * DOCS, width), bf16), [VMEM] * 4)(corner, beside, far, partial)
     blocks = gather_pairs(sent, "dp", replicas)
     gram = call(gram_kernel, struct((docs, docs), f32), [VMEM] * len(blocks))(*blocks)
     return call(

time: 30.7 us -> 30.8 us (level)
  transfers between devices with their start and end apart: 12 -> 12, of which waited for: 9 -> 9; matrix products, arithmetic and copies ran while one was open for 0% -> 0% of each run, Pallas kernels for 8% -> 7%
where the time goes in v6:
time: 30.8 us; the launch traced here: 30.7 us
  starting transfers between devices  13 us (42%)
  waiting for transfers between devices  11.7 us (38%)
  Pallas kernels  5.35 us (17%)
  between operations  0.69 us (2%)
    ppermute x12, starting transfers between devices, swap(): return lax.ppermute(block, axis, [(s, s ^ distance) for s in range(size)])  13 us
    ppermute x12, waiting for transfers between devices, swap(): return lax.ppermute(block, axis, [(s, s ^ distance) for s in range(size)])  11.7 us
    pallas_call x1, Pallas kernels, per_device(): call(scores_kernel, struct((PAIR * HEAD_GROUP, parts * tokens), f32), [VM...  2.3 us
    pallas_call x1, Pallas kernels, per_device(): call(functools.partial(plan_kernel, parts), (struct((tokens, width), bf16...  1.59 us
    pallas_call x1, Pallas kernels, per_device(): call(grads_kernel, (struct((DOCS, features // parts), bf16), struct((DOCS...  1.02 us
  transfers between devices with their start and end apart: 12, of which 9 were waited for; matrix products, arithmetic and copies ran while one was open for 0% of the time, Pallas kernels for 7%

profile of v6, /device:TPU:0, one launch (start us, length us, event | category | flops | bytes accessed | tf_op | source)
XLA Modules:
  0.0 30.7 jit_solution(2221745228885923228)
XLA Ops:
  0.6 1.6 %shard_map.68 = (bf16[128,1792]{1,0:T(8,128)(2,1)S(1)}, bf16[128,256]{1,0:T(8,128)(2,1)S(1)}, bf16[128,256]{1,0:T(8,128)(2,1)S(1)}, bf16[128,2304]{1,0:T(8,128)(...) custom-call(s32[1,8]{1,0:T(1,128)} %lengths_hbm.1, ...), custom_call_target="tpu_custom_call" | custom-call | bytes 1179648 | tf_op jit(solution)/shard_map/pallas_call | solution.py:237
  2.2 0.5 %collective-permute-start = (bf16[128,2304]{1,0:T(8,128)(2,1)S(1)}, bf16[128,2304]{1,0:T(8,128)(2,1)S(1)}, u32[]{:S(2)}, u32[]{:S(2)}) collective-permute-start(bf16[128,2304]{1,0:T(8,128)(2,1)S(1)} %get-tuple-element.17), channel_id=1, source_target_pairs={{0,1},{1,0},{2,3},{3,2},{4,5},{5,4},{6,7},{7,6},{8,9},{9,8},{10,11... | collective-permute-start | bytes 1769480 | tf_op jit(solution)/shard_map/ppermute | solution.py:214
  2.7 2.6 %collective-permute-start.1 = (bf16[128,256]{1,0:T(8,128)(2,1)S(1)}, bf16[128,256]{1,0:T(8,128)(2,1)S(1)}, u32[]{:S(2)}, u32[]{:S(2)}) collective-permute-start(bf16[128,256]{1,0:T(8,128)(2,1)S(1)} %get-tuple-element.16.k_own), channel_id=1, source_target_pairs={{0,2},{1,3},{2,0},{3,1},{4,6},{5,7},{6,4},{7,5},{8,10},{9,11},{10,... | collective-permute-start | bytes 196616 | tf_op jit(solution)/shard_map/ppermute | solution.py:214
  5.3 0.1 collective-permute-start.2
  5.4 1.7 %collective-permute-start.3 = (bf16[128,256]{1,0:T(8,128)(2,1)S(1)}, bf16[128,256]{1,0:T(8,128)(2,1)S(1)}, u32[]{:S(2)}, u32[]{:S(2)}) collective-permute-start(bf16[128,256]{1,0:T(8,128)(2,1)S(1)} %get-tuple-element.20.v_own), channel_id=1, source_target_pairs={{0,2},{1,3},{2,0},{3,1},{4,6},{5,7},{6,4},{7,5},{8,10},{9,11},{10,... | collective-permute-start | bytes 196616 | tf_op jit(solution)/shard_map/ppermute | solution.py:214
  7.1 0.0 collective-permute-start.4
  7.1 0.9 %collective-permute-done.1.k_far = bf16[128,256]{1,0:T(8,128)(2,1)S(1)} collective-permute-done((bf16[128,256]{1,0:T(8,128)(2,1)S(1)}, bf16[128,256]{1,0:T(8,128)(2,1)S(1)}, u32[]{:S(2)}, u32[]{:S(2)}) %collective-permute-start.1) | collective-permute-done | bytes 65568 | tf_op jit(solution)/shard_map/ppermute | solution.py:214
  8.0 1.4 %collective-permute-done.2.k_last = bf16[128,256]{1,0:T(8,128)(2,1)S(1)} collective-permute-done((bf16[128,256]{1,0:T(8,128)(2,1)S(1)}, bf16[128,256]{1,0:T(8,128)(2,1)S(1)}, u32[]{:S(2)}, u32[]{:S(2)}) %collective-permute-start.2) | collective-permute-done | bytes 65568 | tf_op jit(solution)/shard_map/ppermute | solution.py:214
  9.4 0.0 collective-permute-done.near
  9.4 2.3 %shard_map.69.sums_ref = f32[14,512]{1,0:T(8,128)S(1)} custom-call(f32[256,512]{1,0:T(8,128)S(1)} %get-tuple-element.14.bias_ref, bf16[128,1792]{1,0:T(8,128)(2,1)S(1)} %get-tuple-element.15.q_own, bf16[128,256]{1,0:T(8,128)(2,1)S(1)} %get-tuple-element.16.k_own, bf16[128,2304]{1,0:T(8,128)(2,1)S(1)} %collective-permute-done.near, ...), custom_call_target="tpu_custom_call" | custom-call | flops 234881024 | bytes 1966080 | tf_op jit(solution)/shard_map/pallas_call | solution.py:264
  11.7 0.0 collective-permute-done.3.v_far
  11.7 0.5 %collective-permute-done.4.v_last = bf16[128,256]{1,0:T(8,128)(2,1)S(1)} collective-permute-done((bf16[128,256]{1,0:T(8,128)(2,1)S(1)}, bf16[128,256]{1,0:T(8,128)(2,1)S(1)}, u32[]{:S(2)}, u32[]{:S(2)}) %collective-permute-start.4) | collective-permute-done | bytes 65568 | tf_op jit(solution)/shard_map/ppermute | solution.py:214
  12.2 0.2 shard_map.70
  12.4 3.4 %collective-permute-start.5 = (bf16[8,1792]{1,0:T(8,128)(2,1)S(1)}, bf16[8,1792]{1,0:T(8,128)(2,1)S(1)}, u32[]{:S(2)}, u32[]{:S(2)}) collective-permute-start(bf16[8,1792]{1,0:T(8,128)(2,1)S(1)} %get-tuple-element.22), channel_id=1, source_target_pairs={{0,18},{1,19},{2,16},{3,17},{4,22},{5,23},{6,20},{7,21},{8,26},{9,... | collective-permute-start | bytes 86024 | tf_op jit(solution)/shard_map/ppermute | solution.py:214
  15.8 0.3 %collective-permute-start.6 = (bf16[8,1792]{1,0:T(8,128)(2,1)S(1)}, bf16[8,1792]{1,0:T(8,128)(2,1)S(1)}, u32[]{:S(2)}, u32[]{:S(2)}) collective-permute-start(bf16[8,1792]{1,0:T(8,128)(2,1)S(1)} %get-tuple-element.22), channel_id=1, source_target_pairs={{0,16},{4,20},{8,24},{12,28},{16,0},{20,4},{24,8},{28,12},{1,17},{... | collective-permute-start | bytes 86024 | tf_op jit(solution)/shard_map/ppermute | solution.py:214
  16.2 0.7 %collective-permute-start.7 = (bf16[8,1792]{1,0:T(8,128)(2,1)S(1)}, bf16[8,1792]{1,0:T(8,128)(2,1)S(1)}, u32[]{:S(2)}, u32[]{:S(2)}) collective-permute-start(bf16[8,1792]{1,0:T(8,128)(2,1)S(1)} %get-tuple-element.22), channel_id=1, source_target_pairs={{0,2},{1,3},{2,0},{3,1},{4,6},{5,7},{6,4},{7,5},{8,10},{9,11},{10,... | collective-permute-start | bytes 86024 | tf_op jit(solution)/shard_map/ppermute | solution.py:214
  16.8 1.3 %collective-permute-done.5.corner_ref = bf16[8,1792]{1,0:T(8,128)(2,1)S(1)} collective-permute-done((bf16[8,1792]{1,0:T(8,128)(2,1)S(1)}, bf16[8,1792]{1,0:T(8,128)(2,1)S(1)}, u32[]{:S(2)}, u32[]{:S(2)}) %collective-permute-start.5) | collective-permute-done | bytes 28704 | tf_op jit(solution)/shard_map/ppermute | solution.py:214
  18.1 2.8 %collective-permute-done.6.next_ref = bf16[8,1792]{1,0:T(8,128)(2,1)S(1)} collective-permute-done((bf16[8,1792]{1,0:T(8,128)(2,1)S(1)}, bf16[8,1792]{1,0:T(8,128)(2,1)S(1)}, u32[]{:S(2)}, u32[]{:S(2)}) %collective-permute-start.6) | collective-permute-done | bytes 28704 | tf_op jit(solution)/shard_map/ppermute | solution.py:214
  20.9 0.0 collective-permute-done.7.far_ref.refs_5_
  20.9 2.3 %collective-permute-start.10 = (bf16[16,1792]{1,0:T(8,128)(2,1)S(1)}, bf16[16,1792]{1,0:T(8,128)(2,1)S(1)}, u32[]{:S(2)}, u32[]{:S(2)}) collective-permute-start(bf16[16,1792]{1,0:T(8,128)(2,1)S(1)} %shard_map.71.refs_3_), channel_id=1, source_target_pairs={{0,12},{4,8},{8,4},{12,0},{16,28},{20,24},{24,20},{28,16},{1,13},{... | collective-permute-start | bytes 172040 | tf_op jit(solution)/shard_map/ppermute | solution.py:214
  23.2 0.8 %collective-permute-start.8 = (bf16[16,1792]{1,0:T(8,128)(2,1)S(1)}, bf16[16,1792]{1,0:T(8,128)(2,1)S(1)}, u32[]{:S(2)}, u32[]{:S(2)}) collective-permute-start(bf16[16,1792]{1,0:T(8,128)(2,1)S(1)} %shard_map.71.refs_3_), channel_id=1, source_target_pairs={{0,8},{4,12},{8,0},{12,4},{16,24},{20,28},{24,16},{28,20},{1,9},{5... | collective-permute-start | bytes 172040 | tf_op jit(solution)/shard_map/ppermute | solution.py:214
  24.0 0.5 %collective-permute-start.9 = (bf16[16,1792]{1,0:T(8,128)(2,1)S(1)}, bf16[16,1792]{1,0:T(8,128)(2,1)S(1)}, u32[]{:S(2)}, u32[]{:S(2)}) collective-permute-start(bf16[16,1792]{1,0:T(8,128)(2,1)S(1)} %shard_map.71.refs_3_), channel_id=1, source_target_pairs={{0,4},{4,0},{8,12},{12,8},{16,20},{20,16},{24,28},{28,24},{1,5},{5... | collective-permute-start | bytes 172040 | tf_op jit(solution)/shard_map/ppermute | solution.py:214
  24.5 1.6 %collective-permute-done.10.refs_2_ = bf16[16,1792]{1,0:T(8,128)(2,1)S(1)} collective-permute-done((bf16[16,1792]{1,0:T(8,128)(2,1)S(1)}, bf16[16,1792]{1,0:T(8,128)(2,1)S(1)}, u32[]{:S(2)}, u32[]{:S(2)}) %collective-permute-start.10) | collective-permute-done | bytes 57376 | tf_op jit(solution)/shard_map/ppermute | solution.py:214
  26.1 1.3 %collective-permute-done.8.refs_0_ = bf16[16,1792]{1,0:T(8,128)(2,1)S(1)} collective-permute-done((bf16[16,1792]{1,0:T(8,128)(2,1)S(1)}, bf16[16,1792]{1,0:T(8,128)(2,1)S(1)}, u32[]{:S(2)}, u32[]{:S(2)}) %collective-permute-start.8) | collective-permute-done | bytes 57376 | tf_op jit(solution)/shard_map/ppermute | solution.py:214
  27.4 0.8 %collective-permute-done.9.refs_1_ = bf16[16,1792]{1,0:T(8,128)(2,1)S(1)} collective-permute-done((bf16[16,1792]{1,0:T(8,128)(2,1)S(1)}, bf16[16,1792]{1,0:T(8,128)(2,1)S(1)}, u32[]{:S(2)}, u32[]{:S(2)}) %collective-permute-start.9) | collective-permute-done | bytes 57376 | tf_op jit(solution)/shard_map/ppermute | solution.py:214
  28.2 0.2 shard_map.72.gram_one
  28.4 0.1 collective-permute-start.11
  28.4 1.2 %collective-permute-done.11.gram_two = f32[64,64]{1,0:T(8,128)S(1)} collective-permute-done((f32[64,64]{1,0:T(8,128)S(1)}, f32[64,64]{1,0:T(8,128)S(1)}, u32[]{:S(2)}, u32[]{:S(2)}) %collective-permute-start.11) | collective-permute-done | bytes 16416 | tf_op jit(solution)/shard_map/ppermute | solution.py:214
  29.6 1.0 %shard_map.73 = (bf16[8,896]{1,0:T(8,128)(2,1)}, f32[8,896]{1,0:T(8,128)}) custom-call(f32[8,64]{1,0:T(8,128)S(1)} %get-tuple-element.13.partner_ref, f32[64,64]{1,0:T(8,128)S(1)} %shard_map.72.gram_one, f32[64,64]{1,0:T(8,128)S(1)} %collective-permute-done.11.gram_two, bf16[16,1792]{1,0:T(8,128)(2,1)S(1)} %collective-permute-done.8.refs_0_, ...), custom_call_target="tpu_custom_call" | custom-call | tf_op jit(solution)/shard_map/pallas_call | solution.py:280
  (1 shorter events, 0.0 us)
Async XLA Ops:
  2.2 7.1 %collective-permute-start = (bf16[128,2304]{1,0:T(8,128)(2,1)S(1)}, bf16[128,2304]{1,0:T(8,128)(2,1)S(1)}, u32[]{:S(2)}, u32[]{:S(2)}) collective-permute-start(bf16[128,2304]{1,0:T(8,128)(2,1)S(1)} %get-tuple-element.17), channel_id=1, source_target_pairs={{0,1},{1,0},{2,3},{3,2},{4,5},{5,4},{6,7},{7,6},{8,9},{9,8},{10,11... | collective-permute-start | bytes 1769480 | tf_op jit(solution)/shard_map/ppermute | solution.py:214
  2.7 5.3 %collective-permute-start.1 = (bf16[128,256]{1,0:T(8,128)(2,1)S(1)}, bf16[128,256]{1,0:T(8,128)(2,1)S(1)}, u32[]{:S(2)}, u32[]{:S(2)}) collective-permute-start(bf16[128,256]{1,0:T(8,128)(2,1)S(1)} %get-tuple-element.16.k_own), channel_id=1, source_target_pairs={{0,2},{1,3},{2,0},{3,1},{4,6},{5,7},{6,4},{7,5},{8,10},{9,11},{10,... | collective-permute-start | bytes 196616 | tf_op jit(solution)/shard_map/ppermute | solution.py:214
  5.3 4.0 %collective-permute-start.2 = (bf16[128,256]{1,0:T(8,128)(2,1)S(1)}, bf16[128,256]{1,0:T(8,128)(2,1)S(1)}, u32[]{:S(2)}, u32[]{:S(2)}) collective-permute-start(bf16[128,256]{1,0:T(8,128)(2,1)S(1)} %get-tuple-element.18), channel_id=1, source_target_pairs={{0,3},{1,2},{2,1},{3,0},{4,7},{5,6},{6,5},{7,4},{8,11},{9,10},{10,... | collective-permute-start | bytes 196616 | tf_op jit(solution)/shard_map/ppermute | solution.py:214
  5.4 6.3 %collective-permute-start.3 = (bf16[128,256]{1,0:T(8,128)(2,1)S(1)}, bf16[128,256]{1,0:T(8,128)(2,1)S(1)}, u32[]{:S(2)}, u32[]{:S(2)}) collective-permute-start(bf16[128,256]{1,0:T(8,128)(2,1)S(1)} %get-tuple-element.20.v_own), channel_id=1, source_target_pairs={{0,2},{1,3},{2,0},{3,1},{4,6},{5,7},{6,4},{7,5},{8,10},{9,11},{10,... | collective-permute-start | bytes 196616 | tf_op jit(solution)/shard_map/ppermute | solution.py:214
  7.1 5.0 %collective-permute-start.4 = (bf16[128,256]{1,0:T(8,128)(2,1)S(1)}, bf16[128,256]{1,0:T(8,128)(2,1)S(1)}, u32[]{:S(2)}, u32[]{:S(2)}) collective-permute-start(bf16[128,256]{1,0:T(8,128)(2,1)S(1)} %get-tuple-element.21), channel_id=1, source_target_pairs={{0,3},{1,2},{2,1},{3,0},{4,7},{5,6},{6,5},{7,4},{8,11},{9,10},{10,... | collective-permute-start | bytes 196616 | tf_op jit(solution)/shard_map/ppermute | solution.py:214
  12.4 5.7 %collective-permute-start.5 = (bf16[8,1792]{1,0:T(8,128)(2,1)S(1)}, bf16[8,1792]{1,0:T(8,128)(2,1)S(1)}, u32[]{:S(2)}, u32[]{:S(2)}) collective-permute-start(bf16[8,1792]{1,0:T(8,128)(2,1)S(1)} %get-tuple-element.22), channel_id=1, source_target_pairs={{0,18},{1,19},{2,16},{3,17},{4,22},{5,23},{6,20},{7,21},{8,26},{9,... | collective-permute-start | bytes 86024 | tf_op jit(solution)/shard_map/ppermute | solution.py:214
  15.8 5.1 %collective-permute-start.6 = (bf16[8,1792]{1,0:T(8,128)(2,1)S(1)}, bf16[8,1792]{1,0:T(8,128)(2,1)S(1)}, u32[]{:S(2)}, u32[]{:S(2)}) collective-permute-start(bf16[8,1792]{1,0:T(8,128)(2,1)S(1)} %get-tuple-element.22), channel_id=1, source_target_pairs={{0,16},{4,20},{8,24},{12,28},{16,0},{20,4},{24,8},{28,12},{1,17},{... | collective-permute-start | bytes 86024 | tf_op jit(solution)/shard_map/ppermute | solution.py:214
  16.2 4.7 %collective-permute-start.7 = (bf16[8,1792]{1,0:T(8,128)(2,1)S(1)}, bf16[8,1792]{1,0:T(8,128)(2,1)S(1)}, u32[]{:S(2)}, u32[]{:S(2)}) collective-permute-start(bf16[8,1792]{1,0:T(8,128)(2,1)S(1)} %get-tuple-element.22), channel_id=1, source_target_pairs={{0,2},{1,3},{2,0},{3,1},{4,6},{5,7},{6,4},{7,5},{8,10},{9,11},{10,... | collective-permute-start | bytes 86024 | tf_op jit(solution)/shard_map/ppermute | solution.py:214
  20.9 5.1 %collective-permute-start.10 = (bf16[16,1792]{1,0:T(8,128)(2,1)S(1)}, bf16[16,1792]{1,0:T(8,128)(2,1)S(1)}, u32[]{:S(2)}, u32[]{:S(2)}) collective-permute-start(bf16[16,1792]{1,0:T(8,128)(2,1)S(1)} %shard_map.71.refs_3_), channel_id=1, source_target_pairs={{0,12},{4,8},{8,4},{12,0},{16,28},{20,24},{24,20},{28,16},{1,13},{... | collective-permute-start | bytes 172040 | tf_op jit(solution)/shard_map/ppermute | solution.py:214
  23.2 4.2 %collective-permute-start.8 = (bf16[16,1792]{1,0:T(8,128)(2,1)S(1)}, bf16[16,1792]{1,0:T(8,128)(2,1)S(1)}, u32[]{:S(2)}, u32[]{:S(2)}) collective-permute-start(bf16[16,1792]{1,0:T(8,128)(2,1)S(1)} %shard_map.71.refs_3_), channel_id=1, source_target_pairs={{0,8},{4,12},{8,0},{12,4},{16,24},{20,28},{24,16},{28,20},{1,9},{5... | collective-permute-start | bytes 172040 | tf_op jit(solution)/shard_map/ppermute | solution.py:214
  24.0 4.2 %collective-permute-start.9 = (bf16[16,1792]{1,0:T(8,128)(2,1)S(1)}, bf16[16,1792]{1,0:T(8,128)(2,1)S(1)}, u32[]{:S(2)}, u32[]{:S(2)}) collective-permute-start(bf16[16,1792]{1,0:T(8,128)(2,1)S(1)} %shard_map.71.refs_3_), channel_id=1, source_target_pairs={{0,4},{4,0},{8,12},{12,8},{16,20},{20,16},{24,28},{28,24},{1,5},{5... | collective-permute-start | bytes 172040 | tf_op jit(solution)/shard_map/ppermute | solution.py:214
  28.4 1.3 %collective-permute-start.11 = (f32[64,64]{1,0:T(8,128)S(1)}, f32[64,64]{1,0:T(8,128)S(1)}, u32[]{:S(2)}, u32[]{:S(2)}) collective-permute-start(f32[64,64]{1,0:T(8,128)S(1)} %shard_map.72.gram_one), channel_id=1, source_target_pairs={{0,1},{1,0},{2,3},{3,2},{4,5},{5,4},{6,7},{7,6},{8,9},{9,8},{10,11... | collective-permute-start | bytes 49160 | tf_op jit(solution)/shard_map/ppermute | solution.py:214

commit v7 on v3

--- a/solution.py
+++ b/solution.py
@@ -32,7 +32,7 @@
 
 
 def plan_kernel(parts, lengths_hbm, pairs_hbm, q_hbm, k_hbm, v_hbm, *refs):
-    q_out, k_out, v_out, near_out, k_far_out, v_far_out, bias_ref, doc_ref, partner_ref, lengths_ref, pairs_ref, sem, small_sem = refs
+    q_out, k_out, v_out, v_far_out, near_out, bias_ref, doc_ref, partner_ref, lengths_ref, pairs_ref, sem, small_sem = refs
     span = k_hbm.shape[0]
     me = lax.axis_index("sp")
     core = lax.rem(me, PAIR)
@@ -56,14 +56,11 @@
                 )
             )
 
-    pair_width = PAIR * HEAD_SIZE
-    cut(k_hbm, 0, k_out, 0)
-    cut(k_hbm, 1, k_far_out, 0)
-    cut(k_hbm, 1, near_out, PAIR * GROUP_WIDTH)
-    cut(q_hbm, 1, near_out, 0)
-    cut(v_hbm, 1, near_out, PAIR * GROUP_WIDTH + pair_width)
     cut(v_hbm, 0, v_out, 0)
     cut(v_hbm, 1, v_far_out, 0)
+    cut(k_hbm, 0, k_out, 0)
+    cut(k_hbm, 1, near_out, 0)
+    cut(v_hbm, 1, near_out, PAIR * HEAD_SIZE)
     cut(q_hbm, 0, q_out, 0)
     for copy in copies:
         copy.start()
@@ -94,19 +91,25 @@
         copy.wait()
 
 
-def scores_kernel(bias_ref, q_own, k_own, near, k_far, k_last, sums_ref):
+def cut_kernel(k_ref, one_ref, two_ref):
+    other = 1 - lax.rem(lax.axis_index("sp"), PAIR)
+    for p, ref in enumerate((one_ref, two_ref)):
+        ref[...] = k_ref[:, pl.ds(pl.multiple_of((PAIR * p + other) * HEAD_SIZE, HEAD_SIZE), HEAD_SIZE)]
+
+
+def scores_kernel(bias_ref, q_own, q_near, k_own, near, k_far, last_one, last_two, sums_ref):
+    core = lax.rem(lax.axis_index("sp"), PAIR)
     scale = HEAD_SIZE ** (-0.5) * math.log2(math.e)
-    for p in range(PAIR):
+    for p, last in enumerate((last_one, last_two)):
         here = slice(p * HEAD_SIZE, (p + 1) * HEAD_SIZE)
-        beside = PAIR * GROUP_WIDTH + p * HEAD_SIZE
-        key_head = jnp.concatenate(
-            [k_own[:, here], near[:, beside : beside + HEAD_SIZE], k_far[:, here], k_last[:, here]], axis=0
-        )
+        group = PAIR * p + core
+        there = pl.ds(pl.multiple_of(group * HEAD_SIZE, HEAD_SIZE), HEAD_SIZE)
+        key_head = jnp.concatenate([k_own[:, here], near[:, here], k_far[:, there], last[...]], axis=0)
         for h in range(HEAD_GROUP):
             place = (p * HEAD_GROUP + h) * HEAD_SIZE
+            beside = pl.multiple_of(group * GROUP_WIDTH + h * HEAD_SIZE, HEAD_SIZE)
             total = None
-            for t, q_ref in enumerate((q_own, near)):
-                query = q_ref[:, place : place + HEAD_SIZE]
+            for t, query in enumerate((q_own[:, place : place + HEAD_SIZE], q_near[:, pl.ds(beside, HEAD_SIZE)])):
                 rows = query.shape[0]
                 scores = lax.dot_general(
                     query, key_head, (((1,), (1,)), ((), ())), preferred_element_type=jnp.float32
@@ -122,9 +125,10 @@
 
 
 def values_kernel(sums_ref, doc_ref, v_own, near, v_far, v_last, out_ref, sent_ref):
+    core = lax.rem(lax.axis_index("sp"), PAIR)
     for p in range(PAIR):
         here = slice(p * HEAD_SIZE, (p + 1) * HEAD_SIZE)
-        beside = PAIR * (GROUP_WIDTH + HEAD_SIZE) + p * HEAD_SIZE
+        beside = (PAIR + p) * HEAD_SIZE
         value_head = jnp.concatenate(
             [v_own[:, here], near[:, beside : beside + HEAD_SIZE], v_far[:, here], v_last[:, here]], axis=0
         )
@@ -147,7 +151,7 @@
 
 
 def in_order(refs):
-    return (refs[-1], *refs[-3::-1], refs[-2])
+    return refs[::-1]
 
 
 def join_kernel(*refs):
@@ -218,7 +222,7 @@
             shape = (len(blocks) * block.shape[0], block.shape[1])
             block = call(join_kernel, jax.ShapeDtypeStruct(shape, block.dtype), [VMEM] * len(blocks))(*blocks)
         radix = min(4, size // have)
-        blocks = [swap(block, axis, size, r * have) for r in (*range(radix - 2, 0, -1), radix - 1)] + [block]
+        blocks = [swap(block, axis, size, r * have) for r in range(radix - 1, 0, -1)] + [block]
         have *= radix
     return blocks
 
@@ -231,15 +235,14 @@
     docs = DOCS * replicas
     f32, bf16 = jnp.float32, jnp.bfloat16
     struct = jax.ShapeDtypeStruct
-    query_own, key_own, value_own, near, key_send, value_send, bias, of_doc, partner = call(
+    key_far, query_near = swap(keys, "sp", parts, 2), swap(queries, "sp", parts, 1)
+    arguments = [pltpu.with_memory_space_constraint(x, pltpu.HBM) for x in (pair_ids, queries, keys, values)]
+    query_own, key_own, value_own, value_send, near, bias, of_doc, partner = call(
         functools.partial(plan_kernel, parts),
         (
             struct((tokens, width), bf16),
-            struct((tokens, kv_width), bf16),
-            struct((tokens, kv_width), bf16),
-            struct((tokens, width + 2 * kv_width), bf16),
-            struct((tokens, kv_width), bf16),
-            struct((tokens, kv_width), bf16),
+            *(struct((tokens, kv_width), bf16),) * 3,
+            struct((tokens, 2 * kv_width), bf16),
             struct((PAIR * tokens, parts * tokens), f32),
             struct((DOCS, parts * tokens), f32),
             struct((DOCS, docs), f32),
@@ -248,23 +251,25 @@
         [
             pltpu.SMEM((1, DOCS), jnp.int32),
             pltpu.SMEM((DOCS,), jnp.int32),
-            pltpu.SemaphoreType.DMA((8 * PAIR,)),
+            pltpu.SemaphoreType.DMA((6 * PAIR,)),
             pltpu.SemaphoreType.DMA((2,)),
         ],
         moved=2 * tokens * features + 4 * keys.size,
-    )(*(pltpu.with_memory_space_constraint(x, pltpu.HBM) for x in (document_lengths, pair_ids, queries, keys, values)))
+    )(pltpu.with_memory_space_constraint(document_lengths, pltpu.HBM), *arguments)
     near = swap(near, "sp", parts, 1)
     value_far = swap(value_own, "sp", parts, 2)
     value_last = swap(value_send, "sp", parts, 3)
-    key_far = swap(key_own, "sp", parts, 2)
-    key_last = swap(key_send, "sp", parts, 3)
+    last = [
+        swap(cut, "sp", parts, 1)
+        for cut in call(cut_kernel, (struct((tokens, HEAD_SIZE), bf16),) * PAIR, [VMEM])(key_far)
+    ]
     sums = call(
         scores_kernel,
         struct((PAIR * HEAD_GROUP, parts * tokens), f32),
-        [VMEM] * 6,
+        [VMEM] * 8,
         flops=tokens * features * tokens * parts,
         moved=2 * queries.size + 4 * parts * keys.size,
-    )(bias, query_own, key_own, near, key_far, key_last)
+    )(bias, query_own, query_near, key_own, near, key_far, *last)
     partial, rounded = call(
         values_kernel, (struct((DOCS, width), f32), struct((DOCS, width), bf16)), [VMEM] * 6
     )(sums, of_doc, value_own, near, value_far, value_last)

time: 30.7 us -> 31 us (level)
  starting transfers between devices: 13 us -> 14 us
  waiting for transfers between devices: 11.6 us -> 10.7 us
    ppermute x12 -> x14, starting transfers between devices: 13 us -> 14 us  [swap(): return lax.ppermute(block, axis, [(s, s ^ distance) for s in range(size)])]
    ppermute x12 -> x14, waiting for transfers between devices: 11.6 us -> 10.7 us  [swap(): return lax.ppermute(block, axis, [(s, s ^ distance) for s in range(size)])]
  transfers between devices with their start and end apart: 12 -> 14, of which waited for: 9 -> 9; matrix products, arithmetic and copies ran while one was open for 0% -> 0% of each run, Pallas kernels for 8% -> 13%
where the time goes in v7:
time: 31 us; the launch traced here: 30.8 us
  starting transfers between devices  14 us (45%)
  waiting for transfers between devices  10.7 us (35%)
  Pallas kernels  5.44 us (18%)
  between operations  0.71 us (2%)
    ppermute x14, starting transfers between devices, swap(): return lax.ppermute(block, axis, [(s, s ^ distance) for s in range(size)])  14 us
    ppermute x14, waiting for transfers between devices, swap(): return lax.ppermute(block, axis, [(s, s ^ distance) for s in range(size)])  10.7 us
    pallas_call x1, Pallas kernels, per_device(): call(scores_kernel, struct((PAIR * HEAD_GROUP, parts * tokens), f32), [VM...  2.59 us
    pallas_call x1, Pallas kernels, per_device(): call(functools.partial(plan_kernel, parts), (struct((tokens, width), bf16...  1.37 us
    pallas_call x1, Pallas kernels, per_device(): call(grads_kernel, (struct((DOCS, features // parts), bf16), struct((DOCS...  1.02 us
  transfers between devices with their start and end apart: 14, of which 9 were waited for; matrix products, arithmetic and copies ran while one was open for 0% of the time, Pallas kernels for 13%

profile of v7, /device:TPU:0, one launch (start us, length us, event | category | flops | bytes accessed | tf_op | source)
XLA Modules:
  0.0 30.8 jit_solution(15219489563969078716)
XLA Ops:
  0.6 0.5 %collective-permute-start = (bf16[128,3584]{1,0:T(8,128)(2,1)}, bf16[128,3584]{1,0:T(8,128)(2,1)S(1)}, u32[]{:S(2)}, u32[]{:S(2)}) collective-permute-start(bf16[128,3584]{1,0:T(8,128)(2,1)} %q_hbm.1), channel_id=1, source_target_pairs={{0,1},{1,0},{2,3},{3,2},{4,5},{5,4},{6,7},{7,6},{8,9},{9,8},{10,11... | collective-permute-start | bytes 2752520 | tf_op jit(solution)/shard_map/ppermute | solution.py:215
  1.1 2.6 %collective-permute-start.2 = (bf16[128,512]{1,0:T(8,128)(2,1)}, bf16[128,512]{1,0:T(8,128)(2,1)S(1)}, u32[]{:S(2)}, u32[]{:S(2)}) collective-permute-start(bf16[128,512]{1,0:T(8,128)(2,1)} %k_hbm.1), channel_id=1, source_target_pairs={{0,2},{1,3},{2,0},{3,1},{4,6},{5,7},{6,4},{7,5},{8,10},{9,11},{10,... | collective-permute-start | bytes 393224 | tf_op jit(solution)/shard_map/ppermute | solution.py:215
  3.7 1.4 %shard_map.68 = (bf16[128,1792]{1,0:T(8,128)(2,1)S(1)}, bf16[128,256]{1,0:T(8,128)(2,1)S(1)}, bf16[128,256]{1,0:T(8,128)(2,1)S(1)}, bf16[128,256]{1,0:T(8,128)(2...) custom-call(s32[1,8]{1,0:T(1,128)} %lengths_hbm.1, ...), custom_call_target="tpu_custom_call" | custom-call | bytes 1179648 | tf_op jit(solution)/shard_map/pallas_call | solution.py:240
  5.1 0.2 collective-permute-start.1
  5.3 0.3 collective-permute-start.5
  5.6 1.4 %collective-permute-start.6 = (bf16[128,256]{1,0:T(8,128)(2,1)S(1)}, bf16[128,256]{1,0:T(8,128)(2,1)S(1)}, u32[]{:S(2)}, u32[]{:S(2)}) collective-permute-start(bf16[128,256]{1,0:T(8,128)(2,1)S(1)} %get-tuple-element.23), channel_id=1, source_target_pairs={{0,3},{1,2},{2,1},{3,0},{4,7},{5,6},{6,5},{7,4},{8,11},{9,10},{10,... | collective-permute-start | bytes 196616 | tf_op jit(solution)/shard_map/ppermute | solution.py:215
  7.0 1.0 %collective-permute-done.2.k_ref.k_far = bf16[128,512]{1,0:T(8,128)(2,1)S(1)} collective-permute-done((bf16[128,512]{1,0:T(8,128)(2,1)}, bf16[128,512]{1,0:T(8,128)(2,1)S(1)}, u32[]{:S(2)}, u32[]{:S(2)}) %collective-permute-start.2) | collective-permute-done | bytes 131104 | tf_op jit(solution)/shard_map/ppermute | solution.py:215
  8.0 0.1 collective-permute-start.3
  8.1 0.0 collective-permute-done.1.near
  8.1 0.5 %collective-permute-start.4 = (bf16[128,128]{1,0:T(8,128)(2,1)S(1)}, bf16[128,128]{1,0:T(8,128)(2,1)S(1)}, u32[]{:S(2)}, u32[]{:S(2)}) collective-permute-start(bf16[128,128]{1,0:T(8,128)(2,1)S(1)} %get-tuple-element.20), channel_id=1, source_target_pairs={{0,1},{1,0},{2,3},{3,2},{4,5},{5,4},{6,7},{7,6},{8,9},{9,8},{10,11... | collective-permute-start | bytes 98312 | tf_op jit(solution)/shard_map/ppermute | solution.py:215
  8.6 0.7 %collective-permute-done.3.last_one = bf16[128,128]{1,0:T(8,128)(2,1)S(1)} collective-permute-done((bf16[128,128]{1,0:T(8,128)(2,1)S(1)}, bf16[128,128]{1,0:T(8,128)(2,1)S(1)}, u32[]{:S(2)}, u32[]{:S(2)}) %collective-permute-start.3) | collective-permute-done | bytes 32800 | tf_op jit(solution)/shard_map/ppermute | solution.py:215
  9.3 0.2 collective-permute-done.4.last_two
  9.5 0.0 collective-permute-done.q_near
  9.5 2.6 %shard_map.70.sums_ref = f32[14,512]{1,0:T(8,128)S(1)} custom-call(f32[256,512]{1,0:T(8,128)S(1)} %get-tuple-element.15.bias_ref, bf16[128,1792]{1,0:T(8,128)(2,1)S(1)} %get-tuple-element.16.q_own, bf16[128,3584]{1,0:T(8,128)(2,1)S(1)} %collective-permute-done.q_near, bf16[128,256]{1,0:T(8,128)(2,1)S(1)} %get-tuple-element.17.k_own, ...), custom_call_target="tpu_custom_call" | custom-call | flops 234881024 | bytes 1966080 | tf_op jit(solution)/shard_map/pallas_call | solution.py:266
  12.1 0.0 collective-permute-done.5.v_far
  12.1 0.0 collective-permute-done.6.v_last
  12.1 0.2 shard_map.71
  12.3 3.2 %collective-permute-start.7 = (bf16[8,1792]{1,0:T(8,128)(2,1)S(1)}, bf16[8,1792]{1,0:T(8,128)(2,1)S(1)}, u32[]{:S(2)}, u32[]{:S(2)}) collective-permute-start(bf16[8,1792]{1,0:T(8,128)(2,1)S(1)} %get-tuple-element.24), channel_id=1, source_target_pairs={{0,6},{1,7},{2,4},{3,5},{4,2},{5,3},{6,0},{7,1},{8,14},{9,15},{10,... | collective-permute-start | bytes 86024 | tf_op jit(solution)/shard_map/ppermute | solution.py:215
  15.6 0.1 collective-permute-start.8
  15.7 0.6 %collective-permute-start.9 = (bf16[8,1792]{1,0:T(8,128)(2,1)S(1)}, bf16[8,1792]{1,0:T(8,128)(2,1)S(1)}, u32[]{:S(2)}, u32[]{:S(2)}) collective-permute-start(bf16[8,1792]{1,0:T(8,128)(2,1)S(1)} %get-tuple-element.24), channel_id=1, source_target_pairs={{0,4},{4,0},{8,12},{12,8},{16,20},{20,16},{24,28},{28,24},{1,5},{5... | collective-permute-start | bytes 86024 | tf_op jit(solution)/shard_map/ppermute | solution.py:215
  16.2 1.2 %collective-permute-done.7.corner_ref = bf16[8,1792]{1,0:T(8,128)(2,1)S(1)} collective-permute-done((bf16[8,1792]{1,0:T(8,128)(2,1)S(1)}, bf16[8,1792]{1,0:T(8,128)(2,1)S(1)}, u32[]{:S(2)}, u32[]{:S(2)}) %collective-permute-start.7) | collective-permute-done | bytes 28704 | tf_op jit(solution)/shard_map/ppermute | solution.py:215
  17.4 2.0 %collective-permute-done.8.far_ref.refs_5_ = bf16[8,1792]{1,0:T(8,128)(2,1)S(1)} collective-permute-done((bf16[8,1792]{1,0:T(8,128)(2,1)S(1)}, bf16[8,1792]{1,0:T(8,128)(2,1)S(1)}, u32[]{:S(2)}, u32[]{:S(2)}) %collective-permute-start.8) | collective-permute-done | bytes 28704 | tf_op jit(solution)/shard_map/ppermute | solution.py:215
  19.4 0.1 collective-permute-done.9.next_ref
  19.6 3.7 %collective-permute-start.10 = (bf16[16,1792]{1,0:T(8,128)(2,1)S(1)}, bf16[16,1792]{1,0:T(8,128)(2,1)S(1)}, u32[]{:S(2)}, u32[]{:S(2)}) collective-permute-start(bf16[16,1792]{1,0:T(8,128)(2,1)S(1)} %shard_map.72.refs_3_), channel_id=1, source_target_pairs={{0,24},{4,28},{8,16},{12,20},{16,8},{20,12},{24,0},{28,4},{1,25},{... | collective-permute-start | bytes 172040 | tf_op jit(solution)/shard_map/ppermute | solution.py:215
  23.2 0.0 collective-permute-start.11
  23.2 0.8 %collective-permute-start.12 = (bf16[16,1792]{1,0:T(8,128)(2,1)S(1)}, bf16[16,1792]{1,0:T(8,128)(2,1)S(1)}, u32[]{:S(2)}, u32[]{:S(2)}) collective-permute-start(bf16[16,1792]{1,0:T(8,128)(2,1)S(1)} %shard_map.72.refs_3_), channel_id=1, source_target_pairs={{0,8},{4,12},{8,0},{12,4},{16,24},{20,28},{24,16},{28,20},{1,9},{5... | collective-permute-start | bytes 172040 | tf_op jit(solution)/shard_map/ppermute | solution.py:215
  24.0 1.6 %collective-permute-done.10.refs_0_ = bf16[16,1792]{1,0:T(8,128)(2,1)S(1)} collective-permute-done((bf16[16,1792]{1,0:T(8,128)(2,1)S(1)}, bf16[16,1792]{1,0:T(8,128)(2,1)S(1)}, u32[]{:S(2)}, u32[]{:S(2)}) %collective-permute-start.10) | collective-permute-done | bytes 57376 | tf_op jit(solution)/shard_map/ppermute | solution.py:215
  25.6 2.7 %collective-permute-done.11.refs_1_ = bf16[16,1792]{1,0:T(8,128)(2,1)S(1)} collective-permute-done((bf16[16,1792]{1,0:T(8,128)(2,1)S(1)}, bf16[16,1792]{1,0:T(8,128)(2,1)S(1)}, u32[]{:S(2)}, u32[]{:S(2)}) %collective-permute-start.11) | collective-permute-done | bytes 57376 | tf_op jit(solution)/shard_map/ppermute | solution.py:215
  28.3 0.2 shard_map.73.gram_one
  28.5 0.1 collective-permute-start.13
  28.6 1.2 %collective-permute-done.13.gram_two = f32[64,64]{1,0:T(8,128)S(1)} collective-permute-done((f32[64,64]{1,0:T(8,128)S(1)}, f32[64,64]{1,0:T(8,128)S(1)}, u32[]{:S(2)}, u32[]{:S(2)}) %collective-permute-start.13) | collective-permute-done | bytes 16416 | tf_op jit(solution)/shard_map/ppermute | solution.py:215
  29.8 1.0 %shard_map.74 = (bf16[8,896]{1,0:T(8,128)(2,1)}, f32[8,896]{1,0:T(8,128)}) custom-call(f32[8,64]{1,0:T(8,128)S(1)} %get-tuple-element.14.partner_ref, f32[64,64]{1,0:T(8,128)S(1)} %shard_map.73.gram_one, f32[64,64]{1,0:T(8,128)S(1)} %collective-permute-done.13.gram_two, bf16[16,1792]{1,0:T(8,128)(2,1)S(1)} %collective-permute-done.10.refs_0_, ...), custom_call_target="tpu_custom_call" | custom-call | tf_op jit(solution)/shard_map/pallas_call | solution.py:282
  (3 shorter events, 0.0 us)
Async XLA Ops:
  0.6 8.8 %collective-permute-start = (bf16[128,3584]{1,0:T(8,128)(2,1)}, bf16[128,3584]{1,0:T(8,128)(2,1)S(1)}, u32[]{:S(2)}, u32[]{:S(2)}) collective-permute-start(bf16[128,3584]{1,0:T(8,128)(2,1)} %q_hbm.1), channel_id=1, source_target_pairs={{0,1},{1,0},{2,3},{3,2},{4,5},{5,4},{6,7},{7,6},{8,9},{9,8},{10,11... | collective-permute-start | bytes 2752520 | tf_op jit(solution)/shard_map/ppermute | solution.py:215
  1.1 6.9 %collective-permute-start.2 = (bf16[128,512]{1,0:T(8,128)(2,1)}, bf16[128,512]{1,0:T(8,128)(2,1)S(1)}, u32[]{:S(2)}, u32[]{:S(2)}) collective-permute-start(bf16[128,512]{1,0:T(8,128)(2,1)} %k_hbm.1), channel_id=1, source_target_pairs={{0,2},{1,3},{2,0},{3,1},{4,6},{5,7},{6,4},{7,5},{8,10},{9,11},{10,... | collective-permute-start | bytes 393224 | tf_op jit(solution)/shard_map/ppermute | solution.py:215
  5.1 3.0 %collective-permute-start.1 = (bf16[128,512]{1,0:T(8,128)(2,1)S(1)}, bf16[128,512]{1,0:T(8,128)(2,1)S(1)}, u32[]{:S(2)}, u32[]{:S(2)}) collective-permute-start(bf16[128,512]{1,0:T(8,128)(2,1)S(1)} %get-tuple-element.18), channel_id=1, source_target_pairs={{0,1},{1,0},{2,3},{3,2},{4,5},{5,4},{6,7},{7,6},{8,9},{9,8},{10,11... | collective-permute-start | bytes 393224 | tf_op jit(solution)/shard_map/ppermute | solution.py:215
  5.3 6.8 %collective-permute-start.5 = (bf16[128,256]{1,0:T(8,128)(2,1)S(1)}, bf16[128,256]{1,0:T(8,128)(2,1)S(1)}, u32[]{:S(2)}, u32[]{:S(2)}) collective-permute-start(bf16[128,256]{1,0:T(8,128)(2,1)S(1)} %get-tuple-element.22.v_own), channel_id=1, source_target_pairs={{0,2},{1,3},{2,0},{3,1},{4,6},{5,7},{6,4},{7,5},{8,10},{9,11},{10,... | collective-permute-start | bytes 196616 | tf_op jit(solution)/shard_map/ppermute | solution.py:215
  5.6 6.5 %collective-permute-start.6 = (bf16[128,256]{1,0:T(8,128)(2,1)S(1)}, bf16[128,256]{1,0:T(8,128)(2,1)S(1)}, u32[]{:S(2)}, u32[]{:S(2)}) collective-permute-start(bf16[128,256]{1,0:T(8,128)(2,1)S(1)} %get-tuple-element.23), channel_id=1, source_target_pairs={{0,3},{1,2},{2,1},{3,0},{4,7},{5,6},{6,5},{7,4},{8,11},{9,10},{10,... | collective-permute-start | bytes 196616 | tf_op jit(solution)/shard_map/ppermute | solution.py:215
  8.0 1.3 %collective-permute-start.3 = (bf16[128,128]{1,0:T(8,128)(2,1)S(1)}, bf16[128,128]{1,0:T(8,128)(2,1)S(1)}, u32[]{:S(2)}, u32[]{:S(2)}) collective-permute-start(bf16[128,128]{1,0:T(8,128)(2,1)S(1)} %get-tuple-element.19), channel_id=1, source_target_pairs={{0,1},{1,0},{2,3},{3,2},{4,5},{5,4},{6,7},{7,6},{8,9},{9,8},{10,11... | collective-permute-start | bytes 98312 | tf_op jit(solution)/shard_map/ppermute | solution.py:215
  8.1 1.4 %collective-permute-start.4 = (bf16[128,128]{1,0:T(8,128)(2,1)S(1)}, bf16[128,128]{1,0:T(8,128)(2,1)S(1)}, u32[]{:S(2)}, u32[]{:S(2)}) collective-permute-start(bf16[128,128]{1,0:T(8,128)(2,1)S(1)} %get-tuple-element.20), channel_id=1, source_target_pairs={{0,1},{1,0},{2,3},{3,2},{4,5},{5,4},{6,7},{7,6},{8,9},{9,8},{10,11... | collective-permute-start | bytes 98312 | tf_op jit(solution)/shard_map/ppermute | solution.py:215
  12.3 5.1 %collective-permute-start.7 = (bf16[8,1792]{1,0:T(8,128)(2,1)S(1)}, bf16[8,1792]{1,0:T(8,128)(2,1)S(1)}, u32[]{:S(2)}, u32[]{:S(2)}) collective-permute-start(bf16[8,1792]{1,0:T(8,128)(2,1)S(1)} %get-tuple-element.24), channel_id=1, source_target_pairs={{0,6},{1,7},{2,4},{3,5},{4,2},{5,3},{6,0},{7,1},{8,14},{9,15},{10,... | collective-permute-start | bytes 86024 | tf_op jit(solution)/shard_map/ppermute | solution.py:215
  15.6 3.9 %collective-permute-start.8 = (bf16[8,1792]{1,0:T(8,128)(2,1)S(1)}, bf16[8,1792]{1,0:T(8,128)(2,1)S(1)}, u32[]{:S(2)}, u32[]{:S(2)}) collective-permute-start(bf16[8,1792]{1,0:T(8,128)(2,1)S(1)} %get-tuple-element.24), channel_id=1, source_target_pairs={{0,2},{1,3},{2,0},{3,1},{4,6},{5,7},{6,4},{7,5},{8,10},{9,11},{10,... | collective-permute-start | bytes 86024 | tf_op jit(solution)/shard_map/ppermute | solution.py:215
  15.7 3.9 %collective-permute-start.9 = (bf16[8,1792]{1,0:T(8,128)(2,1)S(1)}, bf16[8,1792]{1,0:T(8,128)(2,1)S(1)}, u32[]{:S(2)}, u32[]{:S(2)}) collective-permute-start(bf16[8,1792]{1,0:T(8,128)(2,1)S(1)} %get-tuple-element.24), channel_id=1, source_target_pairs={{0,4},{4,0},{8,12},{12,8},{16,20},{20,16},{24,28},{28,24},{1,5},{5... | collective-permute-start | bytes 86024 | tf_op jit(solution)/shard_map/ppermute | solution.py:215
  19.6 6.1 %collective-permute-start.10 = (bf16[16,1792]{1,0:T(8,128)(2,1)S(1)}, bf16[16,1792]{1,0:T(8,128)(2,1)S(1)}, u32[]{:S(2)}, u32[]{:S(2)}) collective-permute-start(bf16[16,1792]{1,0:T(8,128)(2,1)S(1)} %shard_map.72.refs_3_), channel_id=1, source_target_pairs={{0,24},{4,28},{8,16},{12,20},{16,8},{20,12},{24,0},{28,4},{1,25},{... | collective-permute-start | bytes 172040 | tf_op jit(solution)/shard_map/ppermute | solution.py:215
  23.2 5.1 %collective-permute-start.11 = (bf16[16,1792]{1,0:T(8,128)(2,1)S(1)}, bf16[16,1792]{1,0:T(8,128)(2,1)S(1)}, u32[]{:S(2)}, u32[]{:S(2)}) collective-permute-start(bf16[16,1792]{1,0:T(8,128)(2,1)S(1)} %shard_map.72.refs_3_), channel_id=1, source_target_pairs={{0,16},{4,20},{8,24},{12,28},{16,0},{20,4},{24,8},{28,12},{1,17},{... | collective-permute-start | bytes 172040 | tf_op jit(solution)/shard_map/ppermute | solution.py:215
  23.2 5.1 %collective-permute-start.12 = (bf16[16,1792]{1,0:T(8,128)(2,1)S(1)}, bf16[16,1792]{1,0:T(8,128)(2,1)S(1)}, u32[]{:S(2)}, u32[]{:S(2)}) collective-permute-start(bf16[16,1792]{1,0:T(8,128)(2,1)S(1)} %shard_map.72.refs_3_), channel_id=1, source_target_pairs={{0,8},{4,12},{8,0},{12,4},{16,24},{20,28},{24,16},{28,20},{1,9},{5... | collective-permute-start | bytes 172040 | tf_op jit(solution)/shard_map/ppermute | solution.py:215
  28.5 1.3 %collective-permute-start.13 = (f32[64,64]{1,0:T(8,128)S(1)}, f32[64,64]{1,0:T(8,128)S(1)}, u32[]{:S(2)}, u32[]{:S(2)}) collective-permute-start(f32[64,64]{1,0:T(8,128)S(1)} %shard_map.73.gram_one), channel_id=1, source_target_pairs={{0,1},{1,0},{2,3},{3,2},{4,5},{5,4},{6,7},{7,6},{8,9},{9,8},{10,11... | collective-permute-start | bytes 49160 | tf_op jit(solution)/shard_map/ppermute | solution.py:215

commit v8 on v3

--- a/solution.py
+++ b/solution.py
@@ -171,15 +171,10 @@
     inverse_column = lax.rsqrt(jnp.sum(square, axis=1, keepdims=True) + 1e-6)
     inverse_row = lax.rsqrt(jnp.sum(square, axis=0, keepdims=True) + 1e-6)
     cosine = gram * inverse_column * inverse_row
-    logits = jnp.where(diagonal, -jnp.inf, cosine * (1.0 / SOFTMAX_TEMP))
-    own = logits[:DOCS]
-    largest = jnp.max(own, axis=1, keepdims=True)
-    weights = jnp.exp(own - largest)
-    probs = weights / jnp.sum(weights, axis=1, keepdims=True)
-    largest_row = jnp.max(logits, axis=0, keepdims=True)
-    total_row = jnp.sum(jnp.exp(logits - largest_row), axis=0, keepdims=True)
-    probs = probs + jnp.exp(own - largest_row) / total_row
-    both = probs - partner_ref[...]
+    weights = jnp.where(diagonal, 0.0, jnp.exp(cosine * (1.0 / SOFTMAX_TEMP)))
+    own = weights[:DOCS]
+    total = 1.0 / jnp.sum(own, axis=1, keepdims=True) + 1.0 / jnp.sum(weights, axis=0, keepdims=True)
+    both = own * total - partner_ref[...]
     along = jnp.sum(both * cosine[:DOCS], axis=1, keepdims=True) * (1.0 / SOFTMAX_TEMP)
     weighted = both * inverse_row * (1.0 / SOFTMAX_TEMP)
     high = weighted.astype(jnp.bfloat16)

time: 30.7 us -> 30.7 us (level)
  no operation moved by 1% of the time
where the time goes in v8:
time: 30.7 us; the launch traced here: 30.5 us
  starting transfers between devices  13 us (42%)
  waiting for transfers between devices  11.6 us (38%)
  Pallas kernels  5.27 us (17%)
  between operations  0.69 us (2%)
    ppermute x12, starting transfers between devices, swap(): return lax.ppermute(block, axis, [(s, s ^ distance) for s in range(size)])  13 us
    ppermute x12, waiting for transfers between devices, swap(): return lax.ppermute(block, axis, [(s, s ^ distance) for s in range(size)])  11.6 us
    pallas_call x1, Pallas kernels, per_device(): call(scores_kernel, struct((PAIR * HEAD_GROUP, parts * tokens), f32), [VM...  2.3 us
    pallas_call x1, Pallas kernels, per_device(): call(functools.partial(plan_kernel, parts), (struct((tokens, width), bf16...  1.59 us
    pallas_call x1, Pallas kernels, per_device(): call(grads_kernel, (struct((DOCS, features // parts), bf16), struct((DOCS...  0.94 us
  transfers between devices with their start and end apart: 12, of which 9 were waited for; matrix products, arithmetic and copies ran while one was open for 0% of the time, Pallas kernels for 8%

profile of v8, /device:TPU:0, one launch (start us, length us, event | category | flops | bytes accessed | tf_op | source)
XLA Modules:
  0.0 30.5 jit_solution(2594633715292585465)
XLA Ops:
  0.6 1.6 %shard_map.68 = (bf16[128,1792]{1,0:T(8,128)(2,1)S(1)}, bf16[128,256]{1,0:T(8,128)(2,1)S(1)}, bf16[128,256]{1,0:T(8,128)(2,1)S(1)}, bf16[128,2304]{1,0:T(8,128)(...) custom-call(s32[1,8]{1,0:T(1,128)} %lengths_hbm.1, ...), custom_call_target="tpu_custom_call" | custom-call | bytes 1179648 | tf_op jit(solution)/shard_map/pallas_call | solution.py:229
  2.2 0.5 %collective-permute-start = (bf16[128,2304]{1,0:T(8,128)(2,1)S(1)}, bf16[128,2304]{1,0:T(8,128)(2,1)S(1)}, u32[]{:S(2)}, u32[]{:S(2)}) collective-permute-start(bf16[128,2304]{1,0:T(8,128)(2,1)S(1)} %get-tuple-element.17), channel_id=1, source_target_pairs={{0,1},{1,0},{2,3},{3,2},{4,5},{5,4},{6,7},{7,6},{8,9},{9,8},{10,11... | collective-permute-start | bytes 1769480 | tf_op jit(solution)/shard_map/ppermute | solution.py:206
  2.7 2.6 %collective-permute-start.1 = (bf16[128,256]{1,0:T(8,128)(2,1)S(1)}, bf16[128,256]{1,0:T(8,128)(2,1)S(1)}, u32[]{:S(2)}, u32[]{:S(2)}) collective-permute-start(bf16[128,256]{1,0:T(8,128)(2,1)S(1)} %get-tuple-element.16.k_own), channel_id=1, source_target_pairs={{0,2},{1,3},{2,0},{3,1},{4,6},{5,7},{6,4},{7,5},{8,10},{9,11},{10,... | collective-permute-start | bytes 196616 | tf_op jit(solution)/shard_map/ppermute | solution.py:206
  5.3 0.1 collective-permute-start.2
  5.4 1.7 %collective-permute-start.3 = (bf16[128,256]{1,0:T(8,128)(2,1)S(1)}, bf16[128,256]{1,0:T(8,128)(2,1)S(1)}, u32[]{:S(2)}, u32[]{:S(2)}) collective-permute-start(bf16[128,256]{1,0:T(8,128)(2,1)S(1)} %get-tuple-element.20.v_own), channel_id=1, source_target_pairs={{0,2},{1,3},{2,0},{3,1},{4,6},{5,7},{6,4},{7,5},{8,10},{9,11},{10,... | collective-permute-start | bytes 196616 | tf_op jit(solution)/shard_map/ppermute | solution.py:206
  7.1 0.0 collective-permute-start.4
  7.1 0.9 %collective-permute-done.1.k_far = bf16[128,256]{1,0:T(8,128)(2,1)S(1)} collective-permute-done((bf16[128,256]{1,0:T(8,128)(2,1)S(1)}, bf16[128,256]{1,0:T(8,128)(2,1)S(1)}, u32[]{:S(2)}, u32[]{:S(2)}) %collective-permute-start.1) | collective-permute-done | bytes 65568 | tf_op jit(solution)/shard_map/ppermute | solution.py:206
  8.0 1.4 %collective-permute-done.2.k_last = bf16[128,256]{1,0:T(8,128)(2,1)S(1)} collective-permute-done((bf16[128,256]{1,0:T(8,128)(2,1)S(1)}, bf16[128,256]{1,0:T(8,128)(2,1)S(1)}, u32[]{:S(2)}, u32[]{:S(2)}) %collective-permute-start.2) | collective-permute-done | bytes 65568 | tf_op jit(solution)/shard_map/ppermute | solution.py:206
  9.4 0.0 collective-permute-done.near
  9.4 2.3 %shard_map.69.sums_ref = f32[14,512]{1,0:T(8,128)S(1)} custom-call(f32[256,512]{1,0:T(8,128)S(1)} %get-tuple-element.14.bias_ref, bf16[128,1792]{1,0:T(8,128)(2,1)S(1)} %get-tuple-element.15.q_own, bf16[128,256]{1,0:T(8,128)(2,1)S(1)} %get-tuple-element.16.k_own, bf16[128,2304]{1,0:T(8,128)(2,1)S(1)} %collective-permute-done.near, ...), custom_call_target="tpu_custom_call" | custom-call | flops 234881024 | bytes 1966080 | tf_op jit(solution)/shard_map/pallas_call | solution.py:256
  11.7 0.0 collective-permute-done.3.v_far
  11.7 0.5 %collective-permute-done.4.v_last = bf16[128,256]{1,0:T(8,128)(2,1)S(1)} collective-permute-done((bf16[128,256]{1,0:T(8,128)(2,1)S(1)}, bf16[128,256]{1,0:T(8,128)(2,1)S(1)}, u32[]{:S(2)}, u32[]{:S(2)}) %collective-permute-start.4) | collective-permute-done | bytes 65568 | tf_op jit(solution)/shard_map/ppermute | solution.py:206
  12.2 0.2 shard_map.70
  12.4 2.4 %collective-permute-start.5 = (bf16[8,1792]{1,0:T(8,128)(2,1)S(1)}, bf16[8,1792]{1,0:T(8,128)(2,1)S(1)}, u32[]{:S(2)}, u32[]{:S(2)}) collective-permute-start(bf16[8,1792]{1,0:T(8,128)(2,1)S(1)} %get-tuple-element.22), channel_id=1, source_target_pairs={{0,6},{1,7},{2,4},{3,5},{4,2},{5,3},{6,0},{7,1},{8,14},{9,15},{10,... | collective-permute-start | bytes 86024 | tf_op jit(solution)/shard_map/ppermute | solution.py:206
  14.8 0.7 %collective-permute-start.6 = (bf16[8,1792]{1,0:T(8,128)(2,1)S(1)}, bf16[8,1792]{1,0:T(8,128)(2,1)S(1)}, u32[]{:S(2)}, u32[]{:S(2)}) collective-permute-start(bf16[8,1792]{1,0:T(8,128)(2,1)S(1)} %get-tuple-element.22), channel_id=1, source_target_pairs={{0,2},{1,3},{2,0},{3,1},{4,6},{5,7},{6,4},{7,5},{8,10},{9,11},{10,... | collective-permute-start | bytes 86024 | tf_op jit(solution)/shard_map/ppermute | solution.py:206
  15.4 0.5 %collective-permute-start.7 = (bf16[8,1792]{1,0:T(8,128)(2,1)S(1)}, bf16[8,1792]{1,0:T(8,128)(2,1)S(1)}, u32[]{:S(2)}, u32[]{:S(2)}) collective-permute-start(bf16[8,1792]{1,0:T(8,128)(2,1)S(1)} %get-tuple-element.22), channel_id=1, source_target_pairs={{0,4},{4,0},{8,12},{12,8},{16,20},{20,16},{24,28},{28,24},{1,5},{5... | collective-permute-start | bytes 86024 | tf_op jit(solution)/shard_map/ppermute | solution.py:206
  15.9 1.3 %collective-permute-done.5.corner_ref = bf16[8,1792]{1,0:T(8,128)(2,1)S(1)} collective-permute-done((bf16[8,1792]{1,0:T(8,128)(2,1)S(1)}, bf16[8,1792]{1,0:T(8,128)(2,1)S(1)}, u32[]{:S(2)}, u32[]{:S(2)}) %collective-permute-start.5) | collective-permute-done | bytes 28704 | tf_op jit(solution)/shard_map/ppermute | solution.py:206
  17.2 1.4 %collective-permute-done.6.far_ref.refs_5_ = bf16[8,1792]{1,0:T(8,128)(2,1)S(1)} collective-permute-done((bf16[8,1792]{1,0:T(8,128)(2,1)S(1)}, bf16[8,1792]{1,0:T(8,128)(2,1)S(1)}, u32[]{:S(2)}, u32[]{:S(2)}) %collective-permute-start.6) | collective-permute-done | bytes 28704 | tf_op jit(solution)/shard_map/ppermute | solution.py:206
  18.6 0.7 %collective-permute-done.7.next_ref = bf16[8,1792]{1,0:T(8,128)(2,1)S(1)} collective-permute-done((bf16[8,1792]{1,0:T(8,128)(2,1)S(1)}, bf16[8,1792]{1,0:T(8,128)(2,1)S(1)}, u32[]{:S(2)}, u32[]{:S(2)}) %collective-permute-start.7) | collective-permute-done | bytes 28704 | tf_op jit(solution)/shard_map/ppermute | solution.py:206
  19.3 3.7 %collective-permute-start.10 = (bf16[16,1792]{1,0:T(8,128)(2,1)S(1)}, bf16[16,1792]{1,0:T(8,128)(2,1)S(1)}, u32[]{:S(2)}, u32[]{:S(2)}) collective-permute-start(bf16[16,1792]{1,0:T(8,128)(2,1)S(1)} %shard_map.71.refs_3_), channel_id=1, source_target_pairs={{0,24},{4,28},{8,16},{12,20},{16,8},{20,12},{24,0},{28,4},{1,25},{... | collective-permute-start | bytes 172040 | tf_op jit(solution)/shard_map/ppermute | solution.py:206
  23.0 0.0 collective-permute-start.8
  23.0 0.8 %collective-permute-start.9 = (bf16[16,1792]{1,0:T(8,128)(2,1)S(1)}, bf16[16,1792]{1,0:T(8,128)(2,1)S(1)}, u32[]{:S(2)}, u32[]{:S(2)}) collective-permute-start(bf16[16,1792]{1,0:T(8,128)(2,1)S(1)} %shard_map.71.refs_3_), channel_id=1, source_target_pairs={{0,8},{4,12},{8,0},{12,4},{16,24},{20,28},{24,16},{28,20},{1,9},{5... | collective-permute-start | bytes 172040 | tf_op jit(solution)/shard_map/ppermute | solution.py:206
  23.8 1.7 %collective-permute-done.10.refs_2_ = bf16[16,1792]{1,0:T(8,128)(2,1)S(1)} collective-permute-done((bf16[16,1792]{1,0:T(8,128)(2,1)S(1)}, bf16[16,1792]{1,0:T(8,128)(2,1)S(1)}, u32[]{:S(2)}, u32[]{:S(2)}) %collective-permute-start.10) | collective-permute-done | bytes 57376 | tf_op jit(solution)/shard_map/ppermute | solution.py:206
  25.5 2.6 %collective-permute-done.8.refs_0_ = bf16[16,1792]{1,0:T(8,128)(2,1)S(1)} collective-permute-done((bf16[16,1792]{1,0:T(8,128)(2,1)S(1)}, bf16[16,1792]{1,0:T(8,128)(2,1)S(1)}, u32[]{:S(2)}, u32[]{:S(2)}) %collective-permute-start.8) | collective-permute-done | bytes 57376 | tf_op jit(solution)/shard_map/ppermute | solution.py:206
  28.1 0.0 collective-permute-done.9.refs_1_
  28.1 0.2 shard_map.72.gram_one
  28.3 0.1 collective-permute-start.11
  28.4 1.2 %collective-permute-done.11.gram_two = f32[64,64]{1,0:T(8,128)S(1)} collective-permute-done((f32[64,64]{1,0:T(8,128)S(1)}, f32[64,64]{1,0:T(8,128)S(1)}, u32[]{:S(2)}, u32[]{:S(2)}) %collective-permute-start.11) | collective-permute-done | bytes 16416 | tf_op jit(solution)/shard_map/ppermute | solution.py:206
  29.6 0.9 %shard_map.73 = (bf16[8,896]{1,0:T(8,128)(2,1)}, f32[8,896]{1,0:T(8,128)}) custom-call(f32[8,64]{1,0:T(8,128)S(1)} %get-tuple-element.13.partner_ref, f32[64,64]{1,0:T(8,128)S(1)} %shard_map.72.gram_one, f32[64,64]{1,0:T(8,128)S(1)} %collective-permute-done.11.gram_two, bf16[16,1792]{1,0:T(8,128)(2,1)S(1)} %collective-permute-done.8.refs_0_, ...), custom_call_target="tpu_custom_call" | custom-call | tf_op jit(solution)/shard_map/pallas_call | solution.py:272
  (1 shorter events, 0.0 us)
Async XLA Ops:
  2.2 7.1 %collective-permute-start = (bf16[128,2304]{1,0:T(8,128)(2,1)S(1)}, bf16[128,2304]{1,0:T(8,128)(2,1)S(1)}, u32[]{:S(2)}, u32[]{:S(2)}) collective-permute-start(bf16[128,2304]{1,0:T(8,128)(2,1)S(1)} %get-tuple-element.17), channel_id=1, source_target_pairs={{0,1},{1,0},{2,3},{3,2},{4,5},{5,4},{6,7},{7,6},{8,9},{9,8},{10,11... | collective-permute-start | bytes 1769480 | tf_op jit(solution)/shard_map/ppermute | solution.py:206
  2.7 5.3 %collective-permute-start.1 = (bf16[128,256]{1,0:T(8,128)(2,1)S(1)}, bf16[128,256]{1,0:T(8,128)(2,1)S(1)}, u32[]{:S(2)}, u32[]{:S(2)}) collective-permute-start(bf16[128,256]{1,0:T(8,128)(2,1)S(1)} %get-tuple-element.16.k_own), channel_id=1, source_target_pairs={{0,2},{1,3},{2,0},{3,1},{4,6},{5,7},{6,4},{7,5},{8,10},{9,11},{10,... | collective-permute-start | bytes 196616 | tf_op jit(solution)/shard_map/ppermute | solution.py:206
  5.3 4.0 %collective-permute-start.2 = (bf16[128,256]{1,0:T(8,128)(2,1)S(1)}, bf16[128,256]{1,0:T(8,128)(2,1)S(1)}, u32[]{:S(2)}, u32[]{:S(2)}) collective-permute-start(bf16[128,256]{1,0:T(8,128)(2,1)S(1)} %get-tuple-element.18), channel_id=1, source_target_pairs={{0,3},{1,2},{2,1},{3,0},{4,7},{5,6},{6,5},{7,4},{8,11},{9,10},{10,... | collective-permute-start | bytes 196616 | tf_op jit(solution)/shard_map/ppermute | solution.py:206
  5.4 6.3 %collective-permute-start.3 = (bf16[128,256]{1,0:T(8,128)(2,1)S(1)}, bf16[128,256]{1,0:T(8,128)(2,1)S(1)}, u32[]{:S(2)}, u32[]{:S(2)}) collective-permute-start(bf16[128,256]{1,0:T(8,128)(2,1)S(1)} %get-tuple-element.20.v_own), channel_id=1, source_target_pairs={{0,2},{1,3},{2,0},{3,1},{4,6},{5,7},{6,4},{7,5},{8,10},{9,11},{10,... | collective-permute-start | bytes 196616 | tf_op jit(solution)/shard_map/ppermute | solution.py:206
  7.1 5.0 %collective-permute-start.4 = (bf16[128,256]{1,0:T(8,128)(2,1)S(1)}, bf16[128,256]{1,0:T(8,128)(2,1)S(1)}, u32[]{:S(2)}, u32[]{:S(2)}) collective-permute-start(bf16[128,256]{1,0:T(8,128)(2,1)S(1)} %get-tuple-element.21), channel_id=1, source_target_pairs={{0,3},{1,2},{2,1},{3,0},{4,7},{5,6},{6,5},{7,4},{8,11},{9,10},{10,... | collective-permute-start | bytes 196616 | tf_op jit(solution)/shard_map/ppermute | solution.py:206
  12.4 4.8 %collective-permute-start.5 = (bf16[8,1792]{1,0:T(8,128)(2,1)S(1)}, bf16[8,1792]{1,0:T(8,128)(2,1)S(1)}, u32[]{:S(2)}, u32[]{:S(2)}) collective-permute-start(bf16[8,1792]{1,0:T(8,128)(2,1)S(1)} %get-tuple-element.22), channel_id=1, source_target_pairs={{0,6},{1,7},{2,4},{3,5},{4,2},{5,3},{6,0},{7,1},{8,14},{9,15},{10,... | collective-permute-start | bytes 86024 | tf_op jit(solution)/shard_map/ppermute | solution.py:206
  14.8 3.9 %collective-permute-start.6 = (bf16[8,1792]{1,0:T(8,128)(2,1)S(1)}, bf16[8,1792]{1,0:T(8,128)(2,1)S(1)}, u32[]{:S(2)}, u32[]{:S(2)}) collective-permute-start(bf16[8,1792]{1,0:T(8,128)(2,1)S(1)} %get-tuple-element.22), channel_id=1, source_target_pairs={{0,2},{1,3},{2,0},{3,1},{4,6},{5,7},{6,4},{7,5},{8,10},{9,11},{10,... | collective-permute-start | bytes 86024 | tf_op jit(solution)/shard_map/ppermute | solution.py:206
  15.4 3.9 %collective-permute-start.7 = (bf16[8,1792]{1,0:T(8,128)(2,1)S(1)}, bf16[8,1792]{1,0:T(8,128)(2,1)S(1)}, u32[]{:S(2)}, u32[]{:S(2)}) collective-permute-start(bf16[8,1792]{1,0:T(8,128)(2,1)S(1)} %get-tuple-element.22), channel_id=1, source_target_pairs={{0,4},{4,0},{8,12},{12,8},{16,20},{20,16},{24,28},{28,24},{1,5},{5... | collective-permute-start | bytes 86024 | tf_op jit(solution)/shard_map/ppermute | solution.py:206
  19.3 6.1 %collective-permute-start.10 = (bf16[16,1792]{1,0:T(8,128)(2,1)S(1)}, bf16[16,1792]{1,0:T(8,128)(2,1)S(1)}, u32[]{:S(2)}, u32[]{:S(2)}) collective-permute-start(bf16[16,1792]{1,0:T(8,128)(2,1)S(1)} %shard_map.71.refs_3_), channel_id=1, source_target_pairs={{0,24},{4,28},{8,16},{12,20},{16,8},{20,12},{24,0},{28,4},{1,25},{... | collective-permute-start | bytes 172040 | tf_op jit(solution)/shard_map/ppermute | solution.py:206
  23.0 5.1 %collective-permute-start.8 = (bf16[16,1792]{1,0:T(8,128)(2,1)S(1)}, bf16[16,1792]{1,0:T(8,128)(2,1)S(1)}, u32[]{:S(2)}, u32[]{:S(2)}) collective-permute-start(bf16[16,1792]{1,0:T(8,128)(2,1)S(1)} %shard_map.71.refs_3_), channel_id=1, source_target_pairs={{0,16},{4,20},{8,24},{12,28},{16,0},{20,4},{24,8},{28,12},{1,17},{... | collective-permute-start | bytes 172040 | tf_op jit(solution)/shard_map/ppermute | solution.py:206
  23.0 5.1 %collective-permute-start.9 = (bf16[16,1792]{1,0:T(8,128)(2,1)S(1)}, bf16[16,1792]{1,0:T(8,128)(2,1)S(1)}, u32[]{:S(2)}, u32[]{:S(2)}) collective-permute-start(bf16[16,1792]{1,0:T(8,128)(2,1)S(1)} %shard_map.71.refs_3_), channel_id=1, source_target_pairs={{0,8},{4,12},{8,0},{12,4},{16,24},{20,28},{24,16},{28,20},{1,9},{5... | collective-permute-start | bytes 172040 | tf_op jit(solution)/shard_map/ppermute | solution.py:206
  28.3 1.3 %collective-permute-start.11 = (f32[64,64]{1,0:T(8,128)S(1)}, f32[64,64]{1,0:T(8,128)S(1)}, u32[]{:S(2)}, u32[]{:S(2)}) collective-permute-start(f32[64,64]{1,0:T(8,128)S(1)} %shard_map.72.gram_one), channel_id=1, source_target_pairs={{0,1},{1,0},{2,3},{3,2},{4,5},{5,4},{6,7},{7,6},{8,9},{9,8},{10,11... | collective-permute-start | bytes 49160 | tf_op jit(solution)/shard_map/ppermute | solution.py:206

commit v9 on v7

--- a/solution.py
+++ b/solution.py
@@ -100,28 +100,30 @@
 def scores_kernel(bias_ref, q_own, q_near, k_own, near, k_far, last_one, last_two, sums_ref):
     core = lax.rem(lax.axis_index("sp"), PAIR)
     scale = HEAD_SIZE ** (-0.5) * math.log2(math.e)
+    span = k_own.shape[0]
     for p, last in enumerate((last_one, last_two)):
         here = slice(p * HEAD_SIZE, (p + 1) * HEAD_SIZE)
         group = PAIR * p + core
         there = pl.ds(pl.multiple_of(group * HEAD_SIZE, HEAD_SIZE), HEAD_SIZE)
         key_head = jnp.concatenate([k_own[:, here], near[:, here], k_far[:, there], last[...]], axis=0)
-        for h in range(HEAD_GROUP):
-            place = (p * HEAD_GROUP + h) * HEAD_SIZE
-            beside = pl.multiple_of(group * GROUP_WIDTH + h * HEAD_SIZE, HEAD_SIZE)
-            total = None
-            for t, query in enumerate((q_own[:, place : place + HEAD_SIZE], q_near[:, pl.ds(beside, HEAD_SIZE)])):
-                rows = query.shape[0]
+
+        def one_head(h, carry):
+            place = pl.ds(pl.multiple_of((p * HEAD_GROUP + h) * HEAD_SIZE, HEAD_SIZE), HEAD_SIZE)
+            beside = pl.ds(pl.multiple_of((group * HEAD_GROUP + h) * HEAD_SIZE, HEAD_SIZE), HEAD_SIZE)
+            total = 0.0
+            for t, query in enumerate((q_own[:, place], q_near[:, beside])):
                 scores = lax.dot_general(
                     query, key_head, (((1,), (1,)), ((), ())), preferred_element_type=jnp.float32
                 )
-                scores = scores + bias_ref[t * rows : (t + 1) * rows]
+                scores = scores + bias_ref[t * span : (t + 1) * span]
                 largest = jnp.max(scores, axis=1, keepdims=True)
                 weights = jnp.exp2((scores - largest) * scale)
                 probs = weights * (1.0 / jnp.sum(weights, axis=1, keepdims=True))
-                summed = jnp.sum(probs, axis=0, keepdims=True)
-                total = summed if total is None else total + summed
-            row = p * HEAD_GROUP + h
-            sums_ref[row : row + 1] = total
+                total = total + jnp.sum(probs, axis=0, keepdims=True)
+            sums_ref[p * HEAD_GROUP + h] = total
+            return carry
+
+        lax.fori_loop(0, HEAD_GROUP, one_head, 0)
 
 
 def values_kernel(sums_ref, doc_ref, v_own, near, v_far, v_last, out_ref, sent_ref):
@@ -133,7 +135,7 @@
             [v_own[:, here], near[:, beside : beside + HEAD_SIZE], v_far[:, here], v_last[:, here]], axis=0
         )
         rows = range(p * HEAD_GROUP, (p + 1) * HEAD_GROUP)
-        spread = jnp.concatenate([sums_ref[row : row + 1] * doc_ref[...] for row in rows], axis=0)
+        spread = jnp.concatenate([sums_ref[row] * doc_ref[...] for row in rows], axis=0)
         high = spread.astype(jnp.bfloat16)
         low = (spread - high.astype(jnp.float32)).astype(jnp.bfloat16)
         summed = jnp.dot(high, value_head, preferred_element_type=jnp.float32) + jnp.dot(
@@ -175,15 +177,10 @@
     inverse_column = lax.rsqrt(jnp.sum(square, axis=1, keepdims=True) + 1e-6)
     inverse_row = lax.rsqrt(jnp.sum(square, axis=0, keepdims=True) + 1e-6)
     cosine = gram * inverse_column * inverse_row
-    logits = jnp.where(diagonal, -jnp.inf, cosine * (1.0 / SOFTMAX_TEMP))
-    own = logits[:DOCS]
-    largest = jnp.max(own, axis=1, keepdims=True)
-    weights = jnp.exp(own - largest)
-    probs = weights / jnp.sum(weights, axis=1, keepdims=True)
-    largest_row = jnp.max(logits, axis=0, keepdims=True)
-    total_row = jnp.sum(jnp.exp(logits - largest_row), axis=0, keepdims=True)
-    probs = probs + jnp.exp(own - largest_row) / total_row
-    both = probs - partner_ref[...]
+    weights = jnp.where(diagonal, 0.0, jnp.exp(cosine * (1.0 / SOFTMAX_TEMP)))
+    own = weights[:DOCS]
+    total = 1.0 / jnp.sum(own, axis=1, keepdims=True) + 1.0 / jnp.sum(weights, axis=0, keepdims=True)
+    both = own * total - partner_ref[...]
     along = jnp.sum(both * cosine[:DOCS], axis=1, keepdims=True) * (1.0 / SOFTMAX_TEMP)
     weighted = both * inverse_row * (1.0 / SOFTMAX_TEMP)
     high = weighted.astype(jnp.bfloat16)
@@ -265,7 +262,7 @@
     ]
     sums = call(
         scores_kernel,
-        struct((PAIR * HEAD_GROUP, parts * tokens), f32),
+        struct((PAIR * HEAD_GROUP, 1, parts * tokens), f32),
         [VMEM] * 8,
         flops=tokens * features * tokens * parts,
         moved=2 * queries.size + 4 * parts * keys.size,

time: 31 us -> 34.2 us (1.10)
  Pallas kernels: 5.44 us -> 8.67 us
    pallas_call x1, Pallas kernels: 2.59 us -> 5.9 us  [per_device(): call(scores_kernel, struct((PAIR * HEAD_GROUP, 1, parts * tokens), f32),...]
  transfers between devices with their start and end apart: 14 -> 14, of which waited for: 9 -> 9; matrix products, arithmetic and copies ran while one was open for 0% -> 0% of each run, Pallas kernels for 13% -> 21%
where the time goes in v9:
time: 34.2 us; the launch traced here: 34 us
  starting transfers between devices  14 us (41%)
  waiting for transfers between devices  10.7 us (31%)
  Pallas kernels  8.67 us (25%)
  between operations  0.71 us (2%)
    ppermute x14, starting transfers between devices, swap(): return lax.ppermute(block, axis, [(s, s ^ distance) for s in range(size)])  14 us
    ppermute x14, waiting for transfers between devices, swap(): return lax.ppermute(block, axis, [(s, s ^ distance) for s in range(size)])  10.7 us
    pallas_call x1, Pallas kernels, per_device(): call(scores_kernel, struct((PAIR * HEAD_GROUP, 1, parts * tokens), f32),...  5.9 us
    pallas_call x1, Pallas kernels, per_device(): call(functools.partial(plan_kernel, parts), (struct((tokens, width), bf16...  1.37 us
    pallas_call x1, Pallas kernels, per_device(): call(grads_kernel, (struct((DOCS, features // parts), bf16), struct((DOCS...  0.94 us
  transfers between devices with their start and end apart: 14, of which 9 were waited for; matrix products, arithmetic and copies ran while one was open for 0% of the time, Pallas kernels for 21%

profile of v9, /device:TPU:0, one launch (start us, length us, event | category | flops | bytes accessed | tf_op | source)
XLA Modules:
  0.0 34.0 jit_solution(4448601778173371615)
XLA Ops:
  0.6 0.5 %collective-permute-start = (bf16[128,3584]{1,0:T(8,128)(2,1)}, bf16[128,3584]{1,0:T(8,128)(2,1)S(1)}, u32[]{:S(2)}, u32[]{:S(2)}) collective-permute-start(bf16[128,3584]{1,0:T(8,128)(2,1)} %q_hbm.1), channel_id=1, source_target_pairs={{0,1},{1,0},{2,3},{3,2},{4,5},{5,4},{6,7},{7,6},{8,9},{9,8},{10,11... | collective-permute-start | bytes 2752520 | tf_op jit(solution)/shard_map/ppermute | solution.py:212
  1.1 2.6 %collective-permute-start.2 = (bf16[128,512]{1,0:T(8,128)(2,1)}, bf16[128,512]{1,0:T(8,128)(2,1)S(1)}, u32[]{:S(2)}, u32[]{:S(2)}) collective-permute-start(bf16[128,512]{1,0:T(8,128)(2,1)} %k_hbm.1), channel_id=1, source_target_pairs={{0,2},{1,3},{2,0},{3,1},{4,6},{5,7},{6,4},{7,5},{8,10},{9,11},{10,... | collective-permute-start | bytes 393224 | tf_op jit(solution)/shard_map/ppermute | solution.py:212
  3.7 1.4 %shard_map.68 = (bf16[128,1792]{1,0:T(8,128)(2,1)S(1)}, bf16[128,256]{1,0:T(8,128)(2,1)S(1)}, bf16[128,256]{1,0:T(8,128)(2,1)S(1)}, bf16[128,256]{1,0:T(8,128)(2...) custom-call(s32[1,8]{1,0:T(1,128)} %lengths_hbm.1, ...), custom_call_target="tpu_custom_call" | custom-call | bytes 1179648 | tf_op jit(solution)/shard_map/pallas_call | solution.py:237
  5.1 0.2 collective-permute-start.1
  5.3 0.3 collective-permute-start.5
  5.6 1.4 %collective-permute-start.6 = (bf16[128,256]{1,0:T(8,128)(2,1)S(1)}, bf16[128,256]{1,0:T(8,128)(2,1)S(1)}, u32[]{:S(2)}, u32[]{:S(2)}) collective-permute-start(bf16[128,256]{1,0:T(8,128)(2,1)S(1)} %get-tuple-element.23), channel_id=1, source_target_pairs={{0,3},{1,2},{2,1},{3,0},{4,7},{5,6},{6,5},{7,4},{8,11},{9,10},{10,... | collective-permute-start | bytes 196616 | tf_op jit(solution)/shard_map/ppermute | solution.py:212
  7.0 1.0 %collective-permute-done.2.k_ref.k_far = bf16[128,512]{1,0:T(8,128)(2,1)S(1)} collective-permute-done((bf16[128,512]{1,0:T(8,128)(2,1)}, bf16[128,512]{1,0:T(8,128)(2,1)S(1)}, u32[]{:S(2)}, u32[]{:S(2)}) %collective-permute-start.2) | collective-permute-done | bytes 131104 | tf_op jit(solution)/shard_map/ppermute | solution.py:212
  8.0 0.1 collective-permute-start.3
  8.1 0.0 collective-permute-done.1.near
  8.1 0.5 %collective-permute-start.4 = (bf16[128,128]{1,0:T(8,128)(2,1)S(1)}, bf16[128,128]{1,0:T(8,128)(2,1)S(1)}, u32[]{:S(2)}, u32[]{:S(2)}) collective-permute-start(bf16[128,128]{1,0:T(8,128)(2,1)S(1)} %get-tuple-element.20), channel_id=1, source_target_pairs={{0,1},{1,0},{2,3},{3,2},{4,5},{5,4},{6,7},{7,6},{8,9},{9,8},{10,11... | collective-permute-start | bytes 98312 | tf_op jit(solution)/shard_map/ppermute | solution.py:212
  8.6 0.7 %collective-permute-done.3.last_one = bf16[128,128]{1,0:T(8,128)(2,1)S(1)} collective-permute-done((bf16[128,128]{1,0:T(8,128)(2,1)S(1)}, bf16[128,128]{1,0:T(8,128)(2,1)S(1)}, u32[]{:S(2)}, u32[]{:S(2)}) %collective-permute-start.3) | collective-permute-done | bytes 32800 | tf_op jit(solution)/shard_map/ppermute | solution.py:212
  9.3 0.2 collective-permute-done.4.last_two
  9.5 0.0 collective-permute-done.q_near
  9.5 5.9 %shard_map.70.sums_ref = f32[14,1,512]{2,1,0:T(1,128)S(1)} custom-call(f32[256,512]{1,0:T(8,128)S(1)} %get-tuple-element.15.bias_ref, bf16[128,1792]{1,0:T(8,128)(2,1)S(1)} %get-tuple-element.16.q_own, bf16[128,3584]{1,0:T(8,128)(2,1)S(1)} %collective-permute-done.q_near, bf16[128,256]{1,0:T(8,128)(2,1)S(1)} %get-tuple-element.17.k_own, ...), custom_call_target="tpu_custom_call" | custom-call | flops 234881024 | bytes 1966080 | tf_op jit(solution)/shard_map/pallas_call | solution.py:263
  15.4 0.0 collective-permute-done.5.v_far
  15.4 0.0 collective-permute-done.6.v_last
  15.4 0.2 shard_map.71
  15.6 3.2 %collective-permute-start.7 = (bf16[8,1792]{1,0:T(8,128)(2,1)S(1)}, bf16[8,1792]{1,0:T(8,128)(2,1)S(1)}, u32[]{:S(2)}, u32[]{:S(2)}) collective-permute-start(bf16[8,1792]{1,0:T(8,128)(2,1)S(1)} %get-tuple-element.24), channel_id=1, source_target_pairs={{0,6},{1,7},{2,4},{3,5},{4,2},{5,3},{6,0},{7,1},{8,14},{9,15},{10,... | collective-permute-start | bytes 86024 | tf_op jit(solution)/shard_map/ppermute | solution.py:212
  18.9 0.1 collective-permute-start.8
  19.0 0.6 %collective-permute-start.9 = (bf16[8,1792]{1,0:T(8,128)(2,1)S(1)}, bf16[8,1792]{1,0:T(8,128)(2,1)S(1)}, u32[]{:S(2)}, u32[]{:S(2)}) collective-permute-start(bf16[8,1792]{1,0:T(8,128)(2,1)S(1)} %get-tuple-element.24), channel_id=1, source_target_pairs={{0,4},{4,0},{8,12},{12,8},{16,20},{20,16},{24,28},{28,24},{1,5},{5... | collective-permute-start | bytes 86024 | tf_op jit(solution)/shard_map/ppermute | solution.py:212
  19.5 1.2 %collective-permute-done.7.corner_ref = bf16[8,1792]{1,0:T(8,128)(2,1)S(1)} collective-permute-done((bf16[8,1792]{1,0:T(8,128)(2,1)S(1)}, bf16[8,1792]{1,0:T(8,128)(2,1)S(1)}, u32[]{:S(2)}, u32[]{:S(2)}) %collective-permute-start.7) | collective-permute-done | bytes 28704 | tf_op jit(solution)/shard_map/ppermute | solution.py:212
  20.7 2.0 %collective-permute-done.8.far_ref.refs_5_ = bf16[8,1792]{1,0:T(8,128)(2,1)S(1)} collective-permute-done((bf16[8,1792]{1,0:T(8,128)(2,1)S(1)}, bf16[8,1792]{1,0:T(8,128)(2,1)S(1)}, u32[]{:S(2)}, u32[]{:S(2)}) %collective-permute-start.8) | collective-permute-done | bytes 28704 | tf_op jit(solution)/shard_map/ppermute | solution.py:212
  22.8 0.1 collective-permute-done.9.next_ref
  22.9 3.7 %collective-permute-start.10 = (bf16[16,1792]{1,0:T(8,128)(2,1)S(1)}, bf16[16,1792]{1,0:T(8,128)(2,1)S(1)}, u32[]{:S(2)}, u32[]{:S(2)}) collective-permute-start(bf16[16,1792]{1,0:T(8,128)(2,1)S(1)} %shard_map.72.refs_3_), channel_id=1, source_target_pairs={{0,24},{4,28},{8,16},{12,20},{16,8},{20,12},{24,0},{28,4},{1,25},{... | collective-permute-start | bytes 172040 | tf_op jit(solution)/shard_map/ppermute | solution.py:212
  26.5 0.8 %collective-permute-start.12 = (bf16[16,1792]{1,0:T(8,128)(2,1)S(1)}, bf16[16,1792]{1,0:T(8,128)(2,1)S(1)}, u32[]{:S(2)}, u32[]{:S(2)}) collective-permute-start(bf16[16,1792]{1,0:T(8,128)(2,1)S(1)} %shard_map.72.refs_3_), channel_id=1, source_target_pairs={{0,8},{4,12},{8,0},{12,4},{16,24},{20,28},{24,16},{28,20},{1,9},{5... | collective-permute-start | bytes 172040 | tf_op jit(solution)/shard_map/ppermute | solution.py:212
  27.3 1.6 %collective-permute-done.10.refs_0_ = bf16[16,1792]{1,0:T(8,128)(2,1)S(1)} collective-permute-done((bf16[16,1792]{1,0:T(8,128)(2,1)S(1)}, bf16[16,1792]{1,0:T(8,128)(2,1)S(1)}, u32[]{:S(2)}, u32[]{:S(2)}) %collective-permute-start.10) | collective-permute-done | bytes 57376 | tf_op jit(solution)/shard_map/ppermute | solution.py:212
  28.9 2.7 %collective-permute-done.11.refs_1_ = bf16[16,1792]{1,0:T(8,128)(2,1)S(1)} collective-permute-done((bf16[16,1792]{1,0:T(8,128)(2,1)S(1)}, bf16[16,1792]{1,0:T(8,128)(2,1)S(1)}, u32[]{:S(2)}, u32[]{:S(2)}) %collective-permute-start.11) | collective-permute-done | bytes 57376 | tf_op jit(solution)/shard_map/ppermute | solution.py:212
  31.6 0.0 collective-permute-done.12.refs_2_
  31.6 0.2 shard_map.73.gram_one
  31.8 0.1 collective-permute-start.13
  31.9 1.2 %collective-permute-done.13.gram_two = f32[64,64]{1,0:T(8,128)S(1)} collective-permute-done((f32[64,64]{1,0:T(8,128)S(1)}, f32[64,64]{1,0:T(8,128)S(1)}, u32[]{:S(2)}, u32[]{:S(2)}) %collective-permute-start.13) | collective-permute-done | bytes 16416 | tf_op jit(solution)/shard_map/ppermute | solution.py:212
  33.1 0.9 %shard_map.74 = (bf16[8,896]{1,0:T(8,128)(2,1)}, f32[8,896]{1,0:T(8,128)}) custom-call(f32[8,64]{1,0:T(8,128)S(1)} %get-tuple-element.14.partner_ref, f32[64,64]{1,0:T(8,128)S(1)} %shard_map.73.gram_one, f32[64,64]{1,0:T(8,128)S(1)} %collective-permute-done.13.gram_two, bf16[16,1792]{1,0:T(8,128)(2,1)S(1)} %collective-permute-done.10.refs_0_, ...), custom_call_target="tpu_custom_call" | custom-call | tf_op jit(solution)/shard_map/pallas_call | solution.py:279
  (3 shorter events, 0.0 us)
Async XLA Ops:
  0.6 8.8 %collective-permute-start = (bf16[128,3584]{1,0:T(8,128)(2,1)}, bf16[128,3584]{1,0:T(8,128)(2,1)S(1)}, u32[]{:S(2)}, u32[]{:S(2)}) collective-permute-start(bf16[128,3584]{1,0:T(8,128)(2,1)} %q_hbm.1), channel_id=1, source_target_pairs={{0,1},{1,0},{2,3},{3,2},{4,5},{5,4},{6,7},{7,6},{8,9},{9,8},{10,11... | collective-permute-start | bytes 2752520 | tf_op jit(solution)/shard_map/ppermute | solution.py:212
  1.1 6.9 %collective-permute-start.2 = (bf16[128,512]{1,0:T(8,128)(2,1)}, bf16[128,512]{1,0:T(8,128)(2,1)S(1)}, u32[]{:S(2)}, u32[]{:S(2)}) collective-permute-start(bf16[128,512]{1,0:T(8,128)(2,1)} %k_hbm.1), channel_id=1, source_target_pairs={{0,2},{1,3},{2,0},{3,1},{4,6},{5,7},{6,4},{7,5},{8,10},{9,11},{10,... | collective-permute-start | bytes 393224 | tf_op jit(solution)/shard_map/ppermute | solution.py:212
  5.1 3.0 %collective-permute-start.1 = (bf16[128,512]{1,0:T(8,128)(2,1)S(1)}, bf16[128,512]{1,0:T(8,128)(2,1)S(1)}, u32[]{:S(2)}, u32[]{:S(2)}) collective-permute-start(bf16[128,512]{1,0:T(8,128)(2,1)S(1)} %get-tuple-element.18), channel_id=1, source_target_pairs={{0,1},{1,0},{2,3},{3,2},{4,5},{5,4},{6,7},{7,6},{8,9},{9,8},{10,11... | collective-permute-start | bytes 393224 | tf_op jit(solution)/shard_map/ppermute | solution.py:212
  5.3 10.1 %collective-permute-start.5 = (bf16[128,256]{1,0:T(8,128)(2,1)S(1)}, bf16[128,256]{1,0:T(8,128)(2,1)S(1)}, u32[]{:S(2)}, u32[]{:S(2)}) collective-permute-start(bf16[128,256]{1,0:T(8,128)(2,1)S(1)} %get-tuple-element.22.v_own), channel_id=1, source_target_pairs={{0,2},{1,3},{2,0},{3,1},{4,6},{5,7},{6,4},{7,5},{8,10},{9,11},{10,... | collective-permute-start | bytes 196616 | tf_op jit(solution)/shard_map/ppermute | solution.py:212
  5.6 9.8 %collective-permute-start.6 = (bf16[128,256]{1,0:T(8,128)(2,1)S(1)}, bf16[128,256]{1,0:T(8,128)(2,1)S(1)}, u32[]{:S(2)}, u32[]{:S(2)}) collective-permute-start(bf16[128,256]{1,0:T(8,128)(2,1)S(1)} %get-tuple-element.23), channel_id=1, source_target_pairs={{0,3},{1,2},{2,1},{3,0},{4,7},{5,6},{6,5},{7,4},{8,11},{9,10},{10,... | collective-permute-start | bytes 196616 | tf_op jit(solution)/shard_map/ppermute | solution.py:212
  8.0 1.3 %collective-permute-start.3 = (bf16[128,128]{1,0:T(8,128)(2,1)S(1)}, bf16[128,128]{1,0:T(8,128)(2,1)S(1)}, u32[]{:S(2)}, u32[]{:S(2)}) collective-permute-start(bf16[128,128]{1,0:T(8,128)(2,1)S(1)} %get-tuple-element.19), channel_id=1, source_target_pairs={{0,1},{1,0},{2,3},{3,2},{4,5},{5,4},{6,7},{7,6},{8,9},{9,8},{10,11... | collective-permute-start | bytes 98312 | tf_op jit(solution)/shard_map/ppermute | solution.py:212
  8.1 1.4 %collective-permute-start.4 = (bf16[128,128]{1,0:T(8,128)(2,1)S(1)}, bf16[128,128]{1,0:T(8,128)(2,1)S(1)}, u32[]{:S(2)}, u32[]{:S(2)}) collective-permute-start(bf16[128,128]{1,0:T(8,128)(2,1)S(1)} %get-tuple-element.20), channel_id=1, source_target_pairs={{0,1},{1,0},{2,3},{3,2},{4,5},{5,4},{6,7},{7,6},{8,9},{9,8},{10,11... | collective-permute-start | bytes 98312 | tf_op jit(solution)/shard_map/ppermute | solution.py:212
  15.6 5.1 %collective-permute-start.7 = (bf16[8,1792]{1,0:T(8,128)(2,1)S(1)}, bf16[8,1792]{1,0:T(8,128)(2,1)S(1)}, u32[]{:S(2)}, u32[]{:S(2)}) collective-permute-start(bf16[8,1792]{1,0:T(8,128)(2,1)S(1)} %get-tuple-element.24), channel_id=1, source_target_pairs={{0,6},{1,7},{2,4},{3,5},{4,2},{5,3},{6,0},{7,1},{8,14},{9,15},{10,... | collective-permute-start | bytes 86024 | tf_op jit(solution)/shard_map/ppermute | solution.py:212
  18.9 3.9 %collective-permute-start.8 = (bf16[8,1792]{1,0:T(8,128)(2,1)S(1)}, bf16[8,1792]{1,0:T(8,128)(2,1)S(1)}, u32[]{:S(2)}, u32[]{:S(2)}) collective-permute-start(bf16[8,1792]{1,0:T(8,128)(2,1)S(1)} %get-tuple-element.24), channel_id=1, source_target_pairs={{0,2},{1,3},{2,0},{3,1},{4,6},{5,7},{6,4},{7,5},{8,10},{9,11},{10,... | collective-permute-start | bytes 86024 | tf_op jit(solution)/shard_map/ppermute | solution.py:212
  19.0 3.9 %collective-permute-start.9 = (bf16[8,1792]{1,0:T(8,128)(2,1)S(1)}, bf16[8,1792]{1,0:T(8,128)(2,1)S(1)}, u32[]{:S(2)}, u32[]{:S(2)}) collective-permute-start(bf16[8,1792]{1,0:T(8,128)(2,1)S(1)} %get-tuple-element.24), channel_id=1, source_target_pairs={{0,4},{4,0},{8,12},{12,8},{16,20},{20,16},{24,28},{28,24},{1,5},{5... | collective-permute-start | bytes 86024 | tf_op jit(solution)/shard_map/ppermute | solution.py:212
  22.9 6.1 %collective-permute-start.10 = (bf16[16,1792]{1,0:T(8,128)(2,1)S(1)}, bf16[16,1792]{1,0:T(8,128)(2,1)S(1)}, u32[]{:S(2)}, u32[]{:S(2)}) collective-permute-start(bf16[16,1792]{1,0:T(8,128)(2,1)S(1)} %shard_map.72.refs_3_), channel_id=1, source_target_pairs={{0,24},{4,28},{8,16},{12,20},{16,8},{20,12},{24,0},{28,4},{1,25},{... | collective-permute-start | bytes 172040 | tf_op jit(solution)/shard_map/ppermute | solution.py:212
  26.5 5.1 %collective-permute-start.11 = (bf16[16,1792]{1,0:T(8,128)(2,1)S(1)}, bf16[16,1792]{1,0:T(8,128)(2,1)S(1)}, u32[]{:S(2)}, u32[]{:S(2)}) collective-permute-start(bf16[16,1792]{1,0:T(8,128)(2,1)S(1)} %shard_map.72.refs_3_), channel_id=1, source_target_pairs={{0,16},{4,20},{8,24},{12,28},{16,0},{20,4},{24,8},{28,12},{1,17},{... | collective-permute-start | bytes 172040 | tf_op jit(solution)/shard_map/ppermute | solution.py:212
  26.5 5.1 %collective-permute-start.12 = (bf16[16,1792]{1,0:T(8,128)(2,1)S(1)}, bf16[16,1792]{1,0:T(8,128)(2,1)S(1)}, u32[]{:S(2)}, u32[]{:S(2)}) collective-permute-start(bf16[16,1792]{1,0:T(8,128)(2,1)S(1)} %shard_map.72.refs_3_), channel_id=1, source_target_pairs={{0,8},{4,12},{8,0},{12,4},{16,24},{20,28},{24,16},{28,20},{1,9},{5... | collective-permute-start | bytes 172040 | tf_op jit(solution)/shard_map/ppermute | solution.py:212
  31.8 1.3 %collective-permute-start.13 = (f32[64,64]{1,0:T(8,128)S(1)}, f32[64,64]{1,0:T(8,128)S(1)}, u32[]{:S(2)}, u32[]{:S(2)}) collective-permute-start(f32[64,64]{1,0:T(8,128)S(1)} %shard_map.73.gram_one), channel_id=1, source_target_pairs={{0,1},{1,0},{2,3},{3,2},{4,5},{5,4},{6,7},{7,6},{8,9},{9,8},{10,11... | collective-permute-start | bytes 49160 | tf_op jit(solution)/shard_map/ppermute | solution.py:212

commit v10 on v8

--- a/solution.py
+++ b/solution.py
@@ -88,7 +88,9 @@
     place = jnp.zeros(partner_ref.shape, jnp.int32)
     for d in range(DOCS):
         pair = pairs_ref[d]
-        place = jnp.where(own_row == d, ((pair // DOCS) ^ own) * DOCS + lax.rem(pair, DOCS), place)
+        far = (pair // DOCS) ^ own
+        block = PAIR * ((far & 1) + 2 * (far >> 2)) + ((far >> 1) & 1)
+        place = jnp.where(own_row == d, block * DOCS + lax.rem(pair, DOCS), place)
     partner_ref[...] = jnp.where(own_column == place, 2.0, 0.0)
     for copy in copies:
         copy.wait()
@@ -207,14 +209,14 @@
 
 
 def gather_pairs(block, axis, size):
-    have, blocks = PAIR, [block]
-    while have < size:
-        if have > PAIR:
+    strides, blocks = [1] + [1 << i for i in range(2, size.bit_length() - 1)], [block]
+    while strides:
+        if len(blocks) > 1:
             shape = (len(blocks) * block.shape[0], block.shape[1])
             block = call(join_kernel, jax.ShapeDtypeStruct(shape, block.dtype), [VMEM] * len(blocks))(*blocks)
-        radix = min(4, size // have)
-        blocks = [swap(block, axis, size, r * have) for r in (*range(radix - 2, 0, -1), radix - 1)] + [block]
-        have *= radix
+        low, high, strides = strides[0], sum(strides[1:2]), strides[2:]
+        distances = [low, high, low + high] if high else [low]
+        blocks = [swap(block, axis, size, r) for r in (*distances[-2::-1], distances[-1])] + [block]
     return blocks
 
 
@@ -263,9 +265,9 @@
     partial, rounded = call(
         values_kernel, (struct((DOCS, width), f32), struct((DOCS, width), bf16)), [VMEM] * 6
     )(sums, of_doc, value_own, near, value_far, value_last)
-    corner = swap(rounded, ("dp", "sp"), replicas * parts, parts + 2)
+    corner = swap(rounded, ("dp", "sp"), replicas * parts, 2 * parts + 2)
     far = swap(rounded, "sp", parts, 2)
-    beside = swap(rounded, "dp", replicas, 1)
+    beside = swap(rounded, "dp", replicas, 2)
     sent = call(pool_kernel, struct((PAIR * DOCS, width), bf16), [VMEM] * 4)(corner, far, beside, partial)
     blocks = gather_pairs(sent, "dp", replicas)
     gram = call(gram_kernel, struct((docs, docs), f32), [VMEM] * len(blocks))(*blocks)

time: 30.7 us -> 31.2 us (1.016)
  waiting for transfers between devices: 11.6 us -> 12.1 us
    ppermute x12, waiting for transfers between devices: 11.6 us -> 12.1 us  [swap(): return lax.ppermute(block, axis, [(s, s ^ distance) for s in range(size)])]
  transfers between devices with their start and end apart: 12 -> 12, of which waited for: 9 -> 9; matrix products, arithmetic and copies ran while one was open for 0% -> 0% of each run, Pallas kernels for 8% -> 7%
where the time goes in v10:
time: 31.2 us; the launch traced here: 31 us
  starting transfers between devices  13 us (42%)
  waiting for transfers between devices  12.1 us (39%)
  Pallas kernels  5.27 us (17%)
  between operations  0.69 us (2%)
    ppermute x12, starting transfers between devices, swap(): return lax.ppermute(block, axis, [(s, s ^ distance) for s in range(size)])  13 us
    ppermute x12, waiting for transfers between devices, swap(): return lax.ppermute(block, axis, [(s, s ^ distance) for s in range(size)])  12.1 us
    pallas_call x1, Pallas kernels, per_device(): call(scores_kernel, struct((PAIR * HEAD_GROUP, parts * tokens), f32), [VM...  2.3 us
    pallas_call x1, Pallas kernels, per_device(): call(functools.partial(plan_kernel, parts), (struct((tokens, width), bf16...  1.59 us
    pallas_call x1, Pallas kernels, per_device(): call(grads_kernel, (struct((DOCS, features // parts), bf16), struct((DOCS...  0.94 us
  transfers between devices with their start and end apart: 12, of which 9 were waited for; matrix products, arithmetic and copies ran while one was open for 0% of the time, Pallas kernels for 7%

profile of v10, /device:TPU:0, one launch (start us, length us, event | category | flops | bytes accessed | tf_op | source)
XLA Modules:
  0.0 31.0 jit_solution(7992309718568479462)
XLA Ops:
  0.6 1.6 %shard_map.68 = (bf16[128,1792]{1,0:T(8,128)(2,1)S(1)}, bf16[128,256]{1,0:T(8,128)(2,1)S(1)}, bf16[128,256]{1,0:T(8,128)(2,1)S(1)}, bf16[128,2304]{1,0:T(8,128)(...) custom-call(s32[1,8]{1,0:T(1,128)} %lengths_hbm.1, ...), custom_call_target="tpu_custom_call" | custom-call | bytes 1179648 | tf_op jit(solution)/shard_map/pallas_call | solution.py:231
  2.2 0.5 %collective-permute-start = (bf16[128,2304]{1,0:T(8,128)(2,1)S(1)}, bf16[128,2304]{1,0:T(8,128)(2,1)S(1)}, u32[]{:S(2)}, u32[]{:S(2)}) collective-permute-start(bf16[128,2304]{1,0:T(8,128)(2,1)S(1)} %get-tuple-element.17), channel_id=1, source_target_pairs={{0,1},{1,0},{2,3},{3,2},{4,5},{5,4},{6,7},{7,6},{8,9},{9,8},{10,11... | collective-permute-start | bytes 1769480 | tf_op jit(solution)/shard_map/ppermute | solution.py:208
  2.7 2.6 %collective-permute-start.1 = (bf16[128,256]{1,0:T(8,128)(2,1)S(1)}, bf16[128,256]{1,0:T(8,128)(2,1)S(1)}, u32[]{:S(2)}, u32[]{:S(2)}) collective-permute-start(bf16[128,256]{1,0:T(8,128)(2,1)S(1)} %get-tuple-element.16.k_own), channel_id=1, source_target_pairs={{0,2},{1,3},{2,0},{3,1},{4,6},{5,7},{6,4},{7,5},{8,10},{9,11},{10,... | collective-permute-start | bytes 196616 | tf_op jit(solution)/shard_map/ppermute | solution.py:208
  5.3 0.1 collective-permute-start.2
  5.4 1.7 %collective-permute-start.3 = (bf16[128,256]{1,0:T(8,128)(2,1)S(1)}, bf16[128,256]{1,0:T(8,128)(2,1)S(1)}, u32[]{:S(2)}, u32[]{:S(2)}) collective-permute-start(bf16[128,256]{1,0:T(8,128)(2,1)S(1)} %get-tuple-element.20.v_own), channel_id=1, source_target_pairs={{0,2},{1,3},{2,0},{3,1},{4,6},{5,7},{6,4},{7,5},{8,10},{9,11},{10,... | collective-permute-start | bytes 196616 | tf_op jit(solution)/shard_map/ppermute | solution.py:208
  7.1 0.0 collective-permute-start.4
  7.1 0.9 %collective-permute-done.1.k_far = bf16[128,256]{1,0:T(8,128)(2,1)S(1)} collective-permute-done((bf16[128,256]{1,0:T(8,128)(2,1)S(1)}, bf16[128,256]{1,0:T(8,128)(2,1)S(1)}, u32[]{:S(2)}, u32[]{:S(2)}) %collective-permute-start.1) | collective-permute-done | bytes 65568 | tf_op jit(solution)/shard_map/ppermute | solution.py:208
  8.0 1.4 %collective-permute-done.2.k_last = bf16[128,256]{1,0:T(8,128)(2,1)S(1)} collective-permute-done((bf16[128,256]{1,0:T(8,128)(2,1)S(1)}, bf16[128,256]{1,0:T(8,128)(2,1)S(1)}, u32[]{:S(2)}, u32[]{:S(2)}) %collective-permute-start.2) | collective-permute-done | bytes 65568 | tf_op jit(solution)/shard_map/ppermute | solution.py:208
  9.4 0.0 collective-permute-done.near
  9.4 2.3 %shard_map.69.sums_ref = f32[14,512]{1,0:T(8,128)S(1)} custom-call(f32[256,512]{1,0:T(8,128)S(1)} %get-tuple-element.14.bias_ref, bf16[128,1792]{1,0:T(8,128)(2,1)S(1)} %get-tuple-element.15.q_own, bf16[128,256]{1,0:T(8,128)(2,1)S(1)} %get-tuple-element.16.k_own, bf16[128,2304]{1,0:T(8,128)(2,1)S(1)} %collective-permute-done.near, ...), custom_call_target="tpu_custom_call" | custom-call | flops 234881024 | bytes 1966080 | tf_op jit(solution)/shard_map/pallas_call | solution.py:258
  11.7 0.0 collective-permute-done.3.v_far
  11.7 0.5 %collective-permute-done.4.v_last = bf16[128,256]{1,0:T(8,128)(2,1)S(1)} collective-permute-done((bf16[128,256]{1,0:T(8,128)(2,1)S(1)}, bf16[128,256]{1,0:T(8,128)(2,1)S(1)}, u32[]{:S(2)}, u32[]{:S(2)}) %collective-permute-start.4) | collective-permute-done | bytes 65568 | tf_op jit(solution)/shard_map/ppermute | solution.py:208
  12.2 0.2 shard_map.70
  12.4 2.4 %collective-permute-start.5 = (bf16[8,1792]{1,0:T(8,128)(2,1)S(1)}, bf16[8,1792]{1,0:T(8,128)(2,1)S(1)}, u32[]{:S(2)}, u32[]{:S(2)}) collective-permute-start(bf16[8,1792]{1,0:T(8,128)(2,1)S(1)} %get-tuple-element.22), channel_id=1, source_target_pairs={{0,10},{1,11},{2,8},{3,9},{4,14},{5,15},{6,12},{7,13},{8,2},{9,3},... | collective-permute-start | bytes 86024 | tf_op jit(solution)/shard_map/ppermute | solution.py:208
  14.8 0.7 %collective-permute-start.6 = (bf16[8,1792]{1,0:T(8,128)(2,1)S(1)}, bf16[8,1792]{1,0:T(8,128)(2,1)S(1)}, u32[]{:S(2)}, u32[]{:S(2)}) collective-permute-start(bf16[8,1792]{1,0:T(8,128)(2,1)S(1)} %get-tuple-element.22), channel_id=1, source_target_pairs={{0,2},{1,3},{2,0},{3,1},{4,6},{5,7},{6,4},{7,5},{8,10},{9,11},{10,... | collective-permute-start | bytes 86024 | tf_op jit(solution)/shard_map/ppermute | solution.py:208
  15.5 0.4 %collective-permute-start.7 = (bf16[8,1792]{1,0:T(8,128)(2,1)S(1)}, bf16[8,1792]{1,0:T(8,128)(2,1)S(1)}, u32[]{:S(2)}, u32[]{:S(2)}) collective-permute-start(bf16[8,1792]{1,0:T(8,128)(2,1)S(1)} %get-tuple-element.22), channel_id=1, source_target_pairs={{0,8},{4,12},{8,0},{12,4},{16,24},{20,28},{24,16},{28,20},{1,9},{5... | collective-permute-start | bytes 86024 | tf_op jit(solution)/shard_map/ppermute | solution.py:208
  15.9 1.3 %collective-permute-done.5.corner_ref = bf16[8,1792]{1,0:T(8,128)(2,1)S(1)} collective-permute-done((bf16[8,1792]{1,0:T(8,128)(2,1)S(1)}, bf16[8,1792]{1,0:T(8,128)(2,1)S(1)}, u32[]{:S(2)}, u32[]{:S(2)}) %collective-permute-start.5) | collective-permute-done | bytes 28704 | tf_op jit(solution)/shard_map/ppermute | solution.py:208
  17.2 1.5 %collective-permute-done.6.far_ref.refs_5_ = bf16[8,1792]{1,0:T(8,128)(2,1)S(1)} collective-permute-done((bf16[8,1792]{1,0:T(8,128)(2,1)S(1)}, bf16[8,1792]{1,0:T(8,128)(2,1)S(1)}, u32[]{:S(2)}, u32[]{:S(2)}) %collective-permute-start.6) | collective-permute-done | bytes 28704 | tf_op jit(solution)/shard_map/ppermute | solution.py:208
  18.7 0.7 %collective-permute-done.7.next_ref = bf16[8,1792]{1,0:T(8,128)(2,1)S(1)} collective-permute-done((bf16[8,1792]{1,0:T(8,128)(2,1)S(1)}, bf16[8,1792]{1,0:T(8,128)(2,1)S(1)}, u32[]{:S(2)}, u32[]{:S(2)}) %collective-permute-start.7) | collective-permute-done | bytes 28704 | tf_op jit(solution)/shard_map/ppermute | solution.py:208
  19.4 3.6 %collective-permute-start.10 = (bf16[16,1792]{1,0:T(8,128)(2,1)S(1)}, bf16[16,1792]{1,0:T(8,128)(2,1)S(1)}, u32[]{:S(2)}, u32[]{:S(2)}) collective-permute-start(bf16[16,1792]{1,0:T(8,128)(2,1)S(1)} %shard_map.71.refs_3_), channel_id=1, source_target_pairs={{0,20},{4,16},{8,28},{12,24},{16,4},{20,0},{24,12},{28,8},{1,21},{... | collective-permute-start | bytes 172040 | tf_op jit(solution)/shard_map/ppermute | solution.py:208
  23.0 0.3 %collective-permute-start.8 = (bf16[16,1792]{1,0:T(8,128)(2,1)S(1)}, bf16[16,1792]{1,0:T(8,128)(2,1)S(1)}, u32[]{:S(2)}, u32[]{:S(2)}) collective-permute-start(bf16[16,1792]{1,0:T(8,128)(2,1)S(1)} %shard_map.71.refs_3_), channel_id=1, source_target_pairs={{0,16},{4,20},{8,24},{12,28},{16,0},{20,4},{24,8},{28,12},{1,17},{... | collective-permute-start | bytes 172040 | tf_op jit(solution)/shard_map/ppermute | solution.py:208
  23.3 0.5 %collective-permute-start.9 = (bf16[16,1792]{1,0:T(8,128)(2,1)S(1)}, bf16[16,1792]{1,0:T(8,128)(2,1)S(1)}, u32[]{:S(2)}, u32[]{:S(2)}) collective-permute-start(bf16[16,1792]{1,0:T(8,128)(2,1)S(1)} %shard_map.71.refs_3_), channel_id=1, source_target_pairs={{0,4},{4,0},{8,12},{12,8},{16,20},{20,16},{24,28},{28,24},{1,5},{5... | collective-permute-start | bytes 172040 | tf_op jit(solution)/shard_map/ppermute | solution.py:208
  23.8 3.2 %collective-permute-done.10.refs_2_ = bf16[16,1792]{1,0:T(8,128)(2,1)S(1)} collective-permute-done((bf16[16,1792]{1,0:T(8,128)(2,1)S(1)}, bf16[16,1792]{1,0:T(8,128)(2,1)S(1)}, u32[]{:S(2)}, u32[]{:S(2)}) %collective-permute-start.10) | collective-permute-done | bytes 57376 | tf_op jit(solution)/shard_map/ppermute | solution.py:208
  27.1 1.5 %collective-permute-done.8.refs_0_ = bf16[16,1792]{1,0:T(8,128)(2,1)S(1)} collective-permute-done((bf16[16,1792]{1,0:T(8,128)(2,1)S(1)}, bf16[16,1792]{1,0:T(8,128)(2,1)S(1)}, u32[]{:S(2)}, u32[]{:S(2)}) %collective-permute-start.8) | collective-permute-done | bytes 57376 | tf_op jit(solution)/shard_map/ppermute | solution.py:208
  28.6 0.0 collective-permute-done.9.refs_1_
  28.6 0.2 shard_map.72.gram_one
  28.8 0.1 collective-permute-start.11
  28.9 1.2 %collective-permute-done.11.gram_two = f32[64,64]{1,0:T(8,128)S(1)} collective-permute-done((f32[64,64]{1,0:T(8,128)S(1)}, f32[64,64]{1,0:T(8,128)S(1)}, u32[]{:S(2)}, u32[]{:S(2)}) %collective-permute-start.11) | collective-permute-done | bytes 16416 | tf_op jit(solution)/shard_map/ppermute | solution.py:208
  30.1 0.9 %shard_map.73 = (bf16[8,896]{1,0:T(8,128)(2,1)}, f32[8,896]{1,0:T(8,128)}) custom-call(f32[8,64]{1,0:T(8,128)S(1)} %get-tuple-element.13.partner_ref, f32[64,64]{1,0:T(8,128)S(1)} %shard_map.72.gram_one, f32[64,64]{1,0:T(8,128)S(1)} %collective-permute-done.11.gram_two, bf16[16,1792]{1,0:T(8,128)(2,1)S(1)} %collective-permute-done.8.refs_0_, ...), custom_call_target="tpu_custom_call" | custom-call | tf_op jit(solution)/shard_map/pallas_call | solution.py:274
  (1 shorter events, 0.0 us)
Async XLA Ops:
  2.2 7.1 %collective-permute-start = (bf16[128,2304]{1,0:T(8,128)(2,1)S(1)}, bf16[128,2304]{1,0:T(8,128)(2,1)S(1)}, u32[]{:S(2)}, u32[]{:S(2)}) collective-permute-start(bf16[128,2304]{1,0:T(8,128)(2,1)S(1)} %get-tuple-element.17), channel_id=1, source_target_pairs={{0,1},{1,0},{2,3},{3,2},{4,5},{5,4},{6,7},{7,6},{8,9},{9,8},{10,11... | collective-permute-start | bytes 1769480 | tf_op jit(solution)/shard_map/ppermute | solution.py:208
  2.7 5.3 %collective-permute-start.1 = (bf16[128,256]{1,0:T(8,128)(2,1)S(1)}, bf16[128,256]{1,0:T(8,128)(2,1)S(1)}, u32[]{:S(2)}, u32[]{:S(2)}) collective-permute-start(bf16[128,256]{1,0:T(8,128)(2,1)S(1)} %get-tuple-element.16.k_own), channel_id=1, source_target_pairs={{0,2},{1,3},{2,0},{3,1},{4,6},{5,7},{6,4},{7,5},{8,10},{9,11},{10,... | collective-permute-start | bytes 196616 | tf_op jit(solution)/shard_map/ppermute | solution.py:208
  5.3 4.0 %collective-permute-start.2 = (bf16[128,256]{1,0:T(8,128)(2,1)S(1)}, bf16[128,256]{1,0:T(8,128)(2,1)S(1)}, u32[]{:S(2)}, u32[]{:S(2)}) collective-permute-start(bf16[128,256]{1,0:T(8,128)(2,1)S(1)} %get-tuple-element.18), channel_id=1, source_target_pairs={{0,3},{1,2},{2,1},{3,0},{4,7},{5,6},{6,5},{7,4},{8,11},{9,10},{10,... | collective-permute-start | bytes 196616 | tf_op jit(solution)/shard_map/ppermute | solution.py:208
  5.4 6.3 %collective-permute-start.3 = (bf16[128,256]{1,0:T(8,128)(2,1)S(1)}, bf16[128,256]{1,0:T(8,128)(2,1)S(1)}, u32[]{:S(2)}, u32[]{:S(2)}) collective-permute-start(bf16[128,256]{1,0:T(8,128)(2,1)S(1)} %get-tuple-element.20.v_own), channel_id=1, source_target_pairs={{0,2},{1,3},{2,0},{3,1},{4,6},{5,7},{6,4},{7,5},{8,10},{9,11},{10,... | collective-permute-start | bytes 196616 | tf_op jit(solution)/shard_map/ppermute | solution.py:208
  7.1 5.0 %collective-permute-start.4 = (bf16[128,256]{1,0:T(8,128)(2,1)S(1)}, bf16[128,256]{1,0:T(8,128)(2,1)S(1)}, u32[]{:S(2)}, u32[]{:S(2)}) collective-permute-start(bf16[128,256]{1,0:T(8,128)(2,1)S(1)} %get-tuple-element.21), channel_id=1, source_target_pairs={{0,3},{1,2},{2,1},{3,0},{4,7},{5,6},{6,5},{7,4},{8,11},{9,10},{10,... | collective-permute-start | bytes 196616 | tf_op jit(solution)/shard_map/ppermute | solution.py:208
  12.4 4.8 %collective-permute-start.5 = (bf16[8,1792]{1,0:T(8,128)(2,1)S(1)}, bf16[8,1792]{1,0:T(8,128)(2,1)S(1)}, u32[]{:S(2)}, u32[]{:S(2)}) collective-permute-start(bf16[8,1792]{1,0:T(8,128)(2,1)S(1)} %get-tuple-element.22), channel_id=1, source_target_pairs={{0,10},{1,11},{2,8},{3,9},{4,14},{5,15},{6,12},{7,13},{8,2},{9,3},... | collective-permute-start | bytes 86024 | tf_op jit(solution)/shard_map/ppermute | solution.py:208
  14.8 3.9 %collective-permute-start.6 = (bf16[8,1792]{1,0:T(8,128)(2,1)S(1)}, bf16[8,1792]{1,0:T(8,128)(2,1)S(1)}, u32[]{:S(2)}, u32[]{:S(2)}) collective-permute-start(bf16[8,1792]{1,0:T(8,128)(2,1)S(1)} %get-tuple-element.22), channel_id=1, source_target_pairs={{0,2},{1,3},{2,0},{3,1},{4,6},{5,7},{6,4},{7,5},{8,10},{9,11},{10,... | collective-permute-start | bytes 86024 | tf_op jit(solution)/shard_map/ppermute | solution.py:208
  15.5 3.9 %collective-permute-start.7 = (bf16[8,1792]{1,0:T(8,128)(2,1)S(1)}, bf16[8,1792]{1,0:T(8,128)(2,1)S(1)}, u32[]{:S(2)}, u32[]{:S(2)}) collective-permute-start(bf16[8,1792]{1,0:T(8,128)(2,1)S(1)} %get-tuple-element.22), channel_id=1, source_target_pairs={{0,8},{4,12},{8,0},{12,4},{16,24},{20,28},{24,16},{28,20},{1,9},{5... | collective-permute-start | bytes 86024 | tf_op jit(solution)/shard_map/ppermute | solution.py:208
  19.4 7.7 %collective-permute-start.10 = (bf16[16,1792]{1,0:T(8,128)(2,1)S(1)}, bf16[16,1792]{1,0:T(8,128)(2,1)S(1)}, u32[]{:S(2)}, u32[]{:S(2)}) collective-permute-start(bf16[16,1792]{1,0:T(8,128)(2,1)S(1)} %shard_map.71.refs_3_), channel_id=1, source_target_pairs={{0,20},{4,16},{8,28},{12,24},{16,4},{20,0},{24,12},{28,8},{1,21},{... | collective-permute-start | bytes 172040 | tf_op jit(solution)/shard_map/ppermute | solution.py:208
  23.0 5.6 %collective-permute-start.8 = (bf16[16,1792]{1,0:T(8,128)(2,1)S(1)}, bf16[16,1792]{1,0:T(8,128)(2,1)S(1)}, u32[]{:S(2)}, u32[]{:S(2)}) collective-permute-start(bf16[16,1792]{1,0:T(8,128)(2,1)S(1)} %shard_map.71.refs_3_), channel_id=1, source_target_pairs={{0,16},{4,20},{8,24},{12,28},{16,0},{20,4},{24,8},{28,12},{1,17},{... | collective-permute-start | bytes 172040 | tf_op jit(solution)/shard_map/ppermute | solution.py:208
  23.3 5.2 %collective-permute-start.9 = (bf16[16,1792]{1,0:T(8,128)(2,1)S(1)}, bf16[16,1792]{1,0:T(8,128)(2,1)S(1)}, u32[]{:S(2)}, u32[]{:S(2)}) collective-permute-start(bf16[16,1792]{1,0:T(8,128)(2,1)S(1)} %shard_map.71.refs_3_), channel_id=1, source_target_pairs={{0,4},{4,0},{8,12},{12,8},{16,20},{20,16},{24,28},{28,24},{1,5},{5... | collective-permute-start | bytes 172040 | tf_op jit(solution)/shard_map/ppermute | solution.py:208
  28.8 1.3 %collective-permute-start.11 = (f32[64,64]{1,0:T(8,128)S(1)}, f32[64,64]{1,0:T(8,128)S(1)}, u32[]{:S(2)}, u32[]{:S(2)}) collective-permute-start(f32[64,64]{1,0:T(8,128)S(1)} %shard_map.72.gram_one), channel_id=1, source_target_pairs={{0,1},{1,0},{2,3},{3,2},{4,5},{5,4},{6,7},{7,6},{8,9},{9,8},{10,11... | collective-permute-start | bytes 49160 | tf_op jit(solution)/shard_map/ppermute | solution.py:208

commit v11 on v4

--- a/solution.py
+++ b/solution.py
@@ -36,18 +36,19 @@
     return ref.at[:, pl.ds(pl.multiple_of(group * width, HEAD_SIZE), width)]
 
 
-def cut_kernel(k_hbm, v_hbm, k_out, v_out, near_out, k_far_out, v_far_out, sem):
+def cut_kernel(q_hbm, k_hbm, v_hbm, k_out, v_out, near_out, k_far_out, v_far_out, sem):
     core = lax.rem(lax.axis_index("sp"), PAIR)
-    plans = [(k_hbm, 0, k_out, 0), (k_hbm, 1, k_far_out, 0), (k_hbm, 1, near_out, 0)]
-    plans += [(v_hbm, 1, near_out, PAIR), (v_hbm, 0, v_out, 0), (v_hbm, 1, v_far_out, 0)]
+    near_k, near_v = PAIR * GROUP_WIDTH, PAIR * (GROUP_WIDTH + HEAD_SIZE)
+    plans = [(k_hbm, 0, k_out, 0), (k_hbm, 1, k_far_out, 0), (q_hbm, 1, near_out, 0), (k_hbm, 1, near_out, near_k)]
+    plans += [(v_hbm, 1, near_out, near_v), (v_hbm, 0, v_out, 0), (v_hbm, 1, v_far_out, 0)]
     copies = []
     for source, other, target, start in plans:
+        width = source.shape[1] // KEY_VALUE_HEADS
         for p in range(PAIR):
-            first = (start + p) * HEAD_SIZE
             copies.append(
                 pltpu.make_async_copy(
                     group_columns(source, PAIR * p + (core ^ other)),
-                    target.at[:, first : first + HEAD_SIZE],
+                    target.at[:, start + p * width : start + (p + 1) * width],
                     sem.at[len(copies)],
                 )
             )
@@ -102,17 +103,19 @@
         copy.wait()
 
 
-def scores_kernel(bias_ref, q_own, q_near, k_own, near, k_far, k_last, sums_ref):
-    core = lax.rem(lax.axis_index("sp"), PAIR)
+def scores_kernel(bias_ref, q_own, k_own, near, k_far, k_last, sums_ref):
     scale = HEAD_SIZE ** (-0.5) * math.log2(math.e)
     for p in range(PAIR):
         here = slice(p * HEAD_SIZE, (p + 1) * HEAD_SIZE)
-        key_head = jnp.concatenate([k[:, here] for k in (k_own, near, k_far, k_last)], axis=0)
+        beside = PAIR * GROUP_WIDTH + p * HEAD_SIZE
+        key_head = jnp.concatenate(
+            [k_own[:, here], near[:, beside : beside + HEAD_SIZE], k_far[:, here], k_last[:, here]], axis=0
+        )
         for h in range(HEAD_GROUP):
             place = (p * HEAD_GROUP + h) * HEAD_SIZE
-            beside = pl.multiple_of((PAIR * p + core) * GROUP_WIDTH + h * HEAD_SIZE, HEAD_SIZE)
             total = None
-            for t, query in enumerate((q_own[:, place : place + HEAD_SIZE], q_near[:, pl.ds(beside, HEAD_SIZE)])):
+            for t, q_ref in enumerate((q_own, near)):
+                query = q_ref[:, place : place + HEAD_SIZE]
                 rows = query.shape[0]
                 scores = lax.dot_general(
                     query, key_head, (((1,), (1,)), ((), ())), preferred_element_type=jnp.float32
@@ -130,7 +133,7 @@
 def values_kernel(sums_ref, doc_ref, v_own, near, v_far, v_last, out_ref, sent_ref):
     for p in range(PAIR):
         here = slice(p * HEAD_SIZE, (p + 1) * HEAD_SIZE)
-        beside = (PAIR + p) * HEAD_SIZE
+        beside = PAIR * (GROUP_WIDTH + HEAD_SIZE) + p * HEAD_SIZE
         value_head = jnp.concatenate(
             [v_own[:, here], near[:, beside : beside + HEAD_SIZE], v_far[:, here], v_last[:, here]], axis=0
         )
@@ -153,7 +156,7 @@
 
 
 def in_order(refs):
-    return (refs[-1], refs[0], *refs[-2:0:-1])
+    return (refs[-1], *refs[-3::-1], refs[-2])
 
 
 def join_kernel(*refs):
@@ -224,7 +227,7 @@
             shape = (len(blocks) * block.shape[0], block.shape[1])
             block = call(join_kernel, jax.ShapeDtypeStruct(shape, block.dtype), [VMEM] * len(blocks))(*blocks)
         radix = min(4, size // have)
-        blocks = [swap(block, axis, size, r * have) for r in (1, *range(radix - 1, 1, -1))] + [block]
+        blocks = [swap(block, axis, size, r * have) for r in (*range(radix - 2, 0, -1), radix - 1)] + [block]
         have *= radix
     return blocks
 
@@ -237,16 +240,15 @@
     docs = DOCS * replicas
     f32, bf16 = jnp.float32, jnp.bfloat16
     struct = jax.ShapeDtypeStruct
-    query_near = swap(queries, "sp", parts, 1)
     near_cut = struct((tokens, kv_width), bf16)
     arguments = [pltpu.with_memory_space_constraint(x, pltpu.HBM) for x in (document_lengths, pair_ids, queries, keys, values)]
     key_own, value_own, near, key_send, value_send = call(
         cut_kernel,
-        (near_cut, near_cut, struct((tokens, 2 * kv_width), bf16), near_cut, near_cut),
-        [HBM] * 2,
-        [pltpu.SemaphoreType.DMA((6 * PAIR,))],
-        moved=8 * keys.size,
-    )(*arguments[3:])
+        (near_cut, near_cut, struct((tokens, width + 2 * kv_width), bf16), near_cut, near_cut),
+        [HBM] * 3,
+        [pltpu.SemaphoreType.DMA((7 * PAIR,))],
+        moved=tokens * features + 8 * keys.size,
+    )(*arguments[2:])
     query_own, bias, of_doc, partner = call(
         functools.partial(plan_kernel, parts),
         (
@@ -264,17 +266,17 @@
         moved=2 * tokens * features,
     )(*arguments[:3])
     near = swap(near, "sp", parts, 1)
+    value_far = swap(value_own, "sp", parts, 2)
+    value_last = swap(value_send, "sp", parts, 3)
     key_far = swap(key_own, "sp", parts, 2)
     key_last = swap(key_send, "sp", parts, 3)
-    value_far = swap(value_own, "sp", parts, 2)
-    value_last = swap(value_send, "sp", parts, 3)
     sums = call(
         scores_kernel,
         struct((PAIR * HEAD_GROUP, parts * tokens), f32),
-        [VMEM] * 7,
+        [VMEM] * 6,
         flops=tokens * features * tokens * parts,
         moved=2 * queries.size + 4 * parts * keys.size,
-    )(bias, query_own, query_near, key_own, near, key_far, key_last)
+    )(bias, query_own, key_own, near, key_far, key_last)
     partial, rounded = call(
         values_kernel, (struct((DOCS, width), f32), struct((DOCS, width), bf16)), [VMEM] * 6
     )(sums, of_doc, value_own, near, value_far, value_last)

time: 31 us -> 30.4 us (0.981)
  starting transfers between devices: 13.6 us -> 13 us
    ppermute x13 -> x12, starting transfers between devices: 13.6 us -> 13 us  [swap(): return lax.ppermute(block, axis, [(s, s ^ distance) for s in range(size)])]
    ppermute x13 -> x12, waiting for transfers between devices: 10.6 us -> 10.5 us  [swap(): return lax.ppermute(block, axis, [(s, s ^ distance) for s in range(size)])]
  transfers between devices with their start and end apart: 13 -> 12, of which waited for: 8 -> 8; matrix products, arithmetic and copies ran while one was open for 0% -> 0% of each run, Pallas kernels for 14% -> 11%
where the time goes in v11:
time: 30.4 us; the launch traced here: 30.3 us
  starting transfers between devices  13 us (43%)
  waiting for transfers between devices  10.5 us (35%)
  Pallas kernels  6.12 us (20%)
  between operations  0.7 us (2%)
    ppermute x12, starting transfers between devices, swap(): return lax.ppermute(block, axis, [(s, s ^ distance) for s in range(size)])  13 us
    ppermute x12, waiting for transfers between devices, swap(): return lax.ppermute(block, axis, [(s, s ^ distance) for s in range(size)])  10.5 us
    pallas_call x1, Pallas kernels, per_device(): call(scores_kernel, struct((PAIR * HEAD_GROUP, parts * tokens), f32), [VM...  2.3 us
    pallas_call x1, Pallas kernels, per_device(): call(cut_kernel, (near_cut, near_cut, struct((tokens, width + 2 * kv_widt...  1.28 us
    pallas_call x1, Pallas kernels, per_device(): call(functools.partial(plan_kernel, parts), (struct((tokens, width), bf16...  1.08 us
    pallas_call x1, Pallas kernels, per_device(): call(grads_kernel, (struct((DOCS, features // parts), bf16), struct((DOCS...  1.02 us
  transfers between devices with their start and end apart: 12, of which 8 were waited for; matrix products, arithmetic and copies ran while one was open for 0% of the time, Pallas kernels for 11%

profile of v11, /device:TPU:0, one launch (start us, length us, event | category | flops | bytes accessed | tf_op | source)
XLA Modules:
  0.0 30.3 jit_solution(9239539222522666558)
XLA Ops:
  0.6 1.3 %shard_map.69 = (bf16[128,256]{1,0:T(8,128)(2,1)S(1)}, bf16[128,256]{1,0:T(8,128)(2,1)S(1)}, bf16[128,2304]{1,0:T(8,128)(2,1)S(1)}, bf16[128,256]{1,0:T(8,128)(2,1)S(1)}, bf16[128,256]{1,0:T(8,128)(2,1)S(1)}) custom-call(bf16[128,3584]{1,0:T(8,128)(2,1)} %q_hbm.3, bf16[128,512]{1,0:T(8,128)(2,1)} %k_hbm.1, bf16[128,512]{1,0:T(8,128)(2,1)} %v_hbm.1), custom_call_target="tpu_custom_call" | custom-call | bytes 983040 | tf_op jit(solution)/shard_map/pallas_call | solution.py:245
  1.9 0.5 %collective-permute-start = (bf16[128,2304]{1,0:T(8,128)(2,1)S(1)}, bf16[128,2304]{1,0:T(8,128)(2,1)S(1)}, u32[]{:S(2)}, u32[]{:S(2)}) collective-permute-start(bf16[128,2304]{1,0:T(8,128)(2,1)S(1)} %get-tuple-element.17), channel_id=1, source_target_pairs={{0,1},{1,0},{2,3},{3,2},{4,5},{5,4},{6,7},{7,6},{8,9},{9,8},{10,11... | collective-permute-start | bytes 1769480 | tf_op jit(solution)/shard_map/ppermute | solution.py:220
  2.4 2.6 %collective-permute-start.1 = (bf16[128,256]{1,0:T(8,128)(2,1)S(1)}, bf16[128,256]{1,0:T(8,128)(2,1)S(1)}, u32[]{:S(2)}, u32[]{:S(2)}) collective-permute-start(bf16[128,256]{1,0:T(8,128)(2,1)S(1)} %get-tuple-element.16.k_own), channel_id=1, source_target_pairs={{0,2},{1,3},{2,0},{3,1},{4,6},{5,7},{6,4},{7,5},{8,10},{9,11},{10,... | collective-permute-start | bytes 196616 | tf_op jit(solution)/shard_map/ppermute | solution.py:220
  5.0 0.1 collective-permute-start.2
  5.1 1.7 %collective-permute-start.3 = (bf16[128,256]{1,0:T(8,128)(2,1)S(1)}, bf16[128,256]{1,0:T(8,128)(2,1)S(1)}, u32[]{:S(2)}, u32[]{:S(2)}) collective-permute-start(bf16[128,256]{1,0:T(8,128)(2,1)S(1)} %get-tuple-element.20.v_own), channel_id=1, source_target_pairs={{0,2},{1,3},{2,0},{3,1},{4,6},{5,7},{6,4},{7,5},{8,10},{9,11},{10,... | collective-permute-start | bytes 196616 | tf_op jit(solution)/shard_map/ppermute | solution.py:220
  6.8 0.0 collective-permute-start.4
  6.8 1.1 %shard_map.68 = (bf16[128,1792]{1,0:T(8,128)(2,1)S(1)}, f32[256,512]{1,0:T(8,128)S(1)}, f32[8,512]{1,0:T(8,128)S(1)}, f32[8,64]{1,0:T(8,128)S(1)}) custom-call(s32[1,8]{1,0:T(1,128)} %lengths_hbm.1, s32[8]{0:T(128)} %pairs_hbm.1, bf16[128,3584]{1,0:T(8,128)(2,1)} %q_hbm.3), custom_call_target="tpu_custom_call" | custom-call | bytes 917504 | tf_op jit(solution)/shard_map/pallas_call | solution.py:252
  7.9 0.0 collective-permute-done.1.k_far
  7.9 1.1 %collective-permute-done.2.k_last = bf16[128,256]{1,0:T(8,128)(2,1)S(1)} collective-permute-done((bf16[128,256]{1,0:T(8,128)(2,1)S(1)}, bf16[128,256]{1,0:T(8,128)(2,1)S(1)}, u32[]{:S(2)}, u32[]{:S(2)}) %collective-permute-start.2) | collective-permute-done | bytes 65568 | tf_op jit(solution)/shard_map/ppermute | solution.py:220
  9.0 0.0 collective-permute-done.near
  9.1 2.3 %shard_map.70.sums_ref = f32[14,512]{1,0:T(8,128)S(1)} custom-call(f32[256,512]{1,0:T(8,128)S(1)} %get-tuple-element.14.bias_ref, bf16[128,1792]{1,0:T(8,128)(2,1)S(1)} %get-tuple-element.15.q_own, bf16[128,256]{1,0:T(8,128)(2,1)S(1)} %get-tuple-element.16.k_own, bf16[128,2304]{1,0:T(8,128)(2,1)S(1)} %collective-permute-done.near, ...), custom_call_target="tpu_custom_call" | custom-call | flops 234881024 | bytes 1966080 | tf_op jit(solution)/shard_map/pallas_call | solution.py:273
  11.4 0.0 collective-permute-done.3.v_far
  11.4 0.5 %collective-permute-done.4.v_last = bf16[128,256]{1,0:T(8,128)(2,1)S(1)} collective-permute-done((bf16[128,256]{1,0:T(8,128)(2,1)S(1)}, bf16[128,256]{1,0:T(8,128)(2,1)S(1)}, u32[]{:S(2)}, u32[]{:S(2)}) %collective-permute-start.4) | collective-permute-done | bytes 65568 | tf_op jit(solution)/shard_map/ppermute | solution.py:220
  11.9 0.2 shard_map.71
  12.1 2.4 %collective-permute-start.5 = (bf16[8,1792]{1,0:T(8,128)(2,1)S(1)}, bf16[8,1792]{1,0:T(8,128)(2,1)S(1)}, u32[]{:S(2)}, u32[]{:S(2)}) collective-permute-start(bf16[8,1792]{1,0:T(8,128)(2,1)S(1)} %get-tuple-element.22), channel_id=1, source_target_pairs={{0,6},{1,7},{2,4},{3,5},{4,2},{5,3},{6,0},{7,1},{8,14},{9,15},{10,... | collective-permute-start | bytes 86024 | tf_op jit(solution)/shard_map/ppermute | solution.py:220
  14.4 0.7 %collective-permute-start.6 = (bf16[8,1792]{1,0:T(8,128)(2,1)S(1)}, bf16[8,1792]{1,0:T(8,128)(2,1)S(1)}, u32[]{:S(2)}, u32[]{:S(2)}) collective-permute-start(bf16[8,1792]{1,0:T(8,128)(2,1)S(1)} %get-tuple-element.22), channel_id=1, source_target_pairs={{0,2},{1,3},{2,0},{3,1},{4,6},{5,7},{6,4},{7,5},{8,10},{9,11},{10,... | collective-permute-start | bytes 86024 | tf_op jit(solution)/shard_map/ppermute | solution.py:220
  15.1 0.5 %collective-permute-start.7 = (bf16[8,1792]{1,0:T(8,128)(2,1)S(1)}, bf16[8,1792]{1,0:T(8,128)(2,1)S(1)}, u32[]{:S(2)}, u32[]{:S(2)}) collective-permute-start(bf16[8,1792]{1,0:T(8,128)(2,1)S(1)} %get-tuple-element.22), channel_id=1, source_target_pairs={{0,4},{4,0},{8,12},{12,8},{16,20},{20,16},{24,28},{28,24},{1,5},{5... | collective-permute-start | bytes 86024 | tf_op jit(solution)/shard_map/ppermute | solution.py:220
  15.6 1.3 %collective-permute-done.5.corner_ref = bf16[8,1792]{1,0:T(8,128)(2,1)S(1)} collective-permute-done((bf16[8,1792]{1,0:T(8,128)(2,1)S(1)}, bf16[8,1792]{1,0:T(8,128)(2,1)S(1)}, u32[]{:S(2)}, u32[]{:S(2)}) %collective-permute-start.5) | collective-permute-done | bytes 28704 | tf_op jit(solution)/shard_map/ppermute | solution.py:220
  16.9 1.4 %collective-permute-done.6.far_ref.refs_5_ = bf16[8,1792]{1,0:T(8,128)(2,1)S(1)} collective-permute-done((bf16[8,1792]{1,0:T(8,128)(2,1)S(1)}, bf16[8,1792]{1,0:T(8,128)(2,1)S(1)}, u32[]{:S(2)}, u32[]{:S(2)}) %collective-permute-start.6) | collective-permute-done | bytes 28704 | tf_op jit(solution)/shard_map/ppermute | solution.py:220
  18.3 0.7 %collective-permute-done.7.next_ref = bf16[8,1792]{1,0:T(8,128)(2,1)S(1)} collective-permute-done((bf16[8,1792]{1,0:T(8,128)(2,1)S(1)}, bf16[8,1792]{1,0:T(8,128)(2,1)S(1)}, u32[]{:S(2)}, u32[]{:S(2)}) %collective-permute-start.7) | collective-permute-done | bytes 28704 | tf_op jit(solution)/shard_map/ppermute | solution.py:220
  19.0 3.7 %collective-permute-start.10 = (bf16[16,1792]{1,0:T(8,128)(2,1)S(1)}, bf16[16,1792]{1,0:T(8,128)(2,1)S(1)}, u32[]{:S(2)}, u32[]{:S(2)}) collective-permute-start(bf16[16,1792]{1,0:T(8,128)(2,1)S(1)} %shard_map.72.refs_3_), channel_id=1, source_target_pairs={{0,24},{4,28},{8,16},{12,20},{16,8},{20,12},{24,0},{28,4},{1,25},{... | collective-permute-start | bytes 172040 | tf_op jit(solution)/shard_map/ppermute | solution.py:220
  22.7 0.0 collective-permute-start.8
  22.7 0.8 %collective-permute-start.9 = (bf16[16,1792]{1,0:T(8,128)(2,1)S(1)}, bf16[16,1792]{1,0:T(8,128)(2,1)S(1)}, u32[]{:S(2)}, u32[]{:S(2)}) collective-permute-start(bf16[16,1792]{1,0:T(8,128)(2,1)S(1)} %shard_map.72.refs_3_), channel_id=1, source_target_pairs={{0,8},{4,12},{8,0},{12,4},{16,24},{20,28},{24,16},{28,20},{1,9},{5... | collective-permute-start | bytes 172040 | tf_op jit(solution)/shard_map/ppermute | solution.py:220
  23.5 1.7 %collective-permute-done.10.refs_2_ = bf16[16,1792]{1,0:T(8,128)(2,1)S(1)} collective-permute-done((bf16[16,1792]{1,0:T(8,128)(2,1)S(1)}, bf16[16,1792]{1,0:T(8,128)(2,1)S(1)}, u32[]{:S(2)}, u32[]{:S(2)}) %collective-permute-start.10) | collective-permute-done | bytes 57376 | tf_op jit(solution)/shard_map/ppermute | solution.py:220
  25.2 2.6 %collective-permute-done.8.refs_0_ = bf16[16,1792]{1,0:T(8,128)(2,1)S(1)} collective-permute-done((bf16[16,1792]{1,0:T(8,128)(2,1)S(1)}, bf16[16,1792]{1,0:T(8,128)(2,1)S(1)}, u32[]{:S(2)}, u32[]{:S(2)}) %collective-permute-start.8) | collective-permute-done | bytes 57376 | tf_op jit(solution)/shard_map/ppermute | solution.py:220
  27.8 0.0 collective-permute-done.9.refs_1_
  27.8 0.2 shard_map.73.gram_one
  28.0 0.1 collective-permute-start.11
  28.1 1.2 %collective-permute-done.11.gram_two = f32[64,64]{1,0:T(8,128)S(1)} collective-permute-done((f32[64,64]{1,0:T(8,128)S(1)}, f32[64,64]{1,0:T(8,128)S(1)}, u32[]{:S(2)}, u32[]{:S(2)}) %collective-permute-start.11) | collective-permute-done | bytes 16416 | tf_op jit(solution)/shard_map/ppermute | solution.py:220
  29.3 1.0 %shard_map.74 = (bf16[8,896]{1,0:T(8,128)(2,1)}, f32[8,896]{1,0:T(8,128)}) custom-call(f32[8,64]{1,0:T(8,128)S(1)} %get-tuple-element.13.partner_ref, f32[64,64]{1,0:T(8,128)S(1)} %shard_map.73.gram_one, f32[64,64]{1,0:T(8,128)S(1)} %collective-permute-done.11.gram_two, bf16[16,1792]{1,0:T(8,128)(2,1)S(1)} %collective-permute-done.8.refs_0_, ...), custom_call_target="tpu_custom_call" | custom-call | tf_op jit(solution)/shard_map/pallas_call | solution.py:289
  (1 shorter events, 0.0 us)
Async XLA Ops:
  1.9 7.1 %collective-permute-start = (bf16[128,2304]{1,0:T(8,128)(2,1)S(1)}, bf16[128,2304]{1,0:T(8,128)(2,1)S(1)}, u32[]{:S(2)}, u32[]{:S(2)}) collective-permute-start(bf16[128,2304]{1,0:T(8,128)(2,1)S(1)} %get-tuple-element.17), channel_id=1, source_target_pairs={{0,1},{1,0},{2,3},{3,2},{4,5},{5,4},{6,7},{7,6},{8,9},{9,8},{10,11... | collective-permute-start | bytes 1769480 | tf_op jit(solution)/shard_map/ppermute | solution.py:220
  2.4 5.5 %collective-permute-start.1 = (bf16[128,256]{1,0:T(8,128)(2,1)S(1)}, bf16[128,256]{1,0:T(8,128)(2,1)S(1)}, u32[]{:S(2)}, u32[]{:S(2)}) collective-permute-start(bf16[128,256]{1,0:T(8,128)(2,1)S(1)} %get-tuple-element.16.k_own), channel_id=1, source_target_pairs={{0,2},{1,3},{2,0},{3,1},{4,6},{5,7},{6,4},{7,5},{8,10},{9,11},{10,... | collective-permute-start | bytes 196616 | tf_op jit(solution)/shard_map/ppermute | solution.py:220
  5.0 4.0 %collective-permute-start.2 = (bf16[128,256]{1,0:T(8,128)(2,1)S(1)}, bf16[128,256]{1,0:T(8,128)(2,1)S(1)}, u32[]{:S(2)}, u32[]{:S(2)}) collective-permute-start(bf16[128,256]{1,0:T(8,128)(2,1)S(1)} %get-tuple-element.18), channel_id=1, source_target_pairs={{0,3},{1,2},{2,1},{3,0},{4,7},{5,6},{6,5},{7,4},{8,11},{9,10},{10,... | collective-permute-start | bytes 196616 | tf_op jit(solution)/shard_map/ppermute | solution.py:220
  5.1 6.3 %collective-permute-start.3 = (bf16[128,256]{1,0:T(8,128)(2,1)S(1)}, bf16[128,256]{1,0:T(8,128)(2,1)S(1)}, u32[]{:S(2)}, u32[]{:S(2)}) collective-permute-start(bf16[128,256]{1,0:T(8,128)(2,1)S(1)} %get-tuple-element.20.v_own), channel_id=1, source_target_pairs={{0,2},{1,3},{2,0},{3,1},{4,6},{5,7},{6,4},{7,5},{8,10},{9,11},{10,... | collective-permute-start | bytes 196616 | tf_op jit(solution)/shard_map/ppermute | solution.py:220
  6.8 5.0 %collective-permute-start.4 = (bf16[128,256]{1,0:T(8,128)(2,1)S(1)}, bf16[128,256]{1,0:T(8,128)(2,1)S(1)}, u32[]{:S(2)}, u32[]{:S(2)}) collective-permute-start(bf16[128,256]{1,0:T(8,128)(2,1)S(1)} %get-tuple-element.21), channel_id=1, source_target_pairs={{0,3},{1,2},{2,1},{3,0},{4,7},{5,6},{6,5},{7,4},{8,11},{9,10},{10,... | collective-permute-start | bytes 196616 | tf_op jit(solution)/shard_map/ppermute | solution.py:220
  12.1 4.8 %collective-permute-start.5 = (bf16[8,1792]{1,0:T(8,128)(2,1)S(1)}, bf16[8,1792]{1,0:T(8,128)(2,1)S(1)}, u32[]{:S(2)}, u32[]{:S(2)}) collective-permute-start(bf16[8,1792]{1,0:T(8,128)(2,1)S(1)} %get-tuple-element.22), channel_id=1, source_target_pairs={{0,6},{1,7},{2,4},{3,5},{4,2},{5,3},{6,0},{7,1},{8,14},{9,15},{10,... | collective-permute-start | bytes 86024 | tf_op jit(solution)/shard_map/ppermute | solution.py:220
  14.4 3.9 %collective-permute-start.6 = (bf16[8,1792]{1,0:T(8,128)(2,1)S(1)}, bf16[8,1792]{1,0:T(8,128)(2,1)S(1)}, u32[]{:S(2)}, u32[]{:S(2)}) collective-permute-start(bf16[8,1792]{1,0:T(8,128)(2,1)S(1)} %get-tuple-element.22), channel_id=1, source_target_pairs={{0,2},{1,3},{2,0},{3,1},{4,6},{5,7},{6,4},{7,5},{8,10},{9,11},{10,... | collective-permute-start | bytes 86024 | tf_op jit(solution)/shard_map/ppermute | solution.py:220
  15.1 3.9 %collective-permute-start.7 = (bf16[8,1792]{1,0:T(8,128)(2,1)S(1)}, bf16[8,1792]{1,0:T(8,128)(2,1)S(1)}, u32[]{:S(2)}, u32[]{:S(2)}) collective-permute-start(bf16[8,1792]{1,0:T(8,128)(2,1)S(1)} %get-tuple-element.22), channel_id=1, source_target_pairs={{0,4},{4,0},{8,12},{12,8},{16,20},{20,16},{24,28},{28,24},{1,5},{5... | collective-permute-start | bytes 86024 | tf_op jit(solution)/shard_map/ppermute | solution.py:220
  19.0 6.1 %collective-permute-start.10 = (bf16[16,1792]{1,0:T(8,128)(2,1)S(1)}, bf16[16,1792]{1,0:T(8,128)(2,1)S(1)}, u32[]{:S(2)}, u32[]{:S(2)}) collective-permute-start(bf16[16,1792]{1,0:T(8,128)(2,1)S(1)} %shard_map.72.refs_3_), channel_id=1, source_target_pairs={{0,24},{4,28},{8,16},{12,20},{16,8},{20,12},{24,0},{28,4},{1,25},{... | collective-permute-start | bytes 172040 | tf_op jit(solution)/shard_map/ppermute | solution.py:220
  22.7 5.1 %collective-permute-start.8 = (bf16[16,1792]{1,0:T(8,128)(2,1)S(1)}, bf16[16,1792]{1,0:T(8,128)(2,1)S(1)}, u32[]{:S(2)}, u32[]{:S(2)}) collective-permute-start(bf16[16,1792]{1,0:T(8,128)(2,1)S(1)} %shard_map.72.refs_3_), channel_id=1, source_target_pairs={{0,16},{4,20},{8,24},{12,28},{16,0},{20,4},{24,8},{28,12},{1,17},{... | collective-permute-start | bytes 172040 | tf_op jit(solution)/shard_map/ppermute | solution.py:220
  22.7 5.1 %collective-permute-start.9 = (bf16[16,1792]{1,0:T(8,128)(2,1)S(1)}, bf16[16,1792]{1,0:T(8,128)(2,1)S(1)}, u32[]{:S(2)}, u32[]{:S(2)}) collective-permute-start(bf16[16,1792]{1,0:T(8,128)(2,1)S(1)} %shard_map.72.refs_3_), channel_id=1, source_target_pairs={{0,8},{4,12},{8,0},{12,4},{16,24},{20,28},{24,16},{28,20},{1,9},{5... | collective-permute-start | bytes 172040 | tf_op jit(solution)/shard_map/ppermute | solution.py:220
  28.0 1.3 %collective-permute-start.11 = (f32[64,64]{1,0:T(8,128)S(1)}, f32[64,64]{1,0:T(8,128)S(1)}, u32[]{:S(2)}, u32[]{:S(2)}) collective-permute-start(f32[64,64]{1,0:T(8,128)S(1)} %shard_map.73.gram_one), channel_id=1, source_target_pairs={{0,1},{1,0},{2,3},{3,2},{4,5},{5,4},{6,7},{7,6},{8,9},{9,8},{10,11... | collective-permute-start | bytes 49160 | tf_op jit(solution)/shard_map/ppermute | solution.py:220

commit v12 on v11

--- a/solution.py
+++ b/solution.py
@@ -180,15 +180,10 @@
     inverse_column = lax.rsqrt(jnp.sum(square, axis=1, keepdims=True) + 1e-6)
     inverse_row = lax.rsqrt(jnp.sum(square, axis=0, keepdims=True) + 1e-6)
     cosine = gram * inverse_column * inverse_row
-    logits = jnp.where(diagonal, -jnp.inf, cosine * (1.0 / SOFTMAX_TEMP))
-    own = logits[:DOCS]
-    largest = jnp.max(own, axis=1, keepdims=True)
-    weights = jnp.exp(own - largest)
-    probs = weights / jnp.sum(weights, axis=1, keepdims=True)
-    largest_row = jnp.max(logits, axis=0, keepdims=True)
-    total_row = jnp.sum(jnp.exp(logits - largest_row), axis=0, keepdims=True)
-    probs = probs + jnp.exp(own - largest_row) / total_row
-    both = probs - partner_ref[...]
+    weights = jnp.where(diagonal, 0.0, jnp.exp(cosine * (1.0 / SOFTMAX_TEMP)))
+    own = weights[:DOCS]
+    total = 1.0 / jnp.sum(own, axis=1, keepdims=True) + 1.0 / jnp.sum(weights, axis=0, keepdims=True)
+    both = own * total - partner_ref[...]
     along = jnp.sum(both * cosine[:DOCS], axis=1, keepdims=True) * (1.0 / SOFTMAX_TEMP)
     weighted = both * inverse_row * (1.0 / SOFTMAX_TEMP)
     high = weighted.astype(jnp.bfloat16)

time: 30.4 us -> 30.4 us (level)
  no operation moved by 1% of the time
where the time goes in v12:
time: 30.4 us; the launch traced here: 30.2 us
  starting transfers between devices  13 us (43%)
  waiting for transfers between devices  10.5 us (35%)
  Pallas kernels  6.04 us (20%)
  between operations  0.7 us (2%)
    ppermute x12, starting transfers between devices, swap(): return lax.ppermute(block, axis, [(s, s ^ distance) for s in range(size)])  13 us
    ppermute x12, waiting for transfers between devices, swap(): return lax.ppermute(block, axis, [(s, s ^ distance) for s in range(size)])  10.5 us
    pallas_call x1, Pallas kernels, per_device(): call(scores_kernel, struct((PAIR * HEAD_GROUP, parts * tokens), f32), [VM...  2.3 us
    pallas_call x1, Pallas kernels, per_device(): call(cut_kernel, (near_cut, near_cut, struct((tokens, width + 2 * kv_widt...  1.28 us
    pallas_call x1, Pallas kernels, per_device(): call(functools.partial(plan_kernel, parts), (struct((tokens, width), bf16...  1.08 us
    pallas_call x1, Pallas kernels, per_device(): call(grads_kernel, (struct((DOCS, features // parts), bf16), struct((DOCS...  0.94 us
  transfers between devices with their start and end apart: 12, of which 8 were waited for; matrix products, arithmetic and copies ran while one was open for 0% of the time, Pallas kernels for 11%

profile of v12, /device:TPU:0, one launch (start us, length us, event | category | flops | bytes accessed | tf_op | source)
XLA Modules:
  0.0 30.2 jit_solution(15054840045509224477)
XLA Ops:
  0.6 1.3 %shard_map.69 = (bf16[128,256]{1,0:T(8,128)(2,1)S(1)}, bf16[128,256]{1,0:T(8,128)(2,1)S(1)}, bf16[128,2304]{1,0:T(8,128)(2,1)S(1)}, bf16[128,256]{1,0:T(8,128)(2,1)S(1)}, bf16[128,256]{1,0:T(8,128)(2,1)S(1)}) custom-call(bf16[128,3584]{1,0:T(8,128)(2,1)} %q_hbm.3, bf16[128,512]{1,0:T(8,128)(2,1)} %k_hbm.1, bf16[128,512]{1,0:T(8,128)(2,1)} %v_hbm.1), custom_call_target="tpu_custom_call" | custom-call | bytes 983040 | tf_op jit(solution)/shard_map/pallas_call | solution.py:240
  1.9 0.5 %collective-permute-start = (bf16[128,2304]{1,0:T(8,128)(2,1)S(1)}, bf16[128,2304]{1,0:T(8,128)(2,1)S(1)}, u32[]{:S(2)}, u32[]{:S(2)}) collective-permute-start(bf16[128,2304]{1,0:T(8,128)(2,1)S(1)} %get-tuple-element.17), channel_id=1, source_target_pairs={{0,1},{1,0},{2,3},{3,2},{4,5},{5,4},{6,7},{7,6},{8,9},{9,8},{10,11... | collective-permute-start | bytes 1769480 | tf_op jit(solution)/shard_map/ppermute | solution.py:215
  2.4 2.6 %collective-permute-start.1 = (bf16[128,256]{1,0:T(8,128)(2,1)S(1)}, bf16[128,256]{1,0:T(8,128)(2,1)S(1)}, u32[]{:S(2)}, u32[]{:S(2)}) collective-permute-start(bf16[128,256]{1,0:T(8,128)(2,1)S(1)} %get-tuple-element.16.k_own), channel_id=1, source_target_pairs={{0,2},{1,3},{2,0},{3,1},{4,6},{5,7},{6,4},{7,5},{8,10},{9,11},{10,... | collective-permute-start | bytes 196616 | tf_op jit(solution)/shard_map/ppermute | solution.py:215
  5.0 0.1 collective-permute-start.2
  5.1 1.7 %collective-permute-start.3 = (bf16[128,256]{1,0:T(8,128)(2,1)S(1)}, bf16[128,256]{1,0:T(8,128)(2,1)S(1)}, u32[]{:S(2)}, u32[]{:S(2)}) collective-permute-start(bf16[128,256]{1,0:T(8,128)(2,1)S(1)} %get-tuple-element.20.v_own), channel_id=1, source_target_pairs={{0,2},{1,3},{2,0},{3,1},{4,6},{5,7},{6,4},{7,5},{8,10},{9,11},{10,... | collective-permute-start | bytes 196616 | tf_op jit(solution)/shard_map/ppermute | solution.py:215
  6.8 0.0 collective-permute-start.4
  6.8 1.1 %shard_map.68 = (bf16[128,1792]{1,0:T(8,128)(2,1)S(1)}, f32[256,512]{1,0:T(8,128)S(1)}, f32[8,512]{1,0:T(8,128)S(1)}, f32[8,64]{1,0:T(8,128)S(1)}) custom-call(s32[1,8]{1,0:T(1,128)} %lengths_hbm.1, s32[8]{0:T(128)} %pairs_hbm.1, bf16[128,3584]{1,0:T(8,128)(2,1)} %q_hbm.3), custom_call_target="tpu_custom_call" | custom-call | bytes 917504 | tf_op jit(solution)/shard_map/pallas_call | solution.py:247
  7.9 0.0 collective-permute-done.1.k_far
  7.9 1.1 %collective-permute-done.2.k_last = bf16[128,256]{1,0:T(8,128)(2,1)S(1)} collective-permute-done((bf16[128,256]{1,0:T(8,128)(2,1)S(1)}, bf16[128,256]{1,0:T(8,128)(2,1)S(1)}, u32[]{:S(2)}, u32[]{:S(2)}) %collective-permute-start.2) | collective-permute-done | bytes 65568 | tf_op jit(solution)/shard_map/ppermute | solution.py:215
  9.0 0.0 collective-permute-done.near
  9.1 2.3 %shard_map.70.sums_ref = f32[14,512]{1,0:T(8,128)S(1)} custom-call(f32[256,512]{1,0:T(8,128)S(1)} %get-tuple-element.14.bias_ref, bf16[128,1792]{1,0:T(8,128)(2,1)S(1)} %get-tuple-element.15.q_own, bf16[128,256]{1,0:T(8,128)(2,1)S(1)} %get-tuple-element.16.k_own, bf16[128,2304]{1,0:T(8,128)(2,1)S(1)} %collective-permute-done.near, ...), custom_call_target="tpu_custom_call" | custom-call | flops 234881024 | bytes 1966080 | tf_op jit(solution)/shard_map/pallas_call | solution.py:268
  11.4 0.0 collective-permute-done.3.v_far
  11.4 0.5 %collective-permute-done.4.v_last = bf16[128,256]{1,0:T(8,128)(2,1)S(1)} collective-permute-done((bf16[128,256]{1,0:T(8,128)(2,1)S(1)}, bf16[128,256]{1,0:T(8,128)(2,1)S(1)}, u32[]{:S(2)}, u32[]{:S(2)}) %collective-permute-start.4) | collective-permute-done | bytes 65568 | tf_op jit(solution)/shard_map/ppermute | solution.py:215
  11.9 0.2 shard_map.71
  12.1 2.4 %collective-permute-start.5 = (bf16[8,1792]{1,0:T(8,128)(2,1)S(1)}, bf16[8,1792]{1,0:T(8,128)(2,1)S(1)}, u32[]{:S(2)}, u32[]{:S(2)}) collective-permute-start(bf16[8,1792]{1,0:T(8,128)(2,1)S(1)} %get-tuple-element.22), channel_id=1, source_target_pairs={{0,6},{1,7},{2,4},{3,5},{4,2},{5,3},{6,0},{7,1},{8,14},{9,15},{10,... | collective-permute-start | bytes 86024 | tf_op jit(solution)/shard_map/ppermute | solution.py:215
  14.4 0.7 %collective-permute-start.6 = (bf16[8,1792]{1,0:T(8,128)(2,1)S(1)}, bf16[8,1792]{1,0:T(8,128)(2,1)S(1)}, u32[]{:S(2)}, u32[]{:S(2)}) collective-permute-start(bf16[8,1792]{1,0:T(8,128)(2,1)S(1)} %get-tuple-element.22), channel_id=1, source_target_pairs={{0,2},{1,3},{2,0},{3,1},{4,6},{5,7},{6,4},{7,5},{8,10},{9,11},{10,... | collective-permute-start | bytes 86024 | tf_op jit(solution)/shard_map/ppermute | solution.py:215
  15.1 0.5 %collective-permute-start.7 = (bf16[8,1792]{1,0:T(8,128)(2,1)S(1)}, bf16[8,1792]{1,0:T(8,128)(2,1)S(1)}, u32[]{:S(2)}, u32[]{:S(2)}) collective-permute-start(bf16[8,1792]{1,0:T(8,128)(2,1)S(1)} %get-tuple-element.22), channel_id=1, source_target_pairs={{0,4},{4,0},{8,12},{12,8},{16,20},{20,16},{24,28},{28,24},{1,5},{5... | collective-permute-start | bytes 86024 | tf_op jit(solution)/shard_map/ppermute | solution.py:215
  15.6 1.3 %collective-permute-done.5.corner_ref = bf16[8,1792]{1,0:T(8,128)(2,1)S(1)} collective-permute-done((bf16[8,1792]{1,0:T(8,128)(2,1)S(1)}, bf16[8,1792]{1,0:T(8,128)(2,1)S(1)}, u32[]{:S(2)}, u32[]{:S(2)}) %collective-permute-start.5) | collective-permute-done | bytes 28704 | tf_op jit(solution)/shard_map/ppermute | solution.py:215
  16.9 1.4 %collective-permute-done.6.far_ref.refs_5_ = bf16[8,1792]{1,0:T(8,128)(2,1)S(1)} collective-permute-done((bf16[8,1792]{1,0:T(8,128)(2,1)S(1)}, bf16[8,1792]{1,0:T(8,128)(2,1)S(1)}, u32[]{:S(2)}, u32[]{:S(2)}) %collective-permute-start.6) | collective-permute-done | bytes 28704 | tf_op jit(solution)/shard_map/ppermute | solution.py:215
  18.3 0.7 %collective-permute-done.7.next_ref = bf16[8,1792]{1,0:T(8,128)(2,1)S(1)} collective-permute-done((bf16[8,1792]{1,0:T(8,128)(2,1)S(1)}, bf16[8,1792]{1,0:T(8,128)(2,1)S(1)}, u32[]{:S(2)}, u32[]{:S(2)}) %collective-permute-start.7) | collective-permute-done | bytes 28704 | tf_op jit(solution)/shard_map/ppermute | solution.py:215
  19.0 3.7 %collective-permute-start.10 = (bf16[16,1792]{1,0:T(8,128)(2,1)S(1)}, bf16[16,1792]{1,0:T(8,128)(2,1)S(1)}, u32[]{:S(2)}, u32[]{:S(2)}) collective-permute-start(bf16[16,1792]{1,0:T(8,128)(2,1)S(1)} %shard_map.72.refs_3_), channel_id=1, source_target_pairs={{0,24},{4,28},{8,16},{12,20},{16,8},{20,12},{24,0},{28,4},{1,25},{... | collective-permute-start | bytes 172040 | tf_op jit(solution)/shard_map/ppermute | solution.py:215
  22.7 0.0 collective-permute-start.8
  22.7 0.8 %collective-permute-start.9 = (bf16[16,1792]{1,0:T(8,128)(2,1)S(1)}, bf16[16,1792]{1,0:T(8,128)(2,1)S(1)}, u32[]{:S(2)}, u32[]{:S(2)}) collective-permute-start(bf16[16,1792]{1,0:T(8,128)(2,1)S(1)} %shard_map.72.refs_3_), channel_id=1, source_target_pairs={{0,8},{4,12},{8,0},{12,4},{16,24},{20,28},{24,16},{28,20},{1,9},{5... | collective-permute-start | bytes 172040 | tf_op jit(solution)/shard_map/ppermute | solution.py:215
  23.5 1.7 %collective-permute-done.10.refs_2_ = bf16[16,1792]{1,0:T(8,128)(2,1)S(1)} collective-permute-done((bf16[16,1792]{1,0:T(8,128)(2,1)S(1)}, bf16[16,1792]{1,0:T(8,128)(2,1)S(1)}, u32[]{:S(2)}, u32[]{:S(2)}) %collective-permute-start.10) | collective-permute-done | bytes 57376 | tf_op jit(solution)/shard_map/ppermute | solution.py:215
  25.2 2.6 %collective-permute-done.8.refs_0_ = bf16[16,1792]{1,0:T(8,128)(2,1)S(1)} collective-permute-done((bf16[16,1792]{1,0:T(8,128)(2,1)S(1)}, bf16[16,1792]{1,0:T(8,128)(2,1)S(1)}, u32[]{:S(2)}, u32[]{:S(2)}) %collective-permute-start.8) | collective-permute-done | bytes 57376 | tf_op jit(solution)/shard_map/ppermute | solution.py:215
  27.8 0.0 collective-permute-done.9.refs_1_
  27.8 0.2 shard_map.73.gram_one
  28.0 0.1 collective-permute-start.11
  28.1 1.2 %collective-permute-done.11.gram_two = f32[64,64]{1,0:T(8,128)S(1)} collective-permute-done((f32[64,64]{1,0:T(8,128)S(1)}, f32[64,64]{1,0:T(8,128)S(1)}, u32[]{:S(2)}, u32[]{:S(2)}) %collective-permute-start.11) | collective-permute-done | bytes 16416 | tf_op jit(solution)/shard_map/ppermute | solution.py:215
  29.3 0.9 %shard_map.74 = (bf16[8,896]{1,0:T(8,128)(2,1)}, f32[8,896]{1,0:T(8,128)}) custom-call(f32[8,64]{1,0:T(8,128)S(1)} %get-tuple-element.13.partner_ref, f32[64,64]{1,0:T(8,128)S(1)} %shard_map.73.gram_one, f32[64,64]{1,0:T(8,128)S(1)} %collective-permute-done.11.gram_two, bf16[16,1792]{1,0:T(8,128)(2,1)S(1)} %collective-permute-done.8.refs_0_, ...), custom_call_target="tpu_custom_call" | custom-call | tf_op jit(solution)/shard_map/pallas_call | solution.py:284
  (1 shorter events, 0.0 us)
Async XLA Ops:
  1.9 7.1 %collective-permute-start = (bf16[128,2304]{1,0:T(8,128)(2,1)S(1)}, bf16[128,2304]{1,0:T(8,128)(2,1)S(1)}, u32[]{:S(2)}, u32[]{:S(2)}) collective-permute-start(bf16[128,2304]{1,0:T(8,128)(2,1)S(1)} %get-tuple-element.17), channel_id=1, source_target_pairs={{0,1},{1,0},{2,3},{3,2},{4,5},{5,4},{6,7},{7,6},{8,9},{9,8},{10,11... | collective-permute-start | bytes 1769480 | tf_op jit(solution)/shard_map/ppermute | solution.py:215
  2.4 5.5 %collective-permute-start.1 = (bf16[128,256]{1,0:T(8,128)(2,1)S(1)}, bf16[128,256]{1,0:T(8,128)(2,1)S(1)}, u32[]{:S(2)}, u32[]{:S(2)}) collective-permute-start(bf16[128,256]{1,0:T(8,128)(2,1)S(1)} %get-tuple-element.16.k_own), channel_id=1, source_target_pairs={{0,2},{1,3},{2,0},{3,1},{4,6},{5,7},{6,4},{7,5},{8,10},{9,11},{10,... | collective-permute-start | bytes 196616 | tf_op jit(solution)/shard_map/ppermute | solution.py:215
  5.0 4.0 %collective-permute-start.2 = (bf16[128,256]{1,0:T(8,128)(2,1)S(1)}, bf16[128,256]{1,0:T(8,128)(2,1)S(1)}, u32[]{:S(2)}, u32[]{:S(2)}) collective-permute-start(bf16[128,256]{1,0:T(8,128)(2,1)S(1)} %get-tuple-element.18), channel_id=1, source_target_pairs={{0,3},{1,2},{2,1},{3,0},{4,7},{5,6},{6,5},{7,4},{8,11},{9,10},{10,... | collective-permute-start | bytes 196616 | tf_op jit(solution)/shard_map/ppermute | solution.py:215
  5.1 6.3 %collective-permute-start.3 = (bf16[128,256]{1,0:T(8,128)(2,1)S(1)}, bf16[128,256]{1,0:T(8,128)(2,1)S(1)}, u32[]{:S(2)}, u32[]{:S(2)}) collective-permute-start(bf16[128,256]{1,0:T(8,128)(2,1)S(1)} %get-tuple-element.20.v_own), channel_id=1, source_target_pairs={{0,2},{1,3},{2,0},{3,1},{4,6},{5,7},{6,4},{7,5},{8,10},{9,11},{10,... | collective-permute-start | bytes 196616 | tf_op jit(solution)/shard_map/ppermute | solution.py:215
  6.8 5.0 %collective-permute-start.4 = (bf16[128,256]{1,0:T(8,128)(2,1)S(1)}, bf16[128,256]{1,0:T(8,128)(2,1)S(1)}, u32[]{:S(2)}, u32[]{:S(2)}) collective-permute-start(bf16[128,256]{1,0:T(8,128)(2,1)S(1)} %get-tuple-element.21), channel_id=1, source_target_pairs={{0,3},{1,2},{2,1},{3,0},{4,7},{5,6},{6,5},{7,4},{8,11},{9,10},{10,... | collective-permute-start | bytes 196616 | tf_op jit(solution)/shard_map/ppermute | solution.py:215
  12.1 4.8 %collective-permute-start.5 = (bf16[8,1792]{1,0:T(8,128)(2,1)S(1)}, bf16[8,1792]{1,0:T(8,128)(2,1)S(1)}, u32[]{:S(2)}, u32[]{:S(2)}) collective-permute-start(bf16[8,1792]{1,0:T(8,128)(2,1)S(1)} %get-tuple-element.22), channel_id=1, source_target_pairs={{0,6},{1,7},{2,4},{3,5},{4,2},{5,3},{6,0},{7,1},{8,14},{9,15},{10,... | collective-permute-start | bytes 86024 | tf_op jit(solution)/shard_map/ppermute | solution.py:215
  14.4 3.9 %collective-permute-start.6 = (bf16[8,1792]{1,0:T(8,128)(2,1)S(1)}, bf16[8,1792]{1,0:T(8,128)(2,1)S(1)}, u32[]{:S(2)}, u32[]{:S(2)}) collective-permute-start(bf16[8,1792]{1,0:T(8,128)(2,1)S(1)} %get-tuple-element.22), channel_id=1, source_target_pairs={{0,2},{1,3},{2,0},{3,1},{4,6},{5,7},{6,4},{7,5},{8,10},{9,11},{10,... | collective-permute-start | bytes 86024 | tf_op jit(solution)/shard_map/ppermute | solution.py:215
  15.1 3.9 %collective-permute-start.7 = (bf16[8,1792]{1,0:T(8,128)(2,1)S(1)}, bf16[8,1792]{1,0:T(8,128)(2,1)S(1)}, u32[]{:S(2)}, u32[]{:S(2)}) collective-permute-start(bf16[8,1792]{1,0:T(8,128)(2,1)S(1)} %get-tuple-element.22), channel_id=1, source_target_pairs={{0,4},{4,0},{8,12},{12,8},{16,20},{20,16},{24,28},{28,24},{1,5},{5... | collective-permute-start | bytes 86024 | tf_op jit(solution)/shard_map/ppermute | solution.py:215
  19.0 6.1 %collective-permute-start.10 = (bf16[16,1792]{1,0:T(8,128)(2,1)S(1)}, bf16[16,1792]{1,0:T(8,128)(2,1)S(1)}, u32[]{:S(2)}, u32[]{:S(2)}) collective-permute-start(bf16[16,1792]{1,0:T(8,128)(2,1)S(1)} %shard_map.72.refs_3_), channel_id=1, source_target_pairs={{0,24},{4,28},{8,16},{12,20},{16,8},{20,12},{24,0},{28,4},{1,25},{... | collective-permute-start | bytes 172040 | tf_op jit(solution)/shard_map/ppermute | solution.py:215
  22.7 5.1 %collective-permute-start.8 = (bf16[16,1792]{1,0:T(8,128)(2,1)S(1)}, bf16[16,1792]{1,0:T(8,128)(2,1)S(1)}, u32[]{:S(2)}, u32[]{:S(2)}) collective-permute-start(bf16[16,1792]{1,0:T(8,128)(2,1)S(1)} %shard_map.72.refs_3_), channel_id=1, source_target_pairs={{0,16},{4,20},{8,24},{12,28},{16,0},{20,4},{24,8},{28,12},{1,17},{... | collective-permute-start | bytes 172040 | tf_op jit(solution)/shard_map/ppermute | solution.py:215
  22.7 5.1 %collective-permute-start.9 = (bf16[16,1792]{1,0:T(8,128)(2,1)S(1)}, bf16[16,1792]{1,0:T(8,128)(2,1)S(1)}, u32[]{:S(2)}, u32[]{:S(2)}) collective-permute-start(bf16[16,1792]{1,0:T(8,128)(2,1)S(1)} %shard_map.72.refs_3_), channel_id=1, source_target_pairs={{0,8},{4,12},{8,0},{12,4},{16,24},{20,28},{24,16},{28,20},{1,9},{5... | collective-permute-start | bytes 172040 | tf_op jit(solution)/shard_map/ppermute | solution.py:215
  28.0 1.3 %collective-permute-start.11 = (f32[64,64]{1,0:T(8,128)S(1)}, f32[64,64]{1,0:T(8,128)S(1)}, u32[]{:S(2)}, u32[]{:S(2)}) collective-permute-start(f32[64,64]{1,0:T(8,128)S(1)} %shard_map.73.gram_one), channel_id=1, source_target_pairs={{0,1},{1,0},{2,3},{3,2},{4,5},{5,4},{6,7},{7,6},{8,9},{9,8},{10,11... | collective-permute-start | bytes 49160 | tf_op jit(solution)/shard_map/ppermute | solution.py:215
